TPU v7x, 32 devices: a whole 2x2x4 slice. The times are simulated.
32 devices in a mesh: seq: 8 (over z, x), chan: 4 (over y, core).
Axes of the slice: x: 2, y: 2, z: 4, core: 2. Of those that a mesh axis runs over, the one named last changes fastest.
Arguments:
- block_in: float32 [2, 1024, 1024], P(None, 'seq', 'chan'), may hold values from -6 to 6
- doc_lengths: int32 [2, 16], replicated, may hold values from 0 to 1024, as said below
- out_grad: float32 [2, 1024, 1024], P(None, 'seq', 'chan'), may hold values from -6 to 6
- first_gain: float32 [1024], P('chan'), may hold values from 0.5 to 1.5
- decay_rate: float32 [1024, 64], P('chan'), may hold values from 1.9073486e-05 to 0.05
- turn_angle: float32 [1024, 64], P('chan'), may hold values from -1 to 1
- out_real: float32 [1024, 64], P('chan'), may hold values from -0.75 to 0.75
- out_imag: float32 [1024, 64], P('chan'), may hold values from -0.75 to 0.75
- skip_gain: float32 [1024], P('chan'), may hold values from -4 to 4
- glu_value: bfloat16 [1024, 1024], P(None, 'chan'), may hold values from -0.5 to 0.5
- glu_gate: bfloat16 [1024, 1024], P(None, 'chan'), may hold values from -0.5 to 0.5
- second_gain: float32 [1024], P('chan'), may hold values from 0.5 to 1.5
- ffn_in: bfloat16 [1024, 4096], P(None, 'chan'), may hold values from -0.1875 to 0.1875
- ffn_out: bfloat16 [4096, 1024], P('chan'), may hold values from -0.1875 to 0.1875
Outputs:
- block_out: float32 [2, 1024, 1024], P(None, 'seq', 'chan')
- in_grad: float32 [2, 1024, 1024], P(None, 'seq', 'chan')
- first_gain_grad: float32 [1024], P('chan')
- decay_rate_grad: float32 [1024, 64], P('chan')
- turn_angle_grad: float32 [1024, 64], P('chan')
- out_real_grad: float32 [1024, 64], P('chan')
- out_imag_grad: float32 [1024, 64], P('chan')
- skip_gain_grad: float32 [1024], P('chan')
- glu_value_grad: float32 [1024, 1024], P(None, 'chan')
- glu_gate_grad: float32 [1024, 1024], P(None, 'chan')
- second_gain_grad: float32 [1024], P('chan')
- ffn_in_grad: float32 [1024, 4096], P(None, 'chan')
- ffn_out_grad: float32 [4096, 1024], P('chan')
Inputs may be any that keep to these rules, and one draw needn't show every extreme that they name: `doc_lengths`: in every stream the lengths add up to 1024 or less; the positions after them are padding; documents may be empty.
All inputs are finite; a program needn't handle non-finite values.
Results may differ from a plain program's by a relative error of at most 0.0066.
Values may be sent and summed in bfloat16 or wider, within the bound.
A program may use at most 192 MiB of HBM per device.

v0:
```python
import jax
import jax.numpy as jnp
from jax import lax
from jax.sharding import PartitionSpec as P

epsilon = 1e-05
chan_group = 16
sub_width = 128
highest = lax.Precision.HIGHEST


def carried_in(part, axis, combine, identity, reverse):
    count = lax.axis_size(axis)
    place = lax.axis_index(axis)
    ahead = count - 1 - place if reverse else place
    gathered = jax.tree.map(lambda a: lax.all_gather(a, axis), part)
    state = jax.tree.map(lambda a, e: jnp.zeros_like(a) + jnp.asarray(e, a.dtype), part, identity)

    def one(turn, state):
        source = count - 1 - turn if reverse else turn
        return combine(
            state, jax.tree.map(lambda a: lax.dynamic_index_in_dim(a, source, 0, False), gathered)
        )

    return lax.fori_loop(0, ahead, one, state)


def token_sums(first_sum, second_sum):
    return lax.psum((first_sum, second_sum), "chan")


def norm_forward(values, gain):
    full_width = values.shape[-1] * lax.axis_size("chan")
    totals = token_sums(jnp.sum(values, -1), jnp.sum(values * values, -1))
    average = totals[0] / full_width
    spread = totals[1] / full_width - average * average
    scaler = lax.rsqrt(spread + epsilon)
    normed = (values - average[:, None]) * scaler[:, None]
    return (normed * gain, normed, scaler)


def norm_backward(grad_out, normed, scaler, gain):
    full_width = normed.shape[-1] * lax.axis_size("chan")
    scaled = grad_out * gain
    totals = token_sums(jnp.sum(scaled, -1), jnp.sum(scaled * normed, -1))
    grad_in = scaler[:, None] * (
        scaled - totals[0][:, None] / full_width - normed * (totals[1][:, None] / full_width)
    )
    return (grad_in, jnp.sum(grad_out * normed, axis=0))


def powers(decay, angle, count):
    steps = jnp.arange(count, dtype=jnp.float32)
    magnitude = jnp.exp(-decay[..., None] * steps)
    phase = angle[..., None] * steps
    return (magnitude * jnp.cos(phase), magnitude * jnp.sin(phase))


def weights_of(decay, real_part, imag_part):
    factor = jnp.sqrt(-jnp.expm1(-2.0 * decay))
    return (real_part * factor, imag_part * factor)


def group_params(params):
    decay, angle, real_part, imag_part, skip = params
    groups = decay.shape[0] // chan_group
    states = decay.shape[1]
    shaped = [
        item.reshape(groups, chan_group, states) for item in (decay, angle, real_part, imag_part)
    ]
    return (shaped[0], shaped[1], shaped[2], shaped[3], skip.reshape(groups, chan_group))


def local_mix(inputs, params, masks):
    segment, keep_last = masks
    streams, length, width = inputs.shape
    groups = width // chan_group
    states = params[0].shape[1]
    span = min(sub_width, length)
    pieces = length // span
    index = jnp.arange(span, dtype=jnp.int32)
    lags = jnp.maximum(index[:, None] - index[None, :], 0)
    causal = index[:, None] >= index[None, :]
    grouped_in = inputs.reshape(streams, pieces, span, groups, chan_group).transpose(3, 1, 0, 2, 4)
    seg_pieces = segment.reshape(streams, pieces, span).transpose(1, 0, 2)
    previous = jnp.concatenate([seg_pieces[:1, :, 0], seg_pieces[:-1, :, -1]], axis=0)

    def local_one_group(items):
        group_in, block_decay, block_angle, block_real, block_imag, block_skip = items
        pow_re, pow_im = powers(block_decay, block_angle, span + 1)
        coef_re, coef_im = weights_of(block_decay, block_real, block_imag)
        kernel = jnp.einsum(
            "gn,gnk->gk", coef_re, pow_re[..., :span], precision=highest
        ) - jnp.einsum("gn,gnk->gk", coef_im, pow_im[..., :span], precision=highest)
        toeplitz = kernel[:, lags]
        table_re = coef_re[..., None] * pow_re[..., 1:] - coef_im[..., None] * pow_im[..., 1:]
        table_im = coef_re[..., None] * pow_im[..., 1:] + coef_im[..., None] * pow_re[..., 1:]
        rev_re = pow_re[..., span - 1 :: -1]
        rev_im = pow_im[..., span - 1 :: -1]

        def piece_step(state, piece_items):
            state_re, state_im = state
            piece_in, piece_seg, piece_prev = piece_items
            same = ((piece_seg[:, :, None] == piece_seg[:, None, :]) & causal[None]).astype(
                jnp.float32
            )
            local_out = jnp.einsum("gts,bts,bsg->btg", toeplitz, same, piece_in, precision=highest)
            keep_mask = (piece_seg == piece_prev[:, None]).astype(jnp.float32)
            carried = jnp.einsum(
                "gnt,bgn->btg", table_re, state_re, precision=highest
            ) - jnp.einsum("gnt,bgn->btg", table_im, state_im, precision=highest)
            last_mask = (piece_seg == piece_seg[:, -1:]).astype(jnp.float32)
            tail_in = piece_in * last_mask[:, :, None]
            end_re = jnp.einsum("gns,bsg->bgn", rev_re, tail_in, precision=highest)
            end_im = jnp.einsum("gns,bsg->bgn", rev_im, tail_in, precision=highest)
            step_re = keep_mask[:, -1][:, None, None] * pow_re[None, :, :, span]
            step_im = keep_mask[:, -1][:, None, None] * pow_im[None, :, :, span]
            new_re = step_re * state_re - step_im * state_im + end_re
            new_im = step_re * state_im + step_im * state_re + end_im
            return (
                (new_re, new_im),
                local_out + keep_mask[:, :, None] * carried + block_skip * piece_in,
            )

        zero_state = jnp.zeros((streams, chan_group, states), jnp.float32)
        final_state, mixed = lax.scan(
            piece_step, (zero_state, zero_state), (group_in, seg_pieces, previous)
        )
        magnitude = jnp.exp(-block_decay * length)
        phase = block_angle * length
        decay_re = keep_last[:, None, None] * (magnitude * jnp.cos(phase))[None]
        decay_im = keep_last[:, None, None] * (magnitude * jnp.sin(phase))[None]
        return (mixed, final_state[0], final_state[1], decay_re, decay_im)

    block_decay, block_angle, block_real, block_imag, block_skip = group_params(params)
    outputs = lax.map(
        jax.checkpoint(local_one_group),
        (grouped_in, block_decay, block_angle, block_real, block_imag, block_skip),
    )
    mixed = outputs[0].transpose(2, 1, 3, 0, 4).reshape(streams, length, width)
    states_out = [
        item.transpose(1, 0, 2, 3).reshape(streams, width, states) for item in outputs[1:]
    ]
    return (mixed, states_out[0], states_out[1], states_out[2], states_out[3])


def carry_mix(params, carry_re, carry_im, keep_mask):
    streams, length = keep_mask.shape
    width, states = params[0].shape
    groups = width // chan_group
    grouped_re = carry_re.reshape(streams, groups, chan_group, states).transpose(1, 0, 2, 3)
    grouped_im = carry_im.reshape(streams, groups, chan_group, states).transpose(1, 0, 2, 3)

    def carry_one_group(items):
        block_decay, block_angle, block_real, block_imag, state_re, state_im = items
        pow_re, pow_im = powers(block_decay, block_angle, length + 1)
        coef_re, coef_im = weights_of(block_decay, block_real, block_imag)
        table_re = coef_re[..., None] * pow_re[..., 1:] - coef_im[..., None] * pow_im[..., 1:]
        table_im = coef_re[..., None] * pow_im[..., 1:] + coef_im[..., None] * pow_re[..., 1:]
        return jnp.einsum("gnt,bgn->btg", table_re, state_re, precision=highest) - jnp.einsum(
            "gnt,bgn->btg", table_im, state_im, precision=highest
        )

    block_decay, block_angle, block_real, block_imag, block_skip = group_params(params)
    outputs = lax.map(
        jax.checkpoint(carry_one_group),
        (block_decay, block_angle, block_real, block_imag, grouped_re, grouped_im),
    )
    return outputs.transpose(1, 2, 0, 3).reshape(streams, length, width) * keep_mask[..., None]


def full_mix(inputs, params, carry_re, carry_im, keep_mask, masks):
    local_out, end_re, end_im, decay_re, decay_im = local_mix(inputs, params, masks)
    mixed = local_out + carry_mix(params, carry_re, carry_im, keep_mask)
    return (
        mixed,
        decay_re * carry_re - decay_im * carry_im + end_re,
        decay_re * carry_im + decay_im * carry_re + end_im,
    )


def compose(earlier, later):
    return (
        later[0] * earlier[0] - later[1] * earlier[1],
        later[0] * earlier[1] + later[1] * earlier[0],
        later[2] + later[0] * earlier[2] - later[1] * earlier[3],
        later[3] + later[0] * earlier[3] + later[1] * earlier[2],
    )


def ffn_local(mid_low, grad_low, in_weight, out_weight):
    hidden_pre = jnp.dot(mid_low, in_weight, preferred_element_type=jnp.float32)
    hidden, hidden_pull = jax.vjp(jax.nn.gelu, hidden_pre)
    hidden_low = hidden.astype(jnp.bfloat16)
    result = jnp.dot(hidden_low, out_weight, preferred_element_type=jnp.float32)
    hidden_grad = jnp.dot(grad_low, out_weight.T, preferred_element_type=jnp.float32)
    pre_low = hidden_pull(hidden_grad)[0].astype(jnp.bfloat16)
    out_weight_grad = jnp.dot(hidden_low.T, grad_low, preferred_element_type=jnp.float32)
    in_weight_grad = jnp.dot(mid_low.T, pre_low, preferred_element_type=jnp.float32)
    mid_grad = jnp.dot(pre_low, in_weight.T, preferred_element_type=jnp.float32)
    return (result, mid_grad, in_weight_grad, out_weight_grad)


def per_device(
    block_in,
    doc_lengths,
    out_grad,
    first_gain,
    decay_rate,
    turn_angle,
    out_real,
    out_imag,
    skip_gain,
    glu_value,
    glu_gate,
    second_gain,
    ffn_in,
    ffn_out,
):
    streams, length, width = block_in.shape
    row_count = streams * length
    positions = lax.axis_index("seq") * length + jnp.arange(length, dtype=jnp.int32)
    doc_ends = jnp.cumsum(doc_lengths, axis=1)
    segment = jnp.sum((doc_ends[:, None, :] <= positions[None, :, None]).astype(jnp.int32), axis=2)
    before = jnp.sum((doc_ends <= positions[0] - 1).astype(jnp.int32), axis=1)
    valid_mask = (positions[None, :] < doc_ends[:, -1:]).astype(jnp.float32)
    keep_mask = (segment == before[:, None]).astype(jnp.float32)
    masks = (segment, keep_mask[:, -1])
    params = (decay_rate, turn_angle, out_real, out_imag, skip_gain)
    block_rows = block_in.reshape(row_count, width)
    gained_in, normed_in, scaler_in = norm_forward(block_rows, first_gain)
    mixer_in = gained_in.reshape(streams, length, width) * valid_mask[..., None]
    local_out, end_re, end_im, decay_re, decay_im = local_mix(mixer_in, params, masks)
    unit_map = jnp.ones_like(decay_re)
    empty_map = jnp.zeros_like(decay_re)
    carried = carried_in(
        (decay_re, decay_im, end_re, end_im),
        "seq",
        compose,
        (unit_map, empty_map, empty_map, empty_map),
        False,
    )
    carry_re = carried[2]
    carry_im = carried[3]
    mixer_out = local_out + carry_mix(params, carry_re, carry_im, keep_mask)
    act_low = jax.nn.gelu(mixer_out).astype(jnp.bfloat16).reshape(row_count, width)
    act_full = lax.all_gather(act_low, "chan", axis=1, tiled=True)
    value_pre = jnp.dot(act_full, glu_value, preferred_element_type=jnp.float32)
    gate_pre = jnp.dot(act_full, glu_gate, preferred_element_type=jnp.float32)
    gate_sig = jax.nn.sigmoid(gate_pre)
    resid = block_rows + value_pre * gate_sig
    gained_mid, normed_mid, scaler_mid = norm_forward(resid, second_gain)
    mid_low = gained_mid.astype(jnp.bfloat16)
    grad_rows = out_grad.reshape(row_count, width)
    grad_low = grad_rows.astype(jnp.bfloat16)
    mid_full, grad_full = (
        lax.all_gather(mid_low, "chan", axis=1, tiled=True),
        lax.all_gather(grad_low, "chan", axis=1, tiled=True),
    )
    part_out, part_grad, ffn_in_grad, ffn_out_grad = ffn_local(mid_full, grad_full, ffn_in, ffn_out)
    ffn_result, mid_grad = (
        lax.psum_scatter(part_out, "chan", scatter_dimension=1, tiled=True),
        lax.psum_scatter(part_grad, "chan", scatter_dimension=1, tiled=True),
    )
    block_out = (resid + ffn_result).reshape(streams, length, width)
    mid_in_grad, second_gain_grad = norm_backward(mid_grad, normed_mid, scaler_mid, second_gain)
    resid_grad = grad_rows + mid_in_grad
    value_low = (resid_grad * gate_sig).astype(jnp.bfloat16)
    gate_low = (resid_grad * value_pre * gate_sig * (1.0 - gate_sig)).astype(jnp.bfloat16)
    glu_value_grad = jnp.dot(act_full.T, value_low, preferred_element_type=jnp.float32)
    glu_gate_grad = jnp.dot(act_full.T, gate_low, preferred_element_type=jnp.float32)
    act_part = jnp.dot(value_low, glu_value.T, preferred_element_type=jnp.float32) + jnp.dot(
        gate_low, glu_gate.T, preferred_element_type=jnp.float32
    )
    act_grad = lax.psum_scatter(act_part, "chan", scatter_dimension=1, tiled=True).reshape(
        streams, length, width
    )
    unused_out, gelu_pull = jax.vjp(jax.nn.gelu, mixer_out)
    mixer_grad = gelu_pull(act_grad)[0]

    def carry_only(first_state, second_state):
        return carry_mix(params, first_state, second_state, keep_mask)

    unused_carry, carry_pull = jax.vjp(carry_only, carry_re, carry_im)
    direct_re, direct_im = carry_pull(mixer_grad)
    adjoint = carried_in(
        (decay_re, -decay_im, direct_re, direct_im),
        "seq",
        compose,
        (unit_map, empty_map, empty_map, empty_map),
        True,
    )

    def whole_mix(inputs, decay, angle, real_part, imag_part, skip, first_state, second_state):
        return full_mix(
            inputs,
            (decay, angle, real_part, imag_part, skip),
            first_state,
            second_state,
            keep_mask,
            masks,
        )

    unused_whole, whole_pull = jax.vjp(
        whole_mix,
        mixer_in,
        decay_rate,
        turn_angle,
        out_real,
        out_imag,
        skip_gain,
        carry_re,
        carry_im,
    )
    pulled = whole_pull((mixer_grad, adjoint[2], adjoint[3]))
    unit_grad = (pulled[0] * valid_mask[..., None]).reshape(row_count, width)
    in_norm_grad, first_gain_grad = norm_backward(unit_grad, normed_in, scaler_in, first_gain)
    in_grad = (resid_grad + in_norm_grad).reshape(streams, length, width)
    decay_rate_grad = pulled[1]
    turn_angle_grad = pulled[2]
    out_real_grad = pulled[3]
    out_imag_grad = pulled[4]
    skip_gain_grad = pulled[5]
    (
        first_gain_grad,
        decay_rate_grad,
        turn_angle_grad,
        out_real_grad,
        out_imag_grad,
        skip_gain_grad,
        glu_value_grad,
        glu_gate_grad,
        second_gain_grad,
        ffn_in_grad,
        ffn_out_grad,
    ) = lax.psum(
        (
            first_gain_grad,
            decay_rate_grad,
            turn_angle_grad,
            out_real_grad,
            out_imag_grad,
            skip_gain_grad,
            glu_value_grad,
            glu_gate_grad,
            second_gain_grad,
            ffn_in_grad,
            ffn_out_grad,
        ),
        "seq",
    )
    return (
        block_out,
        in_grad,
        first_gain_grad,
        decay_rate_grad,
        turn_angle_grad,
        out_real_grad,
        out_imag_grad,
        skip_gain_grad,
        glu_value_grad,
        glu_gate_grad,
        second_gain_grad,
        ffn_in_grad,
        ffn_out_grad,
    )


def solution(mesh):
    placed = (
        P(None, "seq", "chan"),
        P(),
        P(None, "seq", "chan"),
        P("chan"),
        P("chan", None),
        P("chan", None),
        P("chan", None),
        P("chan", None),
        P("chan"),
        P(None, "chan"),
        P(None, "chan"),
        P("chan"),
        P(None, "chan"),
        P("chan", None),
    )
    return jax.shard_map(
        per_device,
        mesh=mesh,
        in_specs=placed,
        out_specs=(
            P(None, "seq", "chan"),
            P(None, "seq", "chan"),
            P("chan"),
            P("chan", None),
            P("chan", None),
            P("chan", None),
            P("chan", None),
            P("chan"),
            P(None, "chan"),
            P(None, "chan"),
            P("chan"),
            P(None, "chan"),
            P("chan", None),
        ),
        check_vma=False,
    )
```

profile of v0, /device:TPU:0, one launch (start us, length us, event | category | flops | bytes accessed | tf_op | source)
XLA Modules:
  0.0 6362.6 jit_solution(5672394978822924105)
XLA Ops:
  31.6 1469.2 %while.168 = (s32[]{:T(128)}, f32[16,1,2,128,16]{3,4,0,2,1:T(8,128)S(1)}, f32[16,2,16,64]{3,1,2,0:T(2,128)}, f32[16,2,16,64]{3,1,2,0:T(2,128)}, f32[16,2,16,64]{...) while((s32[]{:T(128)}, ...), condition=%wide.region_8.9_spmd.clone, body=%wide.region_7.8_spmd.clone.sunk | while | flops 21516288 | bytes 26604664 | solution.py:136
  39.6 54.4 gather_fusion
  131.4 54.4 gather_fusion
  223.2 54.4 gather_fusion
  315.0 54.4 gather_fusion
  406.8 54.4 gather_fusion
  498.6 54.4 gather_fusion
  590.4 54.4 gather_fusion
  682.2 54.4 gather_fusion
  774.0 54.4 gather_fusion
  865.8 54.4 gather_fusion
  957.6 54.4 gather_fusion
  1049.4 54.4 gather_fusion
  1141.2 54.4 gather_fusion
  1233.0 54.4 gather_fusion
  1324.8 54.4 gather_fusion
  1416.6 54.4 gather_fusion
  1668.6 130.5 %while.117 = (s32[]{:T(128)}, f32[16,2,128,16]{2,3,0,1:T(8,128)}, f32[16,2,16,64]{3,1,2,0:T(2,128)S(1)}, f32[16,16,64]{2,1,0:T(8,128)}, f32[16,16,64]{2,1,0:T(8,...) while((s32[]{:T(128)}, f32[16,2,128,16]{2,3,0,1:T(8,128)}, ...), condition=%wide.region_12.13_spmd, body=%wide.region_11.12_spmd.sunk | while | flops 7875586 | bytes 3342953 | solution.py:165
  1943.9 172.4 %while.118 = (s32[]{:T(128)}, f32[16,2,16,64]{3,1,2,0:T(2,128)}, f32[16,2,16,64]{3,1,2,0:T(2,128)}, f32[16,16,64]{2,1,0:T(8,128)}, f32[16,16,64]{2,1,0:T(8,128)}...) while((s32[]{:T(128)}, f32[16,2,16,64]{3,1,2,0:T(2,128)}, ...), condition=%wide.region_25.26_spmd, body=%wide.region_24.25_spmd.sunk | while | flops 7875587 | bytes 3350661 | solution.py:165
  2132.2 274.4 %while.167 = (s32[]{:T(128)}, f32[16,16,64]{2,1,0:T(8,128)}, f32[16,16,64]{2,1,0:T(8,128)}, f32[16,16,64]{2,1,0:T(8,128)}, f32[16,16,64]{2,1,0:T(8,128)}, /*inde...) while((s32[]{:T(128)}, f32[16,16,64]{2,1,0:T(8,128)}, ...), condition=%wide.region_55.56_spmd, body=%wide.region_48.55_spmd.sunk | while | flops 10918915 | bytes 8691881 | solution.py:165
  2438.7 3550.1 %while.169 = (s32[]{:T(128)}, f32[16,1,2,128,16]{3,2,4,1,0:T(2,128)}, f32[16,16,64]{2,1,0:T(8,128)}, f32[16,16,64]{2,1,0:T(8,128)}, f32[16,16,64]{2,1,0:T(8,128)...) while((s32[]{:T(128)}, ...), condition=%wide.region_41.42_spmd.clone, body=%wide.region_28.41_spmd.clone.sunk | while | flops 40949744 | bytes 59111684 | solution.py:136
  2450.4 98.3 %scatter_custom_fusion.6 = f32[16,128]{0,1:T(8,128)S(1)} fusion(s32[16384]{0:T(1024)S(1)} %fusion.375, f32[16384,16]{1,0:T(8,128)} %bitcast.715, f32[]{:T(128)} %constant.435.clone.1..sunk), kind=kCustom, calls=%fused_computation.237.clone.1 | custom fusion | flops 262144 | bytes 8704 | tf_op jit(solution)/shard_map/transpose(jvp())/while/body/eval_jaxpr/checkpoint/scatter-add | solution.py:95
  2594.4 54.4 gather_fusion.1
  2672.2 98.3 %scatter_custom_fusion.6 = f32[16,128]{0,1:T(8,128)S(1)} fusion(s32[16384]{0:T(1024)S(1)} %fusion.375, f32[16384,16]{1,0:T(8,128)} %bitcast.715, f32[]{:T(128)} %constant.435.clone.1..sunk), kind=kCustom, calls=%fused_computation.237.clone.1 | custom fusion | flops 262144 | bytes 8704 | tf_op jit(solution)/shard_map/transpose(jvp())/while/body/eval_jaxpr/checkpoint/scatter-add | solution.py:95
  2816.3 54.4 gather_fusion.1
  2894.1 98.3 %scatter_custom_fusion.6 = f32[16,128]{0,1:T(8,128)S(1)} fusion(s32[16384]{0:T(1024)S(1)} %fusion.375, f32[16384,16]{1,0:T(8,128)} %bitcast.715, f32[]{:T(128)} %constant.435.clone.1..sunk), kind=kCustom, calls=%fused_computation.237.clone.1 | custom fusion | flops 262144 | bytes 8704 | tf_op jit(solution)/shard_map/transpose(jvp())/while/body/eval_jaxpr/checkpoint/scatter-add | solution.py:95
  3038.2 54.4 gather_fusion.1
  3116.0 98.3 %scatter_custom_fusion.6 = f32[16,128]{0,1:T(8,128)S(1)} fusion(s32[16384]{0:T(1024)S(1)} %fusion.375, f32[16384,16]{1,0:T(8,128)} %bitcast.715, f32[]{:T(128)} %constant.435.clone.1..sunk), kind=kCustom, calls=%fused_computation.237.clone.1 | custom fusion | flops 262144 | bytes 8704 | tf_op jit(solution)/shard_map/transpose(jvp())/while/body/eval_jaxpr/checkpoint/scatter-add | solution.py:95
  3260.0 54.4 gather_fusion.1
  3337.8 98.3 %scatter_custom_fusion.6 = f32[16,128]{0,1:T(8,128)S(1)} fusion(s32[16384]{0:T(1024)S(1)} %fusion.375, f32[16384,16]{1,0:T(8,128)} %bitcast.715, f32[]{:T(128)} %constant.435.clone.1..sunk), kind=kCustom, calls=%fused_computation.237.clone.1 | custom fusion | flops 262144 | bytes 8704 | tf_op jit(solution)/shard_map/transpose(jvp())/while/body/eval_jaxpr/checkpoint/scatter-add | solution.py:95
  3481.9 54.4 gather_fusion.1
  3559.7 98.3 %scatter_custom_fusion.6 = f32[16,128]{0,1:T(8,128)S(1)} fusion(s32[16384]{0:T(1024)S(1)} %fusion.375, f32[16384,16]{1,0:T(8,128)} %bitcast.715, f32[]{:T(128)} %constant.435.clone.1..sunk), kind=kCustom, calls=%fused_computation.237.clone.1 | custom fusion | flops 262144 | bytes 8704 | tf_op jit(solution)/shard_map/transpose(jvp())/while/body/eval_jaxpr/checkpoint/scatter-add | solution.py:95
  3703.8 54.4 gather_fusion.1
  3781.6 98.3 %scatter_custom_fusion.6 = f32[16,128]{0,1:T(8,128)S(1)} fusion(s32[16384]{0:T(1024)S(1)} %fusion.375, f32[16384,16]{1,0:T(8,128)} %bitcast.715, f32[]{:T(128)} %constant.435.clone.1..sunk), kind=kCustom, calls=%fused_computation.237.clone.1 | custom fusion | flops 262144 | bytes 8704 | tf_op jit(solution)/shard_map/transpose(jvp())/while/body/eval_jaxpr/checkpoint/scatter-add | solution.py:95
  3925.6 54.4 gather_fusion.1
  4003.4 98.3 %scatter_custom_fusion.6 = f32[16,128]{0,1:T(8,128)S(1)} fusion(s32[16384]{0:T(1024)S(1)} %fusion.375, f32[16384,16]{1,0:T(8,128)} %bitcast.715, f32[]{:T(128)} %constant.435.clone.1..sunk), kind=kCustom, calls=%fused_computation.237.clone.1 | custom fusion | flops 262144 | bytes 8704 | tf_op jit(solution)/shard_map/transpose(jvp())/while/body/eval_jaxpr/checkpoint/scatter-add | solution.py:95
  4225.3 98.3 %scatter_custom_fusion.6 = f32[16,128]{0,1:T(8,128)S(1)} fusion(s32[16384]{0:T(1024)S(1)} %fusion.375, f32[16384,16]{1,0:T(8,128)} %bitcast.715, f32[]{:T(128)} %constant.435.clone.1..sunk), kind=kCustom, calls=%fused_computation.237.clone.1 | custom fusion | flops 262144 | bytes 8704 | tf_op jit(solution)/shard_map/transpose(jvp())/while/body/eval_jaxpr/checkpoint/scatter-add | solution.py:95
  4447.2 98.3 %scatter_custom_fusion.6 = f32[16,128]{0,1:T(8,128)S(1)} fusion(s32[16384]{0:T(1024)S(1)} %fusion.375, f32[16384,16]{1,0:T(8,128)} %bitcast.715, f32[]{:T(128)} %constant.435.clone.1..sunk), kind=kCustom, calls=%fused_computation.237.clone.1 | custom fusion | flops 262144 | bytes 8704 | tf_op jit(solution)/shard_map/transpose(jvp())/while/body/eval_jaxpr/checkpoint/scatter-add | solution.py:95
  4669.1 98.3 %scatter_custom_fusion.6 = f32[16,128]{0,1:T(8,128)S(1)} fusion(s32[16384]{0:T(1024)S(1)} %fusion.375, f32[16384,16]{1,0:T(8,128)} %bitcast.715, f32[]{:T(128)} %constant.435.clone.1..sunk), kind=kCustom, calls=%fused_computation.237.clone.1 | custom fusion | flops 262144 | bytes 8704 | tf_op jit(solution)/shard_map/transpose(jvp())/while/body/eval_jaxpr/checkpoint/scatter-add | solution.py:95
  4890.9 98.3 %scatter_custom_fusion.6 = f32[16,128]{0,1:T(8,128)S(1)} fusion(s32[16384]{0:T(1024)S(1)} %fusion.375, f32[16384,16]{1,0:T(8,128)} %bitcast.715, f32[]{:T(128)} %constant.435.clone.1..sunk), kind=kCustom, calls=%fused_computation.237.clone.1 | custom fusion | flops 262144 | bytes 8704 | tf_op jit(solution)/shard_map/transpose(jvp())/while/body/eval_jaxpr/checkpoint/scatter-add | solution.py:95
  5112.8 98.3 %scatter_custom_fusion.6 = f32[16,128]{0,1:T(8,128)S(1)} fusion(s32[16384]{0:T(1024)S(1)} %fusion.375, f32[16384,16]{1,0:T(8,128)} %bitcast.715, f32[]{:T(128)} %constant.435.clone.1..sunk), kind=kCustom, calls=%fused_computation.237.clone.1 | custom fusion | flops 262144 | bytes 8704 | tf_op jit(solution)/shard_map/transpose(jvp())/while/body/eval_jaxpr/checkpoint/scatter-add | solution.py:95
  5256.8 54.4 gather_fusion.1
  5334.7 98.3 %scatter_custom_fusion.6 = f32[16,128]{0,1:T(8,128)S(1)} fusion(s32[16384]{0:T(1024)S(1)} %fusion.375, f32[16384,16]{1,0:T(8,128)} %bitcast.715, f32[]{:T(128)} %constant.435.clone.1..sunk), kind=kCustom, calls=%fused_computation.237.clone.1 | custom fusion | flops 262144 | bytes 8704 | tf_op jit(solution)/shard_map/transpose(jvp())/while/body/eval_jaxpr/checkpoint/scatter-add | solution.py:95
  5478.7 54.4 gather_fusion.1
  5556.5 98.3 %scatter_custom_fusion.6 = f32[16,128]{0,1:T(8,128)S(1)} fusion(s32[16384]{0:T(1024)S(1)} %fusion.375, f32[16384,16]{1,0:T(8,128)} %bitcast.715, f32[]{:T(128)} %constant.435.clone.1..sunk), kind=kCustom, calls=%fused_computation.237.clone.1 | custom fusion | flops 262144 | bytes 8704 | tf_op jit(solution)/shard_map/transpose(jvp())/while/body/eval_jaxpr/checkpoint/scatter-add | solution.py:95
  5700.6 54.4 gather_fusion.1
  5778.4 98.3 %scatter_custom_fusion.6 = f32[16,128]{0,1:T(8,128)S(1)} fusion(s32[16384]{0:T(1024)S(1)} %fusion.375, f32[16384,16]{1,0:T(8,128)} %bitcast.715, f32[]{:T(128)} %constant.435.clone.1..sunk), kind=kCustom, calls=%fused_computation.237.clone.1 | custom fusion | flops 262144 | bytes 8704 | tf_op jit(solution)/shard_map/transpose(jvp())/while/body/eval_jaxpr/checkpoint/scatter-add | solution.py:95
  6023.4 314.3 %all-reduce.22.cloned.1.call-done = (f32[256,64]{1,0:T(8,128)}, f32[256,64]{1,0:T(8,128)}, f32[256,64]{1,0:T(8,128)}, f32[256,64]{1,0:T(8,128)}, f32[1024,256]{1...) async-done(((f32[256,64]{1,0:T(8,128)}, f32[256,64]{1,0:T(8,128)}, f32[256,64]{1,0:T(8,128)}, f32[256,64]{1,0:T(8,128)}, ...) | async-done | bytes 10747920 | tf_op jit(solution)/shard_map/psum | solution.py:336
  (3104 shorter events, 3059.5 us)
Async XLA Ops:
  7.2 1821.1 %copy-start = (bf16[1024,1024]{1,0:T(8,128)(2,1)S(1)}, bf16[1024,1024]{1,0:T(8,128)(2,1)}, u32[]{:S(2)}) copy-start(bf16[1024,1024]{1,0:T(8,128)(2,1)} %param.40) | copy-start | bytes 6291460
  7.2 1536.1 %all-gather.10.cloned.1.call-start = ((), (), s32[]{:S(2)}) async-start(), calls=%async_computation.4 | async-start | bytes 1179648 | tf_op jit(solution)/shard_map/all_gather | solution.py:16
  1502.7 82.3 %all-gather.12.cloned.1.call-start = ((), (), s32[]{:S(2)}) async-start(), calls=%async_computation.5 | async-start | bytes 1179648 | tf_op jit(solution)/shard_map/all_gather | solution.py:16
  1504.5 122.1 %all-gather.14.cloned.1.call-start = ((), (), s32[]{:S(2)}) async-start(), calls=%async_computation.6 | async-start | bytes 1179648 | tf_op jit(solution)/shard_map/all_gather | solution.py:16
  1505.4 162.7 %all-gather.8.cloned.1.call-start = ((), (), s32[]{:S(2)}) async-start(), calls=%async_computation.3 | async-start | bytes 1179648 | tf_op jit(solution)/shard_map/all_gather | solution.py:16
  1506.3 376.2 %reduce-scatter.6.cloned.1.call-start = ((), (), s32[]{:S(2)}) async-start(), calls=%async_computation.8 | async-start | bytes 1310720 | tf_op jit(solution)/shard_map/reduce_scatter | solution.py:263
  1668.6 134.3 %copy-start.47 = (f32[256,256]{1,0:T(8,128)S(1)}, f32[256,256]{1,0:T(8,128)}, u32[]{:S(2)}) copy-start(f32[256,256]{1,0:T(8,128)} %copy.577) | copy-start | bytes 786436
  1834.4 76.1 %reduce-scatter.4.cloned.1.call-start = ((), (), s32[]{:S(2)}) async-start(), calls=%async_computation.7 | async-start | bytes 1310720 | tf_op jit(solution)/shard_map/reduce_scatter | solution.py:262
  1838.3 101.6 %reduce-scatter.8.cloned.1.call-start = ((), (), s32[]{:S(2)}) async-start(), calls=%async_computation.9 | async-start | bytes 1310720 | tf_op jit(solution)/shard_map/reduce_scatter | solution.py:275
  1914.9 492.1 %all-gather.18.cloned.1.call-start = ((), (), s32[]{:S(2)}) async-start(), calls=%async_computation.11 | async-start | bytes 1179648 | tf_op jit(solution)/shard_map/all_gather | solution.py:16
  1915.8 491.2 %all-gather.16.cloned.1.call-start = ((), (), s32[]{:S(2)}) async-start(), calls=%async_computation.10 | async-start | bytes 1179648 | tf_op jit(solution)/shard_map/all_gather | solution.py:16
  2118.1 289.0 %all-gather.20.cloned.1.call-start = ((), (), s32[]{:S(2)}) async-start(), calls=%async_computation.12 | async-start | bytes 1179648 | tf_op jit(solution)/shard_map/all_gather | solution.py:16
  2129.5 4208.2 %all-reduce.22.cloned.1.call-start = ((), (), s32[]{:S(2)}) async-start(), calls=%async_computation.13 | async-start | bytes 22020096 | tf_op jit(solution)/shard_map/psum | solution.py:336
  2132.2 274.4 %copy-start.30 = (f32[256,256]{0,1:T(8,128)S(1)}, f32[256,256]{0,1:T(8,128)}, u32[]{:S(2)}) copy-start(f32[256,256]{0,1:T(8,128)} %copy-done.29) | copy-start | bytes 786436
  2132.2 274.5 %copy-start.26 = (f32[16,1,2,128,16]{3,4,0,2,1:T(8,128)S(1)}, f32[16,1,2,128,16]{3,4,0,2,1:T(8,128)}, u32[]{:S(2)}) copy-start(f32[16,1,2,128,16]{3,4,0,2,1:T(8,128)} %copy-done.24) | copy-start | bytes 786436
  2132.2 274.5 %copy-start.71 = (f32[2,128]{1,0:T(2,128)S(1)}, f32[2,128]{1,0:T(2,128)}, u32[]{:S(2)}) copy-start(f32[2,128]{1,0:T(2,128)} %copy-done.69) | copy-start | bytes 3076
  2442.6 107.5 %copy-start.40 = (f32[16,64]{1,0:T(8,128)}, f32[16,64]{1,0:T(8,128)S(1)}, u32[]{:S(2)}) copy-start(f32[16,64]{1,0:T(8,128)S(1)} %get-tuple-element.3296) | copy-start | bytes 12292 | tf_op jit(solution)/shard_map/transpose(jvp())/while
  2443.3 106.8 %copy-start.42 = (f32[16,64]{1,0:T(8,128)}, f32[16,64]{1,0:T(8,128)S(1)}, u32[]{:S(2)}) copy-start(f32[16,64]{1,0:T(8,128)S(1)} %get-tuple-element.3295) | copy-start | bytes 12292 | tf_op jit(solution)/shard_map/transpose(jvp())/while
  2664.4 107.5 %copy-start.40 = (f32[16,64]{1,0:T(8,128)}, f32[16,64]{1,0:T(8,128)S(1)}, u32[]{:S(2)}) copy-start(f32[16,64]{1,0:T(8,128)S(1)} %get-tuple-element.3296) | copy-start | bytes 12292 | tf_op jit(solution)/shard_map/transpose(jvp())/while
  2665.1 106.8 %copy-start.42 = (f32[16,64]{1,0:T(8,128)}, f32[16,64]{1,0:T(8,128)S(1)}, u32[]{:S(2)}) copy-start(f32[16,64]{1,0:T(8,128)S(1)} %get-tuple-element.3295) | copy-start | bytes 12292 | tf_op jit(solution)/shard_map/transpose(jvp())/while
  2886.3 107.5 %copy-start.40 = (f32[16,64]{1,0:T(8,128)}, f32[16,64]{1,0:T(8,128)S(1)}, u32[]{:S(2)}) copy-start(f32[16,64]{1,0:T(8,128)S(1)} %get-tuple-element.3296) | copy-start | bytes 12292 | tf_op jit(solution)/shard_map/transpose(jvp())/while
  2887.0 106.8 %copy-start.42 = (f32[16,64]{1,0:T(8,128)}, f32[16,64]{1,0:T(8,128)S(1)}, u32[]{:S(2)}) copy-start(f32[16,64]{1,0:T(8,128)S(1)} %get-tuple-element.3295) | copy-start | bytes 12292 | tf_op jit(solution)/shard_map/transpose(jvp())/while
  3108.1 107.5 %copy-start.40 = (f32[16,64]{1,0:T(8,128)}, f32[16,64]{1,0:T(8,128)S(1)}, u32[]{:S(2)}) copy-start(f32[16,64]{1,0:T(8,128)S(1)} %get-tuple-element.3296) | copy-start | bytes 12292 | tf_op jit(solution)/shard_map/transpose(jvp())/while
  3108.9 106.8 %copy-start.42 = (f32[16,64]{1,0:T(8,128)}, f32[16,64]{1,0:T(8,128)S(1)}, u32[]{:S(2)}) copy-start(f32[16,64]{1,0:T(8,128)S(1)} %get-tuple-element.3295) | copy-start | bytes 12292 | tf_op jit(solution)/shard_map/transpose(jvp())/while
  3330.0 107.5 %copy-start.40 = (f32[16,64]{1,0:T(8,128)}, f32[16,64]{1,0:T(8,128)S(1)}, u32[]{:S(2)}) copy-start(f32[16,64]{1,0:T(8,128)S(1)} %get-tuple-element.3296) | copy-start | bytes 12292 | tf_op jit(solution)/shard_map/transpose(jvp())/while
  3330.7 106.8 %copy-start.42 = (f32[16,64]{1,0:T(8,128)}, f32[16,64]{1,0:T(8,128)S(1)}, u32[]{:S(2)}) copy-start(f32[16,64]{1,0:T(8,128)S(1)} %get-tuple-element.3295) | copy-start | bytes 12292 | tf_op jit(solution)/shard_map/transpose(jvp())/while
  3551.9 107.5 %copy-start.40 = (f32[16,64]{1,0:T(8,128)}, f32[16,64]{1,0:T(8,128)S(1)}, u32[]{:S(2)}) copy-start(f32[16,64]{1,0:T(8,128)S(1)} %get-tuple-element.3296) | copy-start | bytes 12292 | tf_op jit(solution)/shard_map/transpose(jvp())/while
  3552.6 106.8 %copy-start.42 = (f32[16,64]{1,0:T(8,128)}, f32[16,64]{1,0:T(8,128)S(1)}, u32[]{:S(2)}) copy-start(f32[16,64]{1,0:T(8,128)S(1)} %get-tuple-element.3295) | copy-start | bytes 12292 | tf_op jit(solution)/shard_map/transpose(jvp())/while
  3773.8 107.5 %copy-start.40 = (f32[16,64]{1,0:T(8,128)}, f32[16,64]{1,0:T(8,128)S(1)}, u32[]{:S(2)}) copy-start(f32[16,64]{1,0:T(8,128)S(1)} %get-tuple-element.3296) | copy-start | bytes 12292 | tf_op jit(solution)/shard_map/transpose(jvp())/while
  3774.5 106.8 %copy-start.42 = (f32[16,64]{1,0:T(8,128)}, f32[16,64]{1,0:T(8,128)S(1)}, u32[]{:S(2)}) copy-start(f32[16,64]{1,0:T(8,128)S(1)} %get-tuple-element.3295) | copy-start | bytes 12292 | tf_op jit(solution)/shard_map/transpose(jvp())/while
  3995.6 107.5 %copy-start.40 = (f32[16,64]{1,0:T(8,128)}, f32[16,64]{1,0:T(8,128)S(1)}, u32[]{:S(2)}) copy-start(f32[16,64]{1,0:T(8,128)S(1)} %get-tuple-element.3296) | copy-start | bytes 12292 | tf_op jit(solution)/shard_map/transpose(jvp())/while
  3996.3 106.8 %copy-start.42 = (f32[16,64]{1,0:T(8,128)}, f32[16,64]{1,0:T(8,128)S(1)}, u32[]{:S(2)}) copy-start(f32[16,64]{1,0:T(8,128)S(1)} %get-tuple-element.3295) | copy-start | bytes 12292 | tf_op jit(solution)/shard_map/transpose(jvp())/while
  4217.5 107.5 %copy-start.40 = (f32[16,64]{1,0:T(8,128)}, f32[16,64]{1,0:T(8,128)S(1)}, u32[]{:S(2)}) copy-start(f32[16,64]{1,0:T(8,128)S(1)} %get-tuple-element.3296) | copy-start | bytes 12292 | tf_op jit(solution)/shard_map/transpose(jvp())/while
  4218.2 106.8 %copy-start.42 = (f32[16,64]{1,0:T(8,128)}, f32[16,64]{1,0:T(8,128)S(1)}, u32[]{:S(2)}) copy-start(f32[16,64]{1,0:T(8,128)S(1)} %get-tuple-element.3295) | copy-start | bytes 12292 | tf_op jit(solution)/shard_map/transpose(jvp())/while
  4439.4 107.5 %copy-start.40 = (f32[16,64]{1,0:T(8,128)}, f32[16,64]{1,0:T(8,128)S(1)}, u32[]{:S(2)}) copy-start(f32[16,64]{1,0:T(8,128)S(1)} %get-tuple-element.3296) | copy-start | bytes 12292 | tf_op jit(solution)/shard_map/transpose(jvp())/while
  4440.1 106.8 %copy-start.42 = (f32[16,64]{1,0:T(8,128)}, f32[16,64]{1,0:T(8,128)S(1)}, u32[]{:S(2)}) copy-start(f32[16,64]{1,0:T(8,128)S(1)} %get-tuple-element.3295) | copy-start | bytes 12292 | tf_op jit(solution)/shard_map/transpose(jvp())/while
  4661.2 107.5 %copy-start.40 = (f32[16,64]{1,0:T(8,128)}, f32[16,64]{1,0:T(8,128)S(1)}, u32[]{:S(2)}) copy-start(f32[16,64]{1,0:T(8,128)S(1)} %get-tuple-element.3296) | copy-start | bytes 12292 | tf_op jit(solution)/shard_map/transpose(jvp())/while
  4662.0 106.8 %copy-start.42 = (f32[16,64]{1,0:T(8,128)}, f32[16,64]{1,0:T(8,128)S(1)}, u32[]{:S(2)}) copy-start(f32[16,64]{1,0:T(8,128)S(1)} %get-tuple-element.3295) | copy-start | bytes 12292 | tf_op jit(solution)/shard_map/transpose(jvp())/while
  4883.1 107.5 %copy-start.40 = (f32[16,64]{1,0:T(8,128)}, f32[16,64]{1,0:T(8,128)S(1)}, u32[]{:S(2)}) copy-start(f32[16,64]{1,0:T(8,128)S(1)} %get-tuple-element.3296) | copy-start | bytes 12292 | tf_op jit(solution)/shard_map/transpose(jvp())/while
  4883.8 106.8 %copy-start.42 = (f32[16,64]{1,0:T(8,128)}, f32[16,64]{1,0:T(8,128)S(1)}, u32[]{:S(2)}) copy-start(f32[16,64]{1,0:T(8,128)S(1)} %get-tuple-element.3295) | copy-start | bytes 12292 | tf_op jit(solution)/shard_map/transpose(jvp())/while
  5105.0 107.5 %copy-start.40 = (f32[16,64]{1,0:T(8,128)}, f32[16,64]{1,0:T(8,128)S(1)}, u32[]{:S(2)}) copy-start(f32[16,64]{1,0:T(8,128)S(1)} %get-tuple-element.3296) | copy-start | bytes 12292 | tf_op jit(solution)/shard_map/transpose(jvp())/while
  5105.7 106.8 %copy-start.42 = (f32[16,64]{1,0:T(8,128)}, f32[16,64]{1,0:T(8,128)S(1)}, u32[]{:S(2)}) copy-start(f32[16,64]{1,0:T(8,128)S(1)} %get-tuple-element.3295) | copy-start | bytes 12292 | tf_op jit(solution)/shard_map/transpose(jvp())/while
  5326.8 107.5 %copy-start.40 = (f32[16,64]{1,0:T(8,128)}, f32[16,64]{1,0:T(8,128)S(1)}, u32[]{:S(2)}) copy-start(f32[16,64]{1,0:T(8,128)S(1)} %get-tuple-element.3296) | copy-start | bytes 12292 | tf_op jit(solution)/shard_map/transpose(jvp())/while
  5327.6 106.8 %copy-start.42 = (f32[16,64]{1,0:T(8,128)}, f32[16,64]{1,0:T(8,128)S(1)}, u32[]{:S(2)}) copy-start(f32[16,64]{1,0:T(8,128)S(1)} %get-tuple-element.3295) | copy-start | bytes 12292 | tf_op jit(solution)/shard_map/transpose(jvp())/while
  5548.7 107.5 %copy-start.40 = (f32[16,64]{1,0:T(8,128)}, f32[16,64]{1,0:T(8,128)S(1)}, u32[]{:S(2)}) copy-start(f32[16,64]{1,0:T(8,128)S(1)} %get-tuple-element.3296) | copy-start | bytes 12292 | tf_op jit(solution)/shard_map/transpose(jvp())/while
  5549.4 106.8 %copy-start.42 = (f32[16,64]{1,0:T(8,128)}, f32[16,64]{1,0:T(8,128)S(1)}, u32[]{:S(2)}) copy-start(f32[16,64]{1,0:T(8,128)S(1)} %get-tuple-element.3295) | copy-start | bytes 12292 | tf_op jit(solution)/shard_map/transpose(jvp())/while
  5770.6 107.5 %copy-start.40 = (f32[16,64]{1,0:T(8,128)}, f32[16,64]{1,0:T(8,128)S(1)}, u32[]{:S(2)}) copy-start(f32[16,64]{1,0:T(8,128)S(1)} %get-tuple-element.3296) | copy-start | bytes 12292 | tf_op jit(solution)/shard_map/transpose(jvp())/while
  5771.3 106.8 %copy-start.42 = (f32[16,64]{1,0:T(8,128)}, f32[16,64]{1,0:T(8,128)S(1)}, u32[]{:S(2)}) copy-start(f32[16,64]{1,0:T(8,128)S(1)} %get-tuple-element.3295) | copy-start | bytes 12292 | tf_op jit(solution)/shard_map/transpose(jvp())/while
  (549 other events, 5616.0 us)
Sparse Core Ops, SparseCore 0:
  1502.8 40.4 all-gather.9
  1546.1 38.8 all-gather.11
  1587.7 38.8 all-gather.13
  1629.2 38.8 all-gather.7
  1834.5 47.8 reduce-scatter.5
  1885.6 24.8 reduce-scatter.3
  1915.0 24.8 reduce-scatter.7
  1942.3 40.2 all-gather.17
  2118.2 40.1 all-gather.15
  2160.6 38.9 all-gather.19
  5995.6 342.1 all-reduce.21
where the time goes:
time: 6410 us; the launch traced here: 6360 us
  local copies, waits for them, and re-layouts  2570 us (40%)
  other arithmetic  2350 us (37%)
  matrix products  806 us (13%)
  waiting for transfers between devices  550 us (9%)
  blocking collectives  65.5 us (1%)
    gather x64, local copies, waits for them, and re-layouts, local_one_group(): toeplitz = kernel[:, lags]  1920 us
    scatter-add x16, other arithmetic, local_one_group(): toeplitz = kernel[:, lags]  1570 us
    psum x1, waiting for transfers between devices, per_device(): lax.psum((first_gain_grad, decay_rate_grad, turn_angle_grad, out_real_gra...  314 us
    reduce_sum x32, other arithmetic, powers(): phase = angle[..., None] * steps  230 us
    dot_general x48, matrix products, carry_one_group(): jnp.einsum('gnt,bgn->btg', table_im, state_im, precision=highest)  152 us
    all_gather x7, waiting for transfers between devices, carried_in(): gathered = jax.tree.map(lambda a: lax.all_gather(a, axis), part)  147 us
    dot_general x48, matrix products, carry_one_group(): jnp.einsum('gnt,bgn->btg', table_re, state_re, precision=highest)  132 us
  transfers between devices with their start and end apart: 11, of which 8 were waited for; matrix products, arithmetic and copies ran while one was open for 8% of the time, Pallas kernels for 0%

commit v1 on v0

v1 whole, which is shorter than its diff:
```python
import functools

import jax
import jax.numpy as jnp
from jax import lax
from jax.experimental import pallas as pl
from jax.experimental.pallas import tpu as pltpu
from jax.sharding import PartitionSpec as P

epsilon = 1e-05
LANES = 128
VM = pl.BlockSpec(memory_space=pltpu.VMEM)
GELU_A = 0.7978845608028654
GELU_B = 0.044715


def gelu_parts(x):
    inner = GELU_A * (x + GELU_B * (x * x * x))
    t = jnp.tanh(inner)
    half = 0.5 * (1.0 + t)
    slope = half + 0.5 * x * (1.0 - t * t) * (GELU_A * (1.0 + 3.0 * GELU_B * (x * x)))
    return x * half, slope


def row(ref, b, p):
    return jnp.broadcast_to(ref[b, pl.ds(p, 1), :], (8, LANES))


def tile(ref, lead, rows, cols):
    return ref[(*lead, rows, cols)].reshape(-1, 8, LANES)


def cmul(ar, ai, br, bi):
    return ar * br - ai * bi, ar * bi + ai * br


def edge_kernel(x_ref, mask_ref, lam_ref, out_ref, row_ref, *, reverse, states_at_once):
    streams, length, width = x_ref.shape
    states = lam_ref.shape[1]
    for c in range(width // LANES):
        cols = pl.ds(c * LANES, LANES)
        row_ref[...] = x_ref[:, :, cols] * mask_ref[...]
        for h in range(states // states_at_once):
            rows = pl.ds(h * states_at_once, states_at_once)
            l1r = tile(lam_ref, (0,), rows, cols)
            l1i = tile(lam_ref, (1,), rows, cols)
            l1i = -l1i if reverse else l1i
            l2r, l2i = cmul(l1r, l1i, l1r, l1i)
            l3r, l3i = cmul(l2r, l2i, l1r, l1i)
            l4r, l4i = cmul(l2r, l2i, l2r, l2i)

            def step(i, carry):
                new = []
                for b in range(streams):
                    sr, si = carry[2 * b], carry[2 * b + 1]
                    base = length - 4 - 4 * i if reverse else 4 * i
                    u = []
                    for j in range(4):
                        u.append(row(row_ref, b, base + (3 - j if reverse else j)))
                    nr = (l4r * sr - l4i * si) + (l3r * u[0] + l2r * u[1]) + (l1r * u[2] + u[3])
                    ni = (l4r * si + l4i * sr) + (l3i * u[0] + l2i * u[1]) + l1i * u[2]
                    new += [nr, ni]
                return tuple(new)

            zero = jnp.zeros((states_at_once // 8, 8, LANES), jnp.float32)
            final = lax.fori_loop(0, length // 4, step, (zero,) * (2 * streams))
            for b in range(streams):
                out_ref[b, 0, rows, cols] = final[2 * b].reshape(-1, LANES)
                out_ref[b, 1, rows, cols] = final[2 * b + 1].reshape(-1, LANES)


def edge_states(values, mask, lam, reverse):
    streams, length, width = values.shape
    states = lam.shape[1]
    return pl.pallas_call(
        functools.partial(edge_kernel, reverse=reverse, states_at_once=min(32, states)),
        out_shape=jax.ShapeDtypeStruct((streams, 2, states, width), jnp.float32),
        in_specs=[VM] * 3,
        out_specs=VM,
        scratch_shapes=[pltpu.VMEM((streams, length, LANES), jnp.float32)],
        compiler_params=pltpu.CompilerParams(vmem_limit_bytes=32 * 1024 * 1024),
    )(values, mask, lam)


def forward_kernel(u_ref, keep_ref, init_ref, lam_ref, coef_ref, skip_ref, y_ref, act_ref, row_ref, part_ref):
    streams, length, width = u_ref.shape
    states = lam_ref.shape[1]
    for c in range(width // LANES):
        cols = pl.ds(c * LANES, LANES)
        every = pl.ds(0, states)
        lr, li = tile(lam_ref, (0,), every, cols), tile(lam_ref, (1,), every, cols)
        cr, ci = tile(coef_ref, (0,), every, cols), tile(coef_ref, (1,), every, cols)
        row_ref[...] = u_ref[:, :, cols]
        for b in range(streams):

            def step(p, carry):
                sr, si = carry
                u = row(row_ref, b, p)
                m = row(keep_ref, b, p)
                sr = sr * m
                si = si * m
                nr = (lr * sr - li * si) + u
                ni = lr * si + li * sr
                acc = (cr * nr - ci * ni).sum(0)
                part_ref[pl.ds(pl.multiple_of(p * 8, 8), 8), :] = acc
                return nr, ni

            start = (tile(init_ref, (b, 0), every, cols), tile(init_ref, (b, 1), every, cols))
            lax.fori_loop(0, length, step, start, unroll=2)
            total = part_ref[pl.ds(0, length, stride=8), :]
            for j in range(1, 8):
                total = total + part_ref[pl.ds(j, length, stride=8), :]
            y = total + skip_ref[:, cols] * u_ref[b, :, cols]
            y_ref[b, :, cols] = y
            act_ref[b, :, cols] = gelu_parts(y)[0].astype(jnp.bfloat16)


def forward_scan(inputs, keep, init, lam, coef, skip):
    streams, length, width = inputs.shape
    return pl.pallas_call(
        forward_kernel,
        out_shape=(
            jax.ShapeDtypeStruct(inputs.shape, jnp.float32),
            jax.ShapeDtypeStruct(inputs.shape, jnp.bfloat16),
        ),
        in_specs=[VM] * 6,
        out_specs=(VM, VM),
        scratch_shapes=[
            pltpu.VMEM((streams, length, LANES), jnp.float32),
            pltpu.VMEM((length * 8, LANES), jnp.float32),
        ],
        compiler_params=pltpu.CompilerParams(vmem_limit_bytes=32 * 1024 * 1024),
    )(inputs, keep, init, lam, coef, skip[None])


def backward_kernel(
    u_ref, g_ref, keep_ref, init_ref, adj_ref, lam_ref, coef_ref, skip_ref,
    du_ref, glam_ref, gco_ref, u_row, g_row, s_ref, part_ref, *, group,
):
    streams, length, width = u_ref.shape
    states = lam_ref.shape[1]
    zero = jnp.zeros((group // 8, 8, LANES), jnp.float32)
    for c in range(width // LANES):
        cols = pl.ds(c * LANES, LANES)
        u_row[...] = u_ref[:, :, cols]
        g_row[...] = g_ref[:, :, cols]
        for h in range(states // group):
            rows = pl.ds(h * group, group)
            lr, li = tile(lam_ref, (0,), rows, cols), tile(lam_ref, (1,), rows, cols)
            cr, ci = tile(coef_ref, (0,), rows, cols), tile(coef_ref, (1,), rows, cols)

            def again(p, carry):
                new = []
                for b in range(streams):
                    sr, si = carry[2 * b], carry[2 * b + 1]
                    u = row(u_row, b, p)
                    m = row(keep_ref, b, p)
                    sr = sr * m
                    si = si * m
                    nr = (lr * sr - li * si) + u
                    ni = lr * si + li * sr
                    s_ref[p + 1, b, 0] = nr
                    s_ref[p + 1, b, 1] = ni
                    new += [nr, ni]
                return tuple(new)

            first = []
            for b in range(streams):
                first += [tile(init_ref, (b, 0), rows, cols), tile(init_ref, (b, 1), rows, cols)]
                s_ref[0, b, 0] = first[-2]
                s_ref[0, b, 1] = first[-1]
            lax.fori_loop(0, length, again, tuple(first), unroll=2)

            def back(i, carry):
                glr, gli, gcr, gci = carry[:4]
                adj = carry[4:]
                p = length - 1 - i
                new = []
                for b in range(streams):
                    ar, ai = adj[2 * b], adj[2 * b + 1]
                    g = row(g_row, b, p)
                    m = row(keep_ref, b, p)
                    nr = (lr * ar + li * ai) + cr * g
                    ni = (lr * ai - li * ar) - ci * g
                    acc = nr.sum(0)
                    at = pl.ds(pl.multiple_of((b * length + p) * 8, 8), 8)
                    if h == 0:
                        part_ref[at, :] = acc
                    else:
                        part_ref[at, :] += acc
                    gcr = gcr + g * s_ref[p + 1, b, 0]
                    gci = gci - g * s_ref[p + 1, b, 1]
                    nr = nr * m
                    ni = ni * m
                    sr, si = s_ref[p, b, 0], s_ref[p, b, 1]
                    glr = glr + (nr * sr + ni * si)
                    gli = gli + (ni * sr - nr * si)
                    new += [nr, ni]
                return (glr, gli, gcr, gci, *new)

            start = []
            for b in range(streams):
                start += [tile(adj_ref, (b, 0), rows, cols), tile(adj_ref, (b, 1), rows, cols)]
            out = lax.fori_loop(0, length, back, (zero, zero, zero, zero, *start))
            glam_ref[0, rows, cols] = out[0].reshape(-1, LANES)
            glam_ref[1, rows, cols] = out[1].reshape(-1, LANES)
            gco_ref[0, rows, cols] = out[2].reshape(-1, LANES)
            gco_ref[1, rows, cols] = out[3].reshape(-1, LANES)
        for b in range(streams):
            total = part_ref[pl.ds(b * length * 8, length, stride=8), :]
            for j in range(1, 8):
                total = total + part_ref[pl.ds(b * length * 8 + j, length, stride=8), :]
            du_ref[b, :, cols] = total + skip_ref[:, cols] * g_ref[b, :, cols]


def backward_scan(inputs, grads, keep, init, adj, lam, coef, skip):
    streams, length, width = inputs.shape
    states = lam.shape[1]
    group = min(32, states)
    return pl.pallas_call(
        functools.partial(backward_kernel, group=group),
        out_shape=(
            jax.ShapeDtypeStruct(inputs.shape, jnp.float32),
            jax.ShapeDtypeStruct((2, states, width), jnp.float32),
            jax.ShapeDtypeStruct((2, states, width), jnp.float32),
        ),
        in_specs=[VM] * 8,
        out_specs=(VM, VM, VM),
        scratch_shapes=[
            pltpu.VMEM((streams, length, LANES), jnp.float32),
            pltpu.VMEM((streams, length, LANES), jnp.float32),
            pltpu.VMEM((length + 1, streams, 2, group // 8, 8, LANES), jnp.float32),
            pltpu.VMEM((streams * length * 8, LANES), jnp.float32),
        ],
        compiler_params=pltpu.CompilerParams(vmem_limit_bytes=40 * 1024 * 1024),
    )(inputs, grads, keep, init, adj, lam, coef, skip[None])


def carry_over(parts, flags, step, reverse):
    count = lax.axis_size("seq")
    place = lax.axis_index("seq")
    gathered = lax.all_gather(parts, "seq")
    ahead = count - 1 - place if reverse else place

    def one(turn, state):
        source = count - 1 - turn if reverse else turn
        part = lax.dynamic_index_in_dim(gathered, source, 0, False)
        flag = lax.dynamic_index_in_dim(flags, source, 0, False)[:, None, None]
        real = flag * (step[0] * state[:, 0] - step[1] * state[:, 1])
        imag = flag * (step[0] * state[:, 1] + step[1] * state[:, 0])
        return part + jnp.stack([real, imag], 1)

    return lax.fori_loop(0, ahead, one, jnp.zeros_like(parts))


def token_sums(*sums):
    return lax.psum(sums, "chan")


def per_device(
    block_in, doc_lengths, out_grad, first_gain, decay_rate, turn_angle, out_real, out_imag,
    skip_gain, glu_value, glu_gate, second_gain, ffn_in, ffn_out,
):
    streams, length, width = block_in.shape
    tokens = streams * length
    full = width * lax.axis_size("chan")
    blocks = lax.axis_size("seq")
    place = lax.axis_index("seq")

    doc_ends = jnp.cumsum(doc_lengths, axis=1)

    def segment_at(positions):
        return jnp.sum((doc_ends[:, None, :] <= positions[None, :, None]).astype(jnp.int32), axis=2)

    positions = place * length + jnp.arange(length, dtype=jnp.int32)
    segment = segment_at(positions)
    before_all = segment_at(positions - 1)
    before = before_all[:, :1]
    keep = (segment == before_all).astype(jnp.float32)
    first_mask = (segment == before).astype(jnp.float32)
    last_mask = (segment == segment[:, -1:]).astype(jnp.float32)
    valid = (positions[None, :] < doc_ends[:, -1:]).astype(jnp.float32)
    starts = jnp.arange(blocks, dtype=jnp.int32) * length
    flags = (segment_at(starts - 1) == segment_at(starts + length - 1)).astype(jnp.float32).T

    def wide(mask):
        return jnp.broadcast_to(mask[:, :, None], (streams, length, LANES))

    decay, angle = decay_rate.T, turn_angle.T
    real, imag = out_real.T, out_imag.T
    magnitude = jnp.exp(-decay)
    lam = jnp.stack([magnitude * jnp.cos(angle), magnitude * jnp.sin(angle)])
    block_mag = jnp.exp(-decay * length)
    block_step = (block_mag * jnp.cos(angle * length), block_mag * jnp.sin(angle * length))
    factor = jnp.sqrt(-jnp.expm1(-2.0 * decay))
    coef = jnp.stack([real * factor, imag * factor])

    rows = block_in.reshape(tokens, width)
    sums = token_sums(jnp.sum(rows, -1), jnp.sum(rows * rows, -1))
    average1 = sums[0] / full
    scaler1 = lax.rsqrt(sums[1] / full - average1 * average1 + epsilon)[:, None]
    normed1 = (rows - average1[:, None]) * scaler1
    valid_rows = valid.reshape(tokens, 1)
    mixer_in = (normed1 * first_gain * valid_rows).reshape(streams, length, width)

    ends = edge_states(mixer_in, wide(last_mask), lam, False)
    init = carry_over(ends, flags, block_step, False)
    mixer_out, act = forward_scan(mixer_in, wide(keep), init, lam, coef, skip_gain)
    act_full = lax.all_gather(act.reshape(tokens, width), "chan", axis=1, tiled=True)

    value_pre = jnp.dot(act_full, glu_value, preferred_element_type=jnp.float32)
    gate_pre = jnp.dot(act_full, glu_gate, preferred_element_type=jnp.float32)
    gate = jax.nn.sigmoid(gate_pre)
    resid = rows + value_pre * gate

    sums = token_sums(jnp.sum(resid, -1), jnp.sum(resid * resid, -1))
    average2 = sums[0] / full
    scaler2 = lax.rsqrt(sums[1] / full - average2 * average2 + epsilon)[:, None]
    normed2 = (resid - average2[:, None]) * scaler2
    mid = (normed2 * second_gain).astype(jnp.bfloat16)
    grad_rows = out_grad.reshape(tokens, width)
    grad_low = grad_rows.astype(jnp.bfloat16)
    mid_full = lax.all_gather(mid, "chan", axis=1, tiled=True)
    grad_full = lax.all_gather(grad_low, "chan", axis=1, tiled=True)

    hidden_pre = jnp.dot(mid_full, ffn_in, preferred_element_type=jnp.float32)
    hidden, slope = gelu_parts(hidden_pre)
    hidden = hidden.astype(jnp.bfloat16)
    part_out = jnp.dot(hidden, ffn_out, preferred_element_type=jnp.float32)
    hidden_grad = jnp.dot(grad_full, ffn_out.T, preferred_element_type=jnp.float32)
    pre_grad = (hidden_grad * slope).astype(jnp.bfloat16)
    part_grad = jnp.dot(pre_grad, ffn_in.T, preferred_element_type=jnp.float32)
    ffn_out_grad = jnp.dot(hidden.T, grad_full, preferred_element_type=jnp.float32)
    ffn_in_grad = jnp.dot(mid_full.T, pre_grad, preferred_element_type=jnp.float32)
    ffn_in_grad, ffn_out_grad = lax.psum(
        (ffn_in_grad.astype(jnp.bfloat16), ffn_out_grad.astype(jnp.bfloat16)), "seq"
    )
    mid_grad = lax.psum_scatter(part_grad, "chan", scatter_dimension=1, tiled=True)
    ffn_result = lax.psum_scatter(part_out, "chan", scatter_dimension=1, tiled=True)
    block_out = (resid + ffn_result).reshape(streams, length, width)

    second_gain_grad = jnp.sum(mid_grad * normed2, axis=0)
    scaled = mid_grad * second_gain
    sums = token_sums(jnp.sum(scaled, -1), jnp.sum(scaled * normed2, -1))
    resid_grad = grad_rows + scaler2 * (
        scaled - sums[0][:, None] / full - normed2 * (sums[1][:, None] / full)
    )

    value_grad = (resid_grad * gate).astype(jnp.bfloat16)
    gate_grad = (resid_grad * value_pre * gate * (1.0 - gate)).astype(jnp.bfloat16)
    glu_value_grad = jnp.dot(act_full.T, value_grad, preferred_element_type=jnp.float32)
    glu_gate_grad = jnp.dot(act_full.T, gate_grad, preferred_element_type=jnp.float32)
    act_part = jnp.dot(value_grad, glu_value.T, preferred_element_type=jnp.float32) + jnp.dot(
        gate_grad, glu_gate.T, preferred_element_type=jnp.float32
    )
    act_grad = lax.psum_scatter(act_part, "chan", scatter_dimension=1, tiled=True)
    mixer_grad = act_grad.reshape(streams, length, width) * gelu_parts(mixer_out)[1]

    starts_sum = edge_states(mixer_grad, wide(first_mask), lam, True)
    starts_part = jnp.stack(
        [
            coef[0] * starts_sum[:, 0] + coef[1] * starts_sum[:, 1],
            coef[0] * starts_sum[:, 1] - coef[1] * starts_sum[:, 0],
        ],
        1,
    )
    adj = carry_over(starts_part, flags, (block_step[0], -block_step[1]), True)
    mixer_in_grad, glam, gco = backward_scan(
        mixer_in, mixer_grad, wide(keep), init, adj, lam, coef, skip_gain
    )
    skip_gain_grad = jnp.sum(mixer_grad * mixer_in, axis=(0, 1))
    ratio = jnp.exp(-2.0 * decay) / factor
    decay_grad = (gco[0] * real + gco[1] * imag) * ratio - (glam[0] * lam[0] + glam[1] * lam[1])
    angle_grad = glam[1] * lam[0] - glam[0] * lam[1]
    table_grads = jnp.stack([decay_grad, angle_grad, factor * gco[0], factor * gco[1]])

    unit_grad = mixer_in_grad.reshape(tokens, width) * valid_rows
    first_gain_grad = jnp.sum(unit_grad * normed1, axis=0)
    scaled = unit_grad * first_gain
    sums = token_sums(jnp.sum(scaled, -1), jnp.sum(scaled * normed1, -1))
    in_grad = resid_grad + scaler1 * (
        scaled - sums[0][:, None] / full - normed1 * (sums[1][:, None] / full)
    )

    gains, table_grads, glu_value_grad, glu_gate_grad = lax.psum(
        (
            jnp.stack([first_gain_grad, skip_gain_grad, second_gain_grad]),
            table_grads,
            glu_value_grad,
            glu_gate_grad,
        ),
        "seq",
    )
    return (
        block_out,
        in_grad.reshape(streams, length, width),
        gains[0],
        table_grads[0].T,
        table_grads[1].T,
        table_grads[2].T,
        table_grads[3].T,
        gains[1],
        glu_value_grad,
        glu_gate_grad,
        gains[2],
        ffn_in_grad.astype(jnp.float32),
        ffn_out_grad.astype(jnp.float32),
    )


def solution(mesh):
    act = P(None, "seq", "chan")
    vec, mat = P("chan"), P("chan", None)
    col = P(None, "chan")
    return jax.shard_map(
        per_device,
        mesh=mesh,
        in_specs=(act, P(), act, vec, mat, mat, mat, mat, vec, col, col, vec, col, mat),
        out_specs=(act, act, vec, mat, mat, mat, mat, vec, col, col, vec, col, mat),
        check_vma=False,
    )
```

time: 6410 us -> 557 us (0.09)
  local copies, waits for them, and re-layouts: 2570 us -> 17.1 us
  other arithmetic: 2350 us -> 43.4 us
  matrix products: 806 us -> 22.6 us
  waiting for transfers between devices: 550 us -> 346 us
    gather x64 -> x0, local copies, waits for them, and re-layouts: 1920 us -> none  [local_one_group(): toeplitz = kernel[:, lags]]
    scatter-add x16 -> x0, other arithmetic: 1570 us -> none  [local_one_group(): toeplitz = kernel[:, lags]]
    dot_general x362 -> x10, matrix products: 803 us -> 19.4 us  [the longest x1 3.74 us: per_device(): part_out = jnp.dot(hidden, ffn_out, preferred_element_type=jnp.float32)]
    reduce_sum x101 -> x6, other arithmetic: 363 us -> 5.32 us  [the longest x1 1.84 us: per_device(): skip_gain_grad = jnp.sum(mixer_grad * mixer_in, axis=(0, 1))]
    squeeze x256 -> x0, local copies, waits for them, and re-layouts: 184 us -> none  [the longest x128 100 us: local_mix(): lax.map(jax.checkpoint(local_one_group), (grouped_in, block_decay, block_...]
    mul x97 -> x10, other arithmetic: 153 us -> 11.1 us  [the longest x7 6.74 us: one(): real = flag * (step[0] * state[:, 0] - step[1] * state[:, 1])]
    rev x96 -> x0, local copies, waits for them, and re-layouts: 129 us -> none  [the longest x48 72 us: local_one_group(): rev_re = pow_re[..., span - 1::-1]]
    psum x1 -> x2, waiting for transfers between devices: 314 us -> 192 us  [the longest x1 114 us: per_device(): lax.psum((ffn_in_grad.astype(jnp.bfloat16), ffn_out_grad.astype(jnp.bfloa...]
  transfers between devices with their start and end apart: 11 -> 7, of which waited for: 8 -> 7; matrix products, arithmetic and copies ran while one was open for 8% -> 9% of each run, Pallas kernels for 0% -> 4%
where the time goes in v1:
time: 557 us; the launch traced here: 556 us
  waiting for transfers between devices  346 us (62%)
  blocking collectives  69.8 us (13%)
  other arithmetic  43.4 us (8%)
  Pallas kernels  41.1 us (7%)
  matrix products  22.6 us (4%)
  local copies, waits for them, and re-layouts  17.1 us (3%)
  between operations  14.6 us (3%)
    psum x1, waiting for transfers between devices, per_device(): lax.psum((ffn_in_grad.astype(jnp.bfloat16), ffn_out_grad.astype(jnp.bfloa...  114 us
    all_gather x2, waiting for transfers between devices, carry_over(): gathered = lax.all_gather(parts, 'seq')  79.8 us
    psum x1, waiting for transfers between devices, per_device(): lax.psum((jnp.stack([first_gain_grad, skip_gain_grad, second_gain_grad]),...  78 us
    reduce_scatter x1, waiting for transfers between devices, per_device(): lax.psum_scatter(part_grad, 'chan', scatter_dimension=1, tiled=True)  31.9 us
    psum x4, blocking collectives, token_sums(): return lax.psum(sums, 'chan')  28.2 us
    reduce_scatter x1, waiting for transfers between devices, per_device(): lax.psum_scatter(act_part, 'chan', scatter_dimension=1, tiled=True)  25 us
    pallas_call x1, Pallas kernels, backward_scan(): pl.pallas_call(functools.partial(backward_kernel, group=group), out_shape...  24 us
    psum x1, blocking collectives, per_device(): lax.psum((jnp.stack([first_gain_grad, skip_gain_grad, second_gain_grad]),...  20.5 us
  transfers between devices with their start and end apart: 7, of which 7 were waited for; matrix products, arithmetic and copies ran while one was open for 9% of the time, Pallas kernels for 4%

profile of v1, /device:TPU:0, one launch (start us, length us, event | category | flops | bytes accessed | tf_op | source)
XLA Modules:
  0.0 555.6 jit_solution(16760311190164510330)
XLA Ops:
  7.3 1.0 reduce_window_sum.11
  9.5 1.1 fusion.46
  11.2 8.3 %all-reduce.4 = (f32[256]{0:T(256)S(1)}, f32[256]{0:T(256)S(1)}) all-reduce(f32[256]{0:T(256)S(1)} %bitcast.202, f32[256]{0:T(256)S(1)} %bitcast.201), channel_id=1, replica_groups=mesh['seq'=8,'chan'=4] {'chan'}, use_global_device_ids=true, to_apply=%region_3.4 | all-reduce | flops 512 | bytes 4096 | tf_op jit(solution)/shard_map/psum | solution.py:257
  20.1 1.3 multiply_bitcast_fusion.1
  21.5 1.9 bitcast_multiply_fusion.10
  23.3 1.2 multiply_multiply_fusion.4.x_ref.u_ref
  24.7 4.2 shard_map.237
  29.9 7.0 %all_gather.25 = bf16[256,1024]{1,0:T(8,128)(2,1)} all-gather(bf16[256,256]{1,0:T(8,128)(2,1)S(1)} %bitcast_convert_fusion), channel_id=1, replica_groups=mesh['seq'=8,'chan'=4] {'chan'}, dimensions={1}, use_global_device_ids=true | all-gather | bytes 655360 | tf_op jit(solution)/shard_map/all_gather | solution.py:324
  36.9 41.8 %all-gather.5.cloned.1.call-done = f32[16,2,64,256]{3,2,1,0:T(8,128)} async-done(((f32[2,2,64,256]{3,2,1,0:T(8,128)}), f32[16,2,64,256]{3,2,1,0:T(8,128)}) %all-gather.5.cloned.1.call-update) | async-done | bytes 2097168 | tf_op jit(solution)/shard_map/all_gather | solution.py:242
  79.5 9.3 %shard_map.238 = (f32[2,128,256]{2,1,0:T(8,128)S(1)}, bf16[2,128,256]{2,1,0:T(8,128)(2,1)S(1)}) custom-call(f32[2,128,256]{2,1,0:T(8,128)S(1)} %multiply_multiply_fusion.4.x_ref.u_ref, f32[2,128,128]{2,1,0:T(8,128)S(1)} %broadcast_in_dim.8.keep_ref, f32[2,2,64,256]{3,2,1,0:T(8,128)S(1)} %get-tuple-element.148.init_ref, ...), custom_call_target="tpu_custom_call" | custom-call | tf_op jit(solution)/shard_map/pallas_call | solution.py:120
  88.7 7.2 %all_gather.23 = bf16[256,1024]{1,0:T(8,128)(2,1)S(1)} all-gather(bf16[256,256]{1,0:T(8,128)(2,1)S(1)} %bitcast.186), channel_id=1, replica_groups=mesh['seq'=8,'chan'=4] {'chan'}, dimensions={1}, use_global_device_ids=true | all-gather | bytes 655360 | tf_op jit(solution)/shard_map/all_gather | solution.py:309
  95.9 1.5 fusion.3
  97.5 1.7 fusion.45
  99.2 6.5 %all-reduce.3 = (f32[256]{0:T(256)S(1)}, f32[256]{0:T(256)S(1)}) all-reduce(f32[256]{0:T(256)} %get-tuple-element.190, f32[256]{0:T(256)} %get-tuple-element.189), channel_id=1, replica_groups=mesh['seq'=8,'chan'=4] {'chan'}, use_global_device_ids=true, to_apply=%region_14.15 | all-reduce | flops 512 | bytes 4096 | tf_op jit(solution)/shard_map/psum | solution.py:257
  105.7 1.1 multiply_convert_fusion.3
  106.9 7.0 %all_gather.24 = bf16[256,1024]{1,0:T(8,128)(2,1)S(1)} all-gather(bf16[256,256]{1,0:T(8,128)(2,1)S(1)} %multiply_convert_fusion.3), channel_id=1, replica_groups=mesh['seq'=8,'chan'=4] {'chan'}, dimensions={1}, use_global_device_ids=true | all-gather | bytes 655360 | tf_op jit(solution)/shard_map/all_gather | solution.py:323
  115.4 1.2 fusion
  117.4 1.7 fusion.51
  119.2 3.7 fusion.44
  123.0 31.9 %reduce-scatter.6.cloned.1.call-done = f32[256,256]{1,0:T(8,128)} async-done(((f32[256,1024]{1,0:T(8,128)}), f32[256,256]{1,0:T(8,128)}) %reduce-scatter.6.cloned.1.call-update) | async-done | bytes 262160 | tf_op jit(solution)/shard_map/reduce_scatter | solution.py:338
  154.9 1.8 multiply_reduce_fusion
  156.7 6.4 %all-reduce.2 = (f32[256]{0:T(256)}, f32[256]{0:T(256)}) all-reduce(f32[256]{0:T(256)} %get-tuple-element.186, f32[256]{0:T(256)} %get-tuple-element.188), channel_id=1, replica_groups=mesh['seq'=8,'chan'=4] {'chan'}, use_global_device_ids=true, to_apply=%region_20.21 | all-reduce | flops 512 | bytes 4096 | tf_op jit(solution)/shard_map/psum | solution.py:257
  163.1 1.2 broadcast_multiply_fusion.2
  164.3 1.2 broadcast_multiply_fusion.3
  165.6 17.5 %reduce-scatter.4.cloned.1.call-done = f32[256,256]{1,0:T(8,128)} async-done(((f32[256,1024]{1,0:T(8,128)}), f32[256,256]{1,0:T(8,128)}) %reduce-scatter.4.cloned.1.call-update) | async-done | bytes 262160 | tf_op jit(solution)/shard_map/reduce_scatter | solution.py:339
  183.1 2.2 multiply_convert_fusion.1
  186.4 1.3 convolution_add_fusion
  187.8 25.0 %reduce-scatter.8.cloned.1.call-done = f32[256,256]{1,0:T(8,128)} async-done(((f32[256,1024]{1,0:T(8,128)}), f32[256,256]{1,0:T(8,128)}) %reduce-scatter.8.cloned.1.call-update) | async-done | bytes 262160 | tf_op jit(solution)/shard_map/reduce_scatter | solution.py:356
  212.7 1.8 multiply_reduce_fusion.1
  215.3 3.6 shard_map.239
  220.7 3.4 convolution_convert_fusion.1
  224.1 2.3 convolution_convert_fusion
  227.2 2.4 fusion.54
  229.6 2.4 fusion.53
  232.0 38.1 %all-gather.7.cloned.1.call-done = f32[16,2,64,256]{3,2,1,0:T(8,128)} async-done(((f32[2,2,64,256]{3,2,1,0:T(8,128)}), f32[16,2,64,256]{3,2,1,0:T(8,128)}) %all-gather.7.cloned.1.call-update) | async-done | bytes 2097168 | tf_op jit(solution)/shard_map/all_gather | solution.py:242
  270.1 18.9 %while.23 = (s32[]{:T(128)}, f32[2,2,64,256]{3,2,1,0:T(8,128)S(1)}, s32[]{:T(128)}, f32[8,2,2,64,256]{4,3,2,1,0:T(8,128)}, f32[8,2]{1,0:T(8,128)}, /*index=5*/f3...) while((s32[]{:T(128)}, f32[2,2,64,256]{3,2,1,0:T(8,128)S(1)}, ...), condition=%wide.region_23.24_spmd, body=%wide.region_22.23_spmd.sunk | while | flops 393222 | bytes 1441987 | solution.py:253
  274.4 1.0 maximum_add_fusion.5
  279.8 1.0 maximum_add_fusion.5
  289.7 24.0 %shard_map.240 = (f32[2,128,256]{2,1,0:T(8,128)S(1)}, f32[2,64,256]{2,1,0:T(8,128)S(1)}, f32[2,64,256]{2,1,0:T(8,128)S(1)}) custom-call(f32[2,128,256]{2,1,0:T(8,128)S(1)} %multiply_multiply_fusion.4.x_ref.u_ref, f32[2,128,256]{2,1,0:T(8,128)S(1)} %get-tuple-element.239.x_ref.g_ref, f32[2,128,128]{2,1,0:T(8,128)S(1)} %broadcast_in_dim.8.keep_ref, ...), custom_call_target="tpu_custom_call" | custom-call | tf_op jit(solution)/shard_map/pallas_call | solution.py:220
  313.7 1.3 fusion.30
  315.7 114.2 %all-reduce.11.cloned.1.call-done = (bf16[1024,1024]{1,0:T(8,128)(2,1)}, bf16[1024,1024]{1,0:T(8,128)(2,1)}) async-done(((bf16[1024,1024]{1,0:T(8,128)(2,1)}, bf16[1024,1024]{1,0:T(8,128)(2,1)}), (bf16[1024,1024]{1,0:T(8,128)(2,1)}, bf16[1024,1024]{1,0:T(8,128)(2,1)})) %all-reduce.11.cloned.1.call-update) | async-done | bytes 4194320 | tf_op jit(solution)/shard_map/psum | solution.py:335
  429.9 4.2 convert_element_type.102
  434.1 2.5 convert_element_type.104
  436.9 6.9 %all-reduce.1 = (f32[256]{0:T(256)S(1)}, f32[256]{0:T(256)S(1)}) all-reduce(f32[256]{0:T(256)S(1)} %bitcast.203, f32[256]{0:T(256)S(1)} %bitcast.204), channel_id=1, replica_groups=mesh['seq'=8,'chan'=4] {'chan'}, use_global_device_ids=true, to_apply=%region_27.28 | all-reduce | flops 512 | bytes 4096 | tf_op jit(solution)/shard_map/psum | solution.py:257
  443.8 20.5 %psum.106 = f32[3,256]{1,0:T(4,128)S(1)} all-reduce(f32[3,256]{1,0:T(4,128)S(1)} %pad_maximum_fusion.4), channel_id=1, replica_groups=mesh['seq'=8,'chan'=4] {'seq'}, use_global_device_ids=true, to_apply=%region_31.32 | all-reduce | flops 768 | bytes 6144 | tf_op jit(solution)/shard_map/psum | solution.py:385
  465.8 78.0 %all-reduce.9.cloned.1.call-done = (f32[4,64,256]{2,1,0:T(8,128)}, f32[1024,256]{1,0:T(8,128)}, f32[1024,256]{1,0:T(8,128)}) async-done(((f32[4,64,256]{2,1,0:T(8,128)}, f32[1024,256]{1,0:T(8,128)}, f32[1024,256]{1,0:T(8,128)}), (f32[4,64,256]{2,1,0:T(8,128)}, f32[1024,256]{1,0:T(8,128)}, f32[1024,256]{1,0:T(8,128)})) %all-reduce.9.cloned.1.call-update) | async-done | bytes 2359312 | tf_op jit(solution)/shard_map/psum | solution.py:385
  543.8 1.7 slice_bitcast_fusion
  545.5 2.3 copy.57
  (143 shorter events, 32.1 us)
Async XLA Ops:
  7.2 107.5 %copy-start = (bf16[1024,1024]{1,0:T(8,128)(2,1)S(1)}, bf16[1024,1024]{1,0:T(8,128)(2,1)}, u32[]{:S(2)}) copy-start(bf16[1024,1024]{1,0:T(8,128)(2,1)} %param.30) | copy-start | bytes 6291460
  7.2 22.7 %copy-start.24 = (f32[2,128,256]{2,1,0:T(8,128)S(1)}, f32[2,128,256]{2,1,0:T(8,128)}, u32[]{:S(2)}) copy-start(f32[2,128,256]{2,1,0:T(8,128)} %param.20) | copy-start | bytes 786436
  7.2 71.5 %all-gather.5.cloned.1.call-start = ((), (), s32[]{:S(2)}) async-start(), calls=%async_computation.6 | async-start | bytes 2359296 | tf_op jit(solution)/shard_map/all_gather | solution.py:242
  23.3 1.2 copy-start.25
  23.3 1.2 copy-start.26
  28.9 126.0 %reduce-scatter.6.cloned.1.call-start = ((), (), s32[]{:S(2)}) async-start(), calls=%async_computation.4 | async-start | bytes 1310720 | tf_op jit(solution)/shard_map/reduce_scatter | solution.py:338
  78.7 0.8 copy-start.1
  78.7 0.6 copy-start.6
  78.7 18.7 %copy-start.3 = (f32[2,128,256]{2,1,0:T(8,128)S(1)}, f32[2,128,256]{2,1,0:T(8,128)}, u32[]{:S(2)}) copy-start(f32[2,128,256]{2,1,0:T(8,128)} %param.18) | copy-start | bytes 786436
  78.7 18.7 %copy-start.14 = (bf16[1024,256]{1,0:T(8,128)(2,1)S(1)}, bf16[1024,256]{1,0:T(8,128)(2,1)}, u32[]{:S(2)}) copy-start(bf16[1024,256]{1,0:T(8,128)(2,1)} %param.27) | copy-start | bytes 1572868
  95.9 3.3 copy-start.5
  97.5 1.7 copy-start.9
  105.7 9.6 %copy-start.30 = (f32[256]{0:T(256)}, f32[256]{0:T(256)S(1)}, u32[]{:S(2)}) copy-start(f32[256]{0:T(256)S(1)} %get-tuple-element.278) | copy-start | bytes 3076
  105.7 9.7 %copy-start.31 = (f32[256]{0:T(256)}, f32[256]{0:T(256)S(1)}, u32[]{:S(2)}) copy-start(f32[256]{0:T(256)S(1)} %get-tuple-element.279) | copy-start | bytes 3076
  106.8 8.6 %copy-start.27 = (bf16[256,1024]{1,0:T(8,128)(2,1)S(1)}, bf16[256,1024]{1,0:T(8,128)(2,1)}, u32[]{:S(2)}) copy-start(bf16[256,1024]{1,0:T(8,128)(2,1)} %all_gather.25) | copy-start | bytes 1572868
  106.8 8.6 %copy-start.37 = (bf16[1024,1024]{1,0:T(8,128)(2,1)S(1)}, bf16[1024,1024]{1,0:T(8,128)(2,1)}, u32[]{:S(2)}) copy-start(bf16[1024,1024]{1,0:T(8,128)(2,1)} %param.31) | copy-start | bytes 6291460
  113.9 0.8 copy-start.7
  115.4 1.2 copy-start.21
  116.6 0.8 copy-start.16
  119.2 35.7 %copy-start.8 = (f32[256,256]{1,0:T(8,128)S(1)}, f32[256,256]{1,0:T(8,128)}, u32[]{:S(2)}) copy-start(f32[256,256]{1,0:T(8,128)} %get-tuple-element.244) | copy-start | bytes 786436
  119.2 63.9 %reduce-scatter.4.cloned.1.call-start = ((), (), s32[]{:S(2)}) async-start(), calls=%async_computation.3 | async-start | bytes 1310720 | tf_op jit(solution)/shard_map/reduce_scatter | solution.py:339
  123.0 89.8 %reduce-scatter.8.cloned.1.call-start = ((), (), s32[]{:S(2)}) async-start(), calls=%async_computation.5 | async-start | bytes 1310720 | tf_op jit(solution)/shard_map/reduce_scatter | solution.py:356
  183.1 2.3 copy-start.10
  183.1 3.0 copy-start.15
  183.1 3.3 copy-start.29
  185.3 0.7 copy-start.11
  185.3 1.0 copy-start.19
  186.0 1.7 copy-start.17
  187.7 82.3 %all-gather.7.cloned.1.call-start = ((), (), s32[]{:S(2)}) async-start(), calls=%async_computation.7 | async-start | bytes 2359296 | tf_op jit(solution)/shard_map/all_gather | solution.py:242
  220.6 209.3 %all-reduce.11.cloned.1.call-start = ((), (), s32[]{:S(2)}) async-start(), calls=%async_computation.9 | async-start | bytes 8388608 | tf_op jit(solution)/shard_map/psum | solution.py:335
  220.6 3.4 copy-start.22
  220.7 3.4 copy-start.28
  226.3 0.9 copy-start.20
  226.3 3.3 copy-start.18
  226.4 317.5 %all-reduce.9.cloned.1.call-start = ((), (), s32[]{:S(2)}) async-start(), calls=%async_computation.8 | async-start | bytes 4718592 | tf_op jit(solution)/shard_map/psum | solution.py:385
  289.0 0.7 copy-start.2
  429.9 4.2 copy-start.13
  434.1 2.5 copy-start.4
  434.1 2.5 copy-start.32
  434.1 9.7 %copy-start.33 = (f32[256]{0:T(256)S(1)}, f32[256]{0:T(256)}, u32[]{:S(2)}) copy-start(f32[256]{0:T(256)} %get-tuple-element.185) | copy-start | bytes 3076
  434.1 9.7 %copy-start.34 = (f32[256]{0:T(256)S(1)}, f32[256]{0:T(256)}, u32[]{:S(2)}) copy-start(f32[256]{0:T(256)} %get-tuple-element.238) | copy-start | bytes 3076
  434.1 30.8 %copy-start.12 = (f32[256,256]{1,0:T(8,128)S(1)}, f32[256,256]{1,0:T(8,128)}, u32[]{:S(2)}) copy-start(f32[256,256]{1,0:T(8,128)} %copy-done.11) | copy-start | bytes 786436
  434.1 30.8 %copy-start.35 = (f32[256]{0:T(256)S(1)}, f32[256]{0:T(256)}, u32[]{:S(2)}) copy-start(f32[256]{0:T(256)} %get-tuple-element.270) | copy-start | bytes 3076
  434.1 30.8 %copy-start.36 = (f32[256]{0:T(256)S(1)}, f32[256]{0:T(256)}, u32[]{:S(2)}) copy-start(f32[256]{0:T(256)} %get-tuple-element.272) | copy-start | bytes 3076
  543.8 4.0 copy-start.23
Sparse Core Ops, SparseCore 0:
  29.0 49.5 all-gather.4
  119.3 35.5 reduce-scatter.5
  158.2 24.8 reduce-scatter.3
  187.8 24.8 reduce-scatter.7
  220.7 49.2 all-gather.6
  274.7 155.1 all-reduce.10
  434.8 108.9 all-reduce.8

commit v2 on v1

v2 whole, which is shorter than its diff:
```python
import functools

import jax
import jax.numpy as jnp
from jax import lax
from jax.experimental import pallas as pl
from jax.experimental.pallas import tpu as pltpu
from jax.sharding import PartitionSpec as P

epsilon = 1e-05
LANES = 128
MESH = pl.DeviceIdType.MESH
VM = pl.BlockSpec(memory_space=pltpu.VMEM)
ANY = pl.BlockSpec(memory_space=pl.ANY)
GELU_A = 0.7978845608028654
GELU_B = 0.044715
NN = (((1,), (0,)), ((), ()))
NT = (((1,), (1,)), ((), ()))
SLOTS = 15
f32, bf16 = jnp.float32, jnp.bfloat16


def gelu_parts(x):
    inner = GELU_A * (x + GELU_B * (x * x * x))
    t = jnp.tanh(inner)
    half = 0.5 * (1.0 + t)
    slope = half + 0.5 * x * (1.0 - t * t) * (GELU_A * (1.0 + 3.0 * GELU_B * (x * x)))
    return x * half, slope


def dot(a, b, dims=NN):
    return lax.dot_general(a, b, dims, preferred_element_type=f32)


def cmul(ar, ai, br, bi):
    return ar * br - ai * bi, ar * bi + ai * br


def power(re, im, count):
    out = None
    while count:
        if count & 1:
            out = (re, im) if out is None else cmul(*out, re, im)
        re, im = cmul(re, im, re, im)
        count >>= 1
    return out


def row(ref, b, p):
    return jnp.broadcast_to(ref[b, pl.ds(p, 1), :], (8, LANES))


def tile(ref, lead, rows, cols):
    return ref[(*lead, rows, cols)].reshape(-1, 8, LANES)


class Ring:
    def __init__(self, sign, left, right, out, cols, first, buf, send, recv, count, place, to):
        self.left, self.right, self.out, self.cols = left, right, out, cols
        self.first, self.buf, self.send, self.recv = first, buf, send, recv
        self.count, self.to = count, to
        self.place = place if sign > 0 else lax.rem(count - place, count)
        self.rows = left.shape[0] // count

    def chunk(self, t):
        c = lax.rem(self.place - t + 2 * self.count, self.count)
        return pl.ds(pl.multiple_of(c * self.rows, self.rows), self.rows)

    def own(self, t):
        return dot(self.left[self.chunk(t), :], self.right[:, self.cols])

    def copy(self, src, dst, t):
        return pltpu.make_async_remote_copy(
            src_ref=src, dst_ref=dst, send_sem=self.send.at[t], recv_sem=self.recv.at[t],
            device_id=self.to, device_id_type=MESH,
        )

    def arrived(self, t):
        self.copy(self.first, self.first, t).wait_recv()

    def head(self, t):
        self.first[...] = self.own(t).astype(bf16)
        self.copy(self.first, self.buf.at[t], t).start()

    def reduce(self, t):
        total = self.own(t)
        self.arrived(t - 1)
        self.buf[t - 1] = (total + self.buf[t - 1].astype(f32)).astype(bf16)
        self.copy(self.buf.at[t - 1], self.buf.at[t], t).start()

    def turn(self, t):
        total = self.own(t)
        self.arrived(t - 1)
        self.out[self.chunk(t), self.cols] = (total + self.buf[t - 1].astype(f32)).astype(bf16)
        self.spread(t)

    def spread(self, t):
        part = self.out.at[self.chunk(t), self.cols]
        self.copy(part, part, t).start()

    def gather(self, t):
        self.arrived(t - 1)
        self.spread(t)

    def run(self, start, stop):
        n = self.count

        def many(lo, hi, body):
            lo, hi = max(start, lo), min(stop, hi)
            if hi - lo == 1:
                body(lo)
            elif hi > lo:
                lax.fori_loop(lo, hi, lambda t, none: body(t), None)

        many(0, 1, self.head)
        many(1, n - 1, self.reduce)
        many(n - 1, n, self.turn)
        many(n, 2 * n - 2, self.gather)
        many(2 * n - 2, 2 * n - 1, lambda t: self.arrived(t - 1))

    def slot(self, i):
        total = 2 * self.count - 1
        self.run(i * total // SLOTS, (i + 1) * total // SLOTS)

    def finish(self):
        def sent(t, none):
            self.copy(self.first, self.first, t).wait_send()

        lax.fori_loop(0, 2 * self.count - 2, sent, None)


def block_kernel(
    sizes,
    docs, x_ref, og_ref, gain1, dec_ref, ang_ref, real_ref, imag_ref, skip_ref, gluv_hbm, glug_hbm, gain2, win_hbm, wout_hbm,
    block_out, in_grad, tables_out, gains_out, gin_out, gout_out, gv_out, gg_out,
    gluv, glug, win, wout,
    keep, first_mask, last_mask, valid,
    param, lam, coef, step_l, factor,
    normed1, u_ref, y_ref, edge_sum, init, adj,
    act_full, val, gate, resid, normed2, grad_full, mid_full, hidden_grad, hidden, pre,
    act_t, mid_t, hidden_t, part_own, mid_grad, out_own, resid_grad, value_grad, gate_grad, act_own, mixer_grad, du,
    row_a, row_b, part, states,
    stat_send, stat_recv, rs_send, rs_recv,
    pair_send, pair_recv, line_send, line_recv, back_send, back_low, back_recv,
    table, table_recv, table_line, table_back,
    first_in, buf_in, first_out, buf_out, first_v, buf_v, first_g, buf_g,
    load_sem, chan_send, chan_recv, seq_send, seq_recv, ring_send, ring_recv,
):
    n_seq, n_chan = sizes
    pairs = n_seq // 2
    streams, length, width = x_ref.shape
    n_states = lam.shape[1]
    tokens = streams * length
    full = width * n_chan
    units = win.shape[1]
    group = states.shape[3] * 8
    s, c = lax.axis_index("seq"), lax.axis_index("chan")
    odd = lax.rem(s, 2)
    level = lax.div(s, 2)
    partner = (s + 1 - 2 * odd, c)
    every = pl.ds(0, n_states)

    def chan_peer(j):
        return lax.rem(c + j, n_chan)

    def chan_block(k, size):
        return pl.ds(pl.multiple_of(k * size, size), size)

    own_cols = chan_block(c, width)

    barrier = pltpu.get_barrier_semaphore()
    for j in range(1, n_chan):
        pl.semaphore_signal(barrier, inc=1, device_id=(s, chan_peer(j)), device_id_type=MESH)
    pl.semaphore_signal(barrier, inc=1, device_id=partner, device_id_type=MESH)
    for d in range(1, pairs):
        other = 2 * lax.rem(level + d, pairs) + odd
        pl.semaphore_signal(barrier, inc=1, device_id=(other, c), device_id_type=MESH)

    loads = [
        pltpu.make_async_copy(src, dst, load_sem.at[i])
        for i, (src, dst) in enumerate(
            ((wout_hbm, wout), (gluv_hbm, gluv), (glug_hbm, glug), (win_hbm, win))
        )
    ]
    for load in loads:
        load.start()

    sent = []

    def chan_copy(src, dst, phase, j):
        return pltpu.make_async_remote_copy(
            src_ref=src, dst_ref=dst, send_sem=chan_send.at[phase, j - 1], recv_sem=chan_recv.at[phase, j - 1],
            device_id=(s, chan_peer(j)), device_id_type=MESH,
        )

    def chan_all(pick, phase):
        copies = []
        for j in range(1, n_chan):
            copy = chan_copy(*pick(j), phase, j)
            copy.start()
            copies.append(copy)
        sent.extend(copies)
        return copies

    def landed(copies):
        for copy in copies:
            copy.wait_recv()

    lane = lax.broadcasted_iota(jnp.int32, (tokens, LANES), 1)

    def stats_start(first, second, k, phase):
        packed = jnp.where(lane == 0, first, jnp.where(lane == 1, second, 0.0))
        stat_send[k] = packed.T[:8]
        return chan_all(lambda j: (stat_send.at[k], stat_recv.at[k, j - 1]), phase)

    def stats_end(copies, k):
        landed(copies)
        total = stat_send[k]
        for j in range(1, n_chan):
            total = total + stat_recv[k, j - 1]
        total = jnp.concatenate([total, jnp.zeros((LANES - 8, tokens), f32)], axis=0).T
        return total[:, 0:1] / full, total[:, 1:2] / full

    rows_in = x_ref[...].reshape(tokens, width)
    grad_full[:, own_cols] = og_ref[...].reshape(tokens, width).astype(bf16)
    sum1 = jnp.sum(rows_in, axis=1, keepdims=True)
    square1 = jnp.sum(rows_in * rows_in, axis=1, keepdims=True)
    pl.semaphore_wait(barrier, n_chan + pairs - 1)
    stat_copies = stats_start(sum1, square1, 0, 0)
    grad_copies = chan_all(lambda j: (grad_full.at[:, own_cols], grad_full.at[:, own_cols]), 1)

    start = s * length
    ends = []
    for b in range(streams):
        total, stream = 0, []
        for k in range(docs.shape[1]):
            total = total + docs[b, k]
            stream.append(total)
        ends.append(stream)

    def passed(b, at):
        count = jnp.int32(0)
        for end in ends[b]:
            count = count + jnp.where(end <= at, 1, 0)
        return count

    def kept(block, b):
        return jnp.where(
            passed(b, block * length - 1) == passed(b, block * length + length - 1), 1.0, 0.0
        )

    position = lax.broadcasted_iota(jnp.int32, (length, LANES), 0) + start
    for b in range(streams):
        here = jnp.zeros((length, LANES), jnp.int32)
        prior = jnp.zeros((length, LANES), jnp.int32)
        for end in ends[b]:
            here = here + jnp.where(position >= end, 1, 0)
            prior = prior + jnp.where(position > end, 1, 0)
        keep[b] = jnp.where(here == prior, 1.0, 0.0)
        first_mask[b] = jnp.where(here == passed(b, start - 1), 1.0, 0.0)
        last_mask[b] = jnp.where(here == passed(b, start + length - 1), 1.0, 0.0)
        valid[b] = jnp.where(position < ends[b][-1], 1.0, 0.0)

    param[0:2] = jnp.concatenate([dec_ref[...], ang_ref[...]], axis=1).T.reshape(2, n_states, width)
    param[2:4] = jnp.concatenate([real_ref[...], imag_ref[...]], axis=1).T.reshape(2, n_states, width)
    decay, angle = param[0], param[1]
    magnitude = jnp.exp(-decay)
    a2 = angle * angle
    sine, cosine = jnp.ones_like(a2), jnp.ones_like(a2)
    for k in (13, 11, 9, 7, 5, 3):
        sine = 1.0 - sine * a2 * (1.0 / (k * (k - 1)))
    for k in (14, 12, 10, 8, 6, 4, 2):
        cosine = 1.0 - cosine * a2 * (1.0 / (k * (k - 1)))
    lam[0] = magnitude * cosine
    lam[1] = magnitude * (sine * angle)
    twice = 2.0 * decay
    series = jnp.ones_like(twice)
    for k in (9, 8, 7, 6, 5, 4, 3, 2):
        series = 1.0 - series * twice * (1.0 / k)
    factor[...] = jnp.sqrt(twice * series)
    coef[0] = param[2] * factor[...]
    coef[1] = param[3] * factor[...]
    step_l[0], step_l[1] = power(lam[0], lam[1], length)

    average, square = stats_end(stat_copies, 0)
    scaler1 = lax.rsqrt(square - average * average + epsilon)
    normed1[...] = (rows_in - average) * scaler1
    for b in range(streams):
        rows = slice(b * length, (b + 1) * length)
        for k in range(width // LANES):
            cols = slice(k * LANES, (k + 1) * LANES)
            u_ref[b, :, cols] = normed1[rows, cols] * gain1[:, cols] * valid[b]

    def edges(values, mask, reverse):
        for k in range(width // LANES):
            cols = pl.ds(k * LANES, LANES)
            row_a[...] = values[:, :, cols] * mask[...]
            for h in range(n_states // group):
                rows = pl.ds(h * group, group)
                l1r, l1i = tile(lam, (0,), rows, cols), tile(lam, (1,), rows, cols)
                l1i = -l1i if reverse else l1i
                l2r, l2i = cmul(l1r, l1i, l1r, l1i)
                l3r, l3i = cmul(l2r, l2i, l1r, l1i)
                l4r, l4i = cmul(l2r, l2i, l2r, l2i)

                def move(i, carry):
                    new = []
                    for b in range(streams):
                        sr, si = carry[2 * b], carry[2 * b + 1]
                        base = length - 4 - 4 * i if reverse else 4 * i
                        u = [row(row_a, b, base + (3 - j if reverse else j)) for j in range(4)]
                        nr = (l4r * sr - l4i * si) + (l3r * u[0] + l2r * u[1]) + (l1r * u[2] + u[3])
                        ni = (l4r * si + l4i * sr) + (l3i * u[0] + l2i * u[1]) + l1i * u[2]
                        new += [nr, ni]
                    return tuple(new)

                zero = jnp.zeros((group // 8, 8, LANES), f32)
                final = lax.fori_loop(0, length // 4, move, (zero,) * (2 * streams))
                cr, ci = tile(coef, (0,), rows, cols), tile(coef, (1,), rows, cols)
                for b in range(streams):
                    fr, fi = final[2 * b], final[2 * b + 1]
                    if reverse:
                        fr, fi = cmul(cr, -ci, fr, fi)
                    edge_sum[b, 0, rows, cols] = fr.reshape(-1, LANES)
                    edge_sum[b, 1, rows, cols] = fi.reshape(-1, LANES)

    def carry_over(target, which, reverse, fill):
        def seq_copy(src, dst, k, to):
            return pltpu.make_async_remote_copy(
                src_ref=src, dst_ref=dst, send_sem=seq_send.at[which, k], recv_sem=seq_recv.at[which, k],
                device_id=to, device_id_type=MESH,
            )

        sr = step_l[0]
        si = -step_l[1] if reverse else step_l[1]
        dr, di = cmul(sr, si, sr, si)
        leads = odd == (1 if reverse else 0)
        pair_send[which] = edge_sum[...].astype(bf16)
        across = seq_copy(pair_send.at[which], pair_recv.at[which], 0, partner)
        across.start()
        fill(0)
        across.wait_recv()
        lead = 2 * level + (1 if reverse else 0)
        trail = 2 * level + (0 if reverse else 1)

        def advance(flag, vr, vi, ur, ui):
            r, i = cmul(ur, ui, vr, vi)
            return r * flag, i * flag

        mine_r, mine_i = edge_sum[odd, 0], edge_sum[odd, 1]
        other_r, other_i = pair_recv[which, odd, 0].astype(f32), pair_recv[which, odd, 1].astype(f32)
        flag = jnp.where(odd == 1, kept(trail, 1), kept(trail, 0))
        lr, li = jnp.where(leads, mine_r, other_r), jnp.where(leads, mine_i, other_i)
        tr, ti = jnp.where(leads, other_r, mine_r), jnp.where(leads, other_i, mine_i)
        ar, ai = advance(flag, lr, li, sr, si)
        line_send[which, 0] = (ar + tr).astype(bf16)
        line_send[which, 1] = (ai + ti).astype(bf16)
        for d in range(1, pairs):
            to = level - d if reverse else level + d

            @pl.when(to >= 0 if reverse else to < pairs)
            def _(d=d, to=to):
                seq_copy(line_send.at[which], line_recv.at[which, d - 1], 1 + d, (2 * to + odd, c)).start()

        fill(1)
        back_send[which] = jnp.zeros(back_send.shape[1:], f32)
        for d in range(pairs - 1, 0, -1):
            source = level + d if reverse else level - d

            @pl.when(source < pairs if reverse else source >= 0)
            def _(d=d, source=source):
                seq_copy(line_send.at[which], line_recv.at[which, d - 1], 1 + d, partner).wait_recv()
                both = [kept(2 * source, b) * kept(2 * source + 1, b) for b in (0, 1)]
                flag = jnp.where(odd == 1, both[1], both[0])
                vr, vi = advance(flag, back_send[which, 0], back_send[which, 1], dr, di)
                back_send[which, 0] = vr + line_recv[which, d - 1, 0].astype(f32)
                back_send[which, 1] = vi + line_recv[which, d - 1, 1].astype(f32)

        back_low[which] = back_send[which].astype(bf16)
        home = seq_copy(back_low.at[which], back_recv.at[which], 1, partner)
        home.start()
        fill(2)
        home.wait_recv()
        for b in range(streams):
            flag = kept(lead, b)
            for k in range(2):
                target[b, k] = jnp.where(odd == b, back_send[which, k], back_recv[which, k].astype(f32))
            vr, vi = advance(flag, target[b, 0], target[b, 1], sr, si)
            vr = vr + pair_recv[which, b, 0].astype(f32)
            vi = vi + pair_recv[which, b, 1].astype(f32)
            target[b, 0] = jnp.where(leads, target[b, 0], vr)
            target[b, 1] = jnp.where(leads, target[b, 1], vi)

        def done():
            across.wait_send()
            home.wait_send()
            for d in range(1, pairs):
                to = level - d if reverse else level + d

                @pl.when(to >= 0 if reverse else to < pairs)
                def _(d=d):
                    seq_copy(line_send.at[which], line_recv.at[which, d - 1], 1 + d, partner).wait_send()

        return done

    place = jnp.where(odd == 0, level, n_seq - 1 - level)

    def ring_device(q):
        return (jnp.where(q < pairs, 2 * q, 2 * (n_seq - 1 - q) + 1), c)

    after = ring_device(lax.rem(place + 1, n_seq))
    ahead = ring_device(lax.rem(place + n_seq - 1, n_seq))
    half = units // 2
    rings = []
    for sign, left, right, out, first, buf in (
        (1, mid_t, pre, gin_out, first_in, buf_in),
        (-1, hidden_t, grad_full, gout_out, first_out, buf_out),
    ):
        for k in range(2):
            size = right.shape[1] // 2
            i = len(rings)
            rings.append(
                Ring(sign, left, right, out, pl.ds(k * size, size), first.at[k], buf.at[k], ring_send.at[i], ring_recv.at[i],
                     n_seq, place, after if sign > 0 else ahead)
            )
    rings = [rings[0], rings[2], rings[1], rings[3]]
    glu_rings = [
        Ring(1, act_t, value_grad, gv_out, pl.ds(0, width), first_v, buf_v, ring_send.at[4], ring_recv.at[4], n_seq, place, after),
        Ring(-1, act_t, gate_grad, gg_out, pl.ds(0, width), first_g, buf_g, ring_send.at[5], ring_recv.at[5], n_seq, place, ahead),
    ]
    at = [0, 0]

    def move_rings(count=1):
        for _ in range(count):
            if at[0] < SLOTS:
                for ring in rings:
                    ring.slot(at[0])
                at[0] += 1

    def move_glu(count=1):
        for _ in range(count):
            if at[1] < SLOTS:
                for ring in glu_rings:
                    ring.slot(at[1])
                at[1] += 1

    edges(u_ref, last_mask, False)
    unit_block = min(units, 256)

    def hidden_grad_part(i):
        cols = pl.ds(i * unit_block, unit_block)
        hidden_grad[:, cols] = dot(grad_full[...], wout[cols, :], NT)

    def fill_forward(i):
        if i == 0:
            loads[0].wait()
            landed(grad_copies)
        count = units // unit_block
        for k in range(i * count // 3, (i + 1) * count // 3):
            hidden_grad_part(k)

    carry_done = [carry_over(init, 0, False, fill_forward)]
    act_copies = []
    for k in range(width // LANES):
        cols = pl.ds(k * LANES, LANES)
        lr, li = tile(lam, (0,), every, cols), tile(lam, (1,), every, cols)
        cr, ci = tile(coef, (0,), every, cols), tile(coef, (1,), every, cols)
        row_a[...] = u_ref[:, :, cols]
        for b in range(streams):

            def move(p, carry, b=b, lr=lr, li=li, cr=cr, ci=ci):
                sr, si = carry
                u = row(row_a, b, p)
                m = row(keep, b, p)
                sr = sr * m
                si = si * m
                nr = (lr * sr - li * si) + u
                ni = lr * si + li * sr
                part[pl.ds(pl.multiple_of(p * 8, 8), 8), :] = (cr * nr - ci * ni).sum(0)
                return nr, ni

            begin = (tile(init, (b, 0), every, cols), tile(init, (b, 1), every, cols))
            lax.fori_loop(0, length, move, begin, unroll=2)
            total = part[pl.ds(0, length, stride=8), :]
            for j in range(1, 8):
                total = total + part[pl.ds(j, length, stride=8), :]
            y = total + skip_ref[:, cols] * u_ref[b, :, cols]
            y_ref[b, :, cols] = y
            to = pl.ds(pl.multiple_of(c * width + k * LANES, LANES), LANES)
            act_full[b * length : (b + 1) * length, to] = gelu_parts(y)[0].astype(bf16)
        act_copies.append(chan_all(lambda j: (act_full.at[:, to], act_full.at[:, to]), 2 + k))
    base = 2 + width // LANES

    loads[1].wait()
    loads[2].wait()
    for copies in act_copies:
        landed(copies)
    val[...] = dot(act_full[...], gluv[...])
    gate[...] = jax.nn.sigmoid(dot(act_full[...], glug[...]))
    resid[...] = rows_in_of(x_ref, tokens, width) + val[...] * gate[...]

    sum2 = jnp.sum(resid[...], axis=1, keepdims=True)
    square2 = jnp.sum(resid[...] * resid[...], axis=1, keepdims=True)
    stat_copies = stats_start(sum2, square2, 1, base)
    for k in range(n_chan):
        act_t[pl.ds(k * width, width), :] = act_full[:, k * width : (k + 1) * width].T
    average, square = stats_end(stat_copies, 1)
    scaler2 = lax.rsqrt(square - average * average + epsilon)
    normed2[...] = (resid[...] - average) * scaler2
    mid_full[:, own_cols] = (normed2[...] * gain2[...]).astype(bf16)
    mid_copies = chan_all(lambda j: (mid_full.at[:, own_cols], mid_full.at[:, own_cols]), base + 1)
    loads[3].wait()
    landed(mid_copies)

    for k in range(units // unit_block):
        cols = pl.ds(k * unit_block, unit_block)
        value, slope = gelu_parts(dot(mid_full[...], win[:, cols]))
        hidden[:, cols] = value.astype(bf16)
        pre[:, cols] = (hidden_grad[:, cols] * slope).astype(bf16)
        hidden_t[cols, :] = hidden[:, cols].T
    for k in range(n_chan):
        mid_t[pl.ds(k * width, width), :] = mid_full[:, k * width : (k + 1) * width].T
    move_rings()

    def scatter_start(piece, own, k, phase):
        copies = []
        for j in range(1, n_chan):
            rs_send[k, j - 1] = piece(chan_block(chan_peer(j), width)).astype(bf16)
            copy = chan_copy(rs_send.at[k, j - 1], rs_recv.at[k, j - 1], phase, j)
            copy.start()
            copies.append(copy)
        sent.extend(copies)
        own[...] = piece(own_cols)
        return copies

    def scatter_end(copies, own, k):
        landed(copies)
        total = own[...]
        for j in range(1, n_chan):
            total = total + rs_recv[k, j - 1].astype(f32)
        return total

    grad_parts = scatter_start(lambda rows: dot(pre[...], win[rows, :], NT), part_own, 0, base + 2)
    out_parts = scatter_start(lambda cols: dot(hidden[...], wout[:, cols]), out_own, 1, base + 3)
    move_rings()

    mid_grad[...] = scatter_end(grad_parts, part_own, 0)
    scaled = mid_grad[...] * gain2[...]
    stat_copies = stats_start(
        jnp.sum(scaled, axis=1, keepdims=True),
        jnp.sum(scaled * normed2[...], axis=1, keepdims=True), 2, base + 4,
    )
    gains = jnp.sum(mid_grad[...] * normed2[...], axis=0, keepdims=True)
    first, second = stats_end(stat_copies, 2)
    resid_grad[...] = og_ref[...].reshape(tokens, width) + scaler2 * (
        mid_grad[...] * gain2[...] - first - normed2[...] * second
    )

    value_grad[...] = (resid_grad[...] * gate[...]).astype(bf16)
    gate_grad[...] = (resid_grad[...] * val[...] * gate[...] * (1.0 - gate[...])).astype(bf16)
    act_parts = scatter_start(
        lambda rows: dot(value_grad[...], gluv[rows, :], NT) + dot(gate_grad[...], glug[rows, :], NT), act_own, 2, base + 5
    )
    move_rings()
    move_glu()
    act_grad = scatter_end(act_parts, act_own, 2)
    mixer_grad[...] = act_grad.reshape(streams, length, width) * gelu_parts(y_ref[...])[1]

    edges(mixer_grad, first_mask, True)
    move_rings()
    move_glu()

    def fill_backward(i):
        if i == 0:
            total = scatter_end(out_parts, out_own, 1)
            block_out[...] = (resid[...] + total).reshape(streams, length, width)
        move_rings()
        move_glu()

    carry_done.append(carry_over(adj, 1, True, fill_backward))
    zero = jnp.zeros((group // 8, 8, LANES), f32)
    for k in range(width // LANES):
        cols = pl.ds(k * LANES, LANES)
        row_a[...] = u_ref[:, :, cols]
        row_b[...] = mixer_grad[:, :, cols]
        for h in range(n_states // group):
            rows = pl.ds(h * group, group)
            lr, li = tile(lam, (0,), rows, cols), tile(lam, (1,), rows, cols)
            cr, ci = tile(coef, (0,), rows, cols), tile(coef, (1,), rows, cols)

            def again(p, carry, lr=lr, li=li):
                new = []
                for b in range(streams):
                    sr, si = carry[2 * b], carry[2 * b + 1]
                    u = row(row_a, b, p)
                    m = row(keep, b, p)
                    sr = sr * m
                    si = si * m
                    nr = (lr * sr - li * si) + u
                    ni = lr * si + li * sr
                    states[p + 1, b, 0] = nr
                    states[p + 1, b, 1] = ni
                    new += [nr, ni]
                return tuple(new)

            begin = []
            for b in range(streams):
                begin += [tile(init, (b, 0), rows, cols), tile(init, (b, 1), rows, cols)]
                states[0, b, 0] = begin[-2]
                states[0, b, 1] = begin[-1]
            lax.fori_loop(0, length, again, tuple(begin), unroll=2)

            def back(i, carry, h=h, lr=lr, li=li, cr=cr, ci=ci):
                glr, gli, gcr, gci = carry[:4]
                adjoint = carry[4:]
                p = length - 1 - i
                new = []
                for b in range(streams):
                    ar, ai = adjoint[2 * b], adjoint[2 * b + 1]
                    g = row(row_b, b, p)
                    m = row(keep, b, p)
                    nr = (lr * ar + li * ai) + cr * g
                    ni = (lr * ai - li * ar) - ci * g
                    spot = pl.ds(pl.multiple_of((b * length + p) * 8, 8), 8)
                    if h == 0:
                        part[spot, :] = nr.sum(0)
                    else:
                        part[spot, :] += nr.sum(0)
                    gcr = gcr + g * states[p + 1, b, 0]
                    gci = gci - g * states[p + 1, b, 1]
                    nr = nr * m
                    ni = ni * m
                    sr, si = states[p, b, 0], states[p, b, 1]
                    glr = glr + (nr * sr + ni * si)
                    gli = gli + (ni * sr - nr * si)
                    new += [nr, ni]
                return (glr, gli, gcr, gci, *new)

            begin = []
            for b in range(streams):
                begin += [tile(adj, (b, 0), rows, cols), tile(adj, (b, 1), rows, cols)]
            sums = lax.fori_loop(0, length, back, (zero, zero, zero, zero, *begin))
            glr, gli, gcr, gci = [item.reshape(-1, LANES) for item in sums[:4]]
            share = factor[rows, cols]
            ratio = (1.0 - share * share) / share
            spots = [pl.ds(i * n_states + h * group, group) for i in range(4)]
            table[spots[0], cols] = (gcr * param[2, rows, cols] + gci * param[3, rows, cols]) * ratio - (
                glr * lam[0, rows, cols] + gli * lam[1, rows, cols]
            )
            table[spots[1], cols] = gli * lam[0, rows, cols] - glr * lam[1, rows, cols]
            table[spots[2], cols] = share * gcr
            table[spots[3], cols] = share * gci
            move_rings()
            move_glu()
        for b in range(streams):
            total = part[pl.ds(b * length * 8, length, stride=8), :]
            for j in range(1, 8):
                total = total + part[pl.ds(b * length * 8 + j, length, stride=8), :]
            u_grad = total + skip_ref[:, cols] * row_b[b]
            du[b * length : (b + 1) * length, cols] = u_grad * valid[b]

    scaled = du[...] * gain1[...]
    stat_copies = stats_start(
        jnp.sum(scaled, axis=1, keepdims=True),
        jnp.sum(scaled * normed1[...], axis=1, keepdims=True), 3, base + 6,
    )
    gain_rows = [
        jnp.sum(du[...] * normed1[...], axis=0, keepdims=True),
        jnp.sum(jnp.sum(mixer_grad[...] * u_ref[...], axis=0), axis=0, keepdims=True),
        gains,
    ]
    table[4 * n_states :, :] = jnp.concatenate(
        [*gain_rows, jnp.zeros((table.shape[0] - 4 * n_states - 3, width), f32)], axis=0
    )

    def table_copy(src, dst, k, to):
        return pltpu.make_async_remote_copy(
            src_ref=src, dst_ref=dst, send_sem=seq_send.at[2, k], recv_sem=seq_recv.at[2, k],
            device_id=to, device_id_type=MESH,
        )

    swap = table_copy(table, table_recv, 0, partner)
    swap.start()
    first, second = stats_end(stat_copies, 3)
    in_grad[...] = (
        resid_grad[...] + scaler1 * (du[...] * gain1[...] - first - normed1[...] * second)
    ).reshape(streams, length, width)
    move_rings()
    move_glu()
    swap.wait()
    half_rows = table.shape[0] // 2
    mine = pl.ds(pl.multiple_of(odd * half_rows, 8), half_rows)
    table_line[level] = table[mine, :] + table_recv[mine, :]
    lines = []
    for d in range(1, pairs):
        to = 2 * lax.rem(level + d, pairs) + odd
        copy = pltpu.make_async_remote_copy(
            src_ref=table_line.at[level], dst_ref=table_line.at[level],
            send_sem=seq_send.at[2, 1 + d], recv_sem=seq_recv.at[2, 1 + d],
            device_id=(to, c), device_id_type=MESH,
        )
        copy.start()
        lines.append(copy)
    move_rings()
    move_glu()
    for copy in lines:
        copy.wait_recv()
    total = table_line[0]
    for k in range(1, pairs):
        total = total + table_line[k]
    table[mine, :] = total
    merge = table_copy(table.at[mine, :], table_back, 1, partner)
    merge.start()
    move_rings()
    move_glu()
    merge.wait_recv()
    table[pl.ds(pl.multiple_of((1 - odd) * half_rows, 8), half_rows), :] = table_back[...]
    tables_out[0] = table[0 : 2 * n_states, :].T
    tables_out[1] = table[2 * n_states : 4 * n_states, :].T
    gains_out[...] = table[4 * n_states : 4 * n_states + 8, :]
    while min(at) < SLOTS:
        move_rings()
        move_glu()
    for ring in (*rings, *glu_rings):
        ring.finish()
    for copy in (*sent, *lines, merge):
        copy.wait_send()
    for done in carry_done:
        done()


def rows_in_of(ref, tokens, width):
    return ref[...].reshape(tokens, width)


def cast_kernel(
    gin, gout, gv, gg, block, grad, tables, gains,
    gin_out, gout_out, gv_out, gg_out, block_out, grad_out, dec_out, ang_out, real_out, imag_out,
):
    gin_out[...] = gin[...].astype(f32)
    gout_out[...] = gout[...].astype(f32)
    gv_out[...] = gv[...].astype(f32)
    gg_out[...] = gg[...].astype(f32)

    @pl.when(pl.program_id(0) == 0)
    def _():
        block_out[...] = block[...]
        grad_out[...] = grad[...]
        n = dec_out.shape[1]
        dec_out[...] = tables[0, :, :n]
        ang_out[...] = tables[0, :, n:]
        real_out[...] = tables[1, :, :n]
        imag_out[...] = tables[1, :, n:]


def per_device(
    sizes, block_in, doc_lengths, out_grad, first_gain, decay_rate, turn_angle, out_real, out_imag,
    skip_gain, glu_value, glu_gate, second_gain, ffn_in, ffn_out,
):
    n_seq, n_chan = sizes
    pairs = n_seq // 2
    streams, length, width = block_in.shape
    n_states = decay_rate.shape[1]
    tokens = streams * length
    full = width * n_chan
    units = ffn_in.shape[1]
    glu_cols = glu_value.shape[1]
    group = min(32, n_states)
    like = jax.ShapeDtypeStruct
    table_rows = 4 * n_states + 16
    phases = 2 + width // LANES + 7
    ticks = 2 * n_seq - 2
    in_rows, out_rows, glu_rows = full // n_seq, units // n_seq, full // n_seq
    act = (streams, length, width)
    flat = (tokens, width)
    mask = (streams, length, LANES)
    tab = (2, n_states, width)
    V = pltpu.VMEM
    scratch = [
        V((full, glu_cols), bf16), V((full, glu_cols), bf16), V((full, units), bf16), V((units, full), bf16),
        V(mask, f32), V(mask, f32), V(mask, f32), V(mask, f32),
        V((4, n_states, width), f32), V(tab, f32), V(tab, f32), V(tab, f32), V((n_states, width), f32),
        V(flat, f32), V(act, f32), V(act, f32), V((streams, *tab), f32), V((streams, *tab), f32), V((streams, *tab), f32),
        V((tokens, full), bf16), V((tokens, glu_cols), f32), V((tokens, glu_cols), f32), V(flat, f32), V(flat, f32),
        V((tokens, full), bf16), V((tokens, full), bf16), V((tokens, units), f32), V((tokens, units), bf16), V((tokens, units), bf16),
        V((full, tokens), bf16), V((full, tokens), bf16), V((units, tokens), bf16),
        V(flat, f32), V(flat, f32), V(flat, f32), V(flat, f32), V((tokens, glu_cols), bf16), V((tokens, glu_cols), bf16), V(flat, f32),
        V(act, f32), V(flat, f32),
        V(mask, f32), V(mask, f32), V((tokens * 8, LANES), f32), V((length + 1, streams, 2, group // 8, 8, LANES), f32),
        V((4, 8, tokens), f32), V((4, n_chan - 1, 8, tokens), f32), V((3, n_chan - 1, *flat), bf16), V((3, n_chan - 1, *flat), bf16),
        V((2, streams, *tab), bf16), V((2, streams, *tab), bf16), V((2, *tab), bf16), V((2, pairs - 1, *tab), bf16),
        V((2, *tab), f32), V((2, *tab), bf16), V((2, *tab), bf16),
        V((table_rows, width), f32), V((table_rows, width), f32), V((pairs, table_rows // 2, width), f32), V((table_rows // 2, width), f32),
        V((2, in_rows, units // 2), bf16), V((2, n_seq - 1, in_rows, units // 2), bf16),
        V((2, out_rows, full // 2), bf16), V((2, n_seq - 1, out_rows, full // 2), bf16),
        V((glu_rows, glu_cols), bf16), V((n_seq - 1, glu_rows, glu_cols), bf16),
        V((glu_rows, glu_cols), bf16), V((n_seq - 1, glu_rows, glu_cols), bf16),
        pltpu.SemaphoreType.DMA((4,)),
        pltpu.SemaphoreType.DMA((phases, n_chan - 1)), pltpu.SemaphoreType.DMA((phases, n_chan - 1)),
        pltpu.SemaphoreType.DMA((3, pairs + 1)), pltpu.SemaphoreType.DMA((3, pairs + 1)),
        pltpu.SemaphoreType.DMA((6, ticks)), pltpu.SemaphoreType.DMA((6, ticks)),
    ]
    specs = [pl.BlockSpec(memory_space=pltpu.SMEM)] + [VM] * 8 + [ANY, ANY, VM, ANY, ANY]
    made = pl.pallas_call(
        functools.partial(block_kernel, sizes),
        out_shape=(
            like(act, f32), like(act, f32), like((2, width, 2 * n_states), f32), like((8, width), f32),
            like((full, units), bf16), like((units, full), bf16), like((full, glu_cols), bf16), like((full, glu_cols), bf16),
        ),
        in_specs=specs,
        out_specs=(VM,) * 8,
        scratch_shapes=scratch,
        compiler_params=pltpu.CompilerParams(
            collective_id=0, has_side_effects=True, vmem_limit_bytes=58 * 1024 * 1024
        ),
        name="block",
    )(
        doc_lengths, block_in, out_grad, first_gain[None], decay_rate, turn_angle, out_real, out_imag, skip_gain[None],
        glu_value, glu_gate, second_gain[None], ffn_in, ffn_out,
    )
    block_out, in_grad, tables, gains, gin, gout, gv, gg = made
    steps = 4

    def rows(n, m):
        return pl.BlockSpec((n // steps, m), lambda i: (i, 0))

    def whole(*shape):
        return pl.BlockSpec(shape, lambda i: (0,) * len(shape))

    small = (width, n_states)
    cast = pl.pallas_call(
        cast_kernel,
        grid=(steps,),
        out_shape=(
            like((full, units), f32), like((units, full), f32), like((full, glu_cols), f32), like((full, glu_cols), f32),
            like(act, f32), like(act, f32), like(small, f32), like(small, f32), like(small, f32), like(small, f32),
        ),
        in_specs=[
            rows(full, units), rows(units, full), rows(full, glu_cols), rows(full, glu_cols), whole(*act), whole(*act),
            whole(2, width, 2 * n_states), whole(8, width),
        ],
        out_specs=(
            rows(full, units), rows(units, full), rows(full, glu_cols), rows(full, glu_cols), whole(*act), whole(*act),
            whole(*small), whole(*small), whole(*small), whole(*small),
        ),
        compiler_params=pltpu.CompilerParams(vmem_limit_bytes=32 * 1024 * 1024),
        name="cast",
    )(gin, gout, gv, gg, block_out, in_grad, tables, gains)
    gin, gout, gv, gg, block_out, in_grad, dec, ang, real, imag = cast
    return (
        block_out, in_grad, gains[0], dec, ang, real, imag, gains[1], gv, gg, gains[2], gin, gout,
    )


def solution(mesh):
    act = P(None, "seq", "chan")
    vec, mat = P("chan"), P("chan", None)
    col = P(None, "chan")
    sizes = (mesh.shape["seq"], mesh.shape["chan"])
    return jax.shard_map(
        functools.partial(per_device, sizes),
        mesh=mesh,
        in_specs=(act, P(), act, vec, mat, mat, mat, mat, vec, col, col, vec, col, mat),
        out_specs=(act, act, vec, mat, mat, mat, mat, vec, col, col, vec, col, mat),
        check_vma=False,
    )
```

time: 557 us -> 213 us (0.38)
  waiting for transfers between devices: 346 us -> 0 us
  Pallas kernels: 41.1 us -> 192 us
  blocking collectives: 69.8 us -> 0 us
  other arithmetic: 43.4 us -> 0 us
  matrix products: 22.6 us -> 0 us
  between operations: 14.6 us -> 0.68 us
    psum x2 -> x0, waiting for transfers between devices: 192 us -> none  [the longest x1 114 us: per_device(): lax.psum((ffn_in_grad.astype(jnp.bfloat16), ffn_out_grad.astype(jnp.bfloa...]
    pallas_call x4 -> x2, Pallas kernels: 41.1 us -> 192 us  [the longest x1 188 us: per_device(): pl.pallas_call(functools.partial(block_kernel, sizes), out_shape=(like(ac...]
    all_gather x2 -> x0, waiting for transfers between devices: 79.8 us -> none  [carry_over(): gathered = lax.all_gather(parts, 'seq')]
    reduce_scatter x3 -> x0, waiting for transfers between devices: 74.3 us -> none  [the longest x1 31.9 us: per_device(): lax.psum_scatter(part_grad, 'chan', scatter_dimension=1, tiled=True)]
    psum x5 -> x0, blocking collectives: 48.7 us -> none  [the longest x4 28.2 us: token_sums(): return lax.psum(sums, 'chan')]
    dot_general x12 -> x0, matrix products: 22.6 us -> none  [the longest x1 3.74 us: per_device(): part_out = jnp.dot(hidden, ffn_out, preferred_element_type=jnp.float32)]
    all_gather x3 -> x0, blocking collectives: 21.1 us -> none  [the longest x1 7.16 us: per_device(): lax.all_gather(act.reshape(tokens, width), 'chan', axis=1, tiled=True)]
    convert_element_type x9 -> x0, other arithmetic: 11.3 us -> none  [the longest x1 4.22 us: per_device(): ffn_in_grad.astype(jnp.float32)]
  transfers between devices with their start and end apart: 7 -> 0, of which waited for: 7 -> 0; matrix products, arithmetic and copies ran while one was open for 9% -> 0% of each run, Pallas kernels for 4% -> 0%
where the time goes in v2:
time: 213 us; the launch traced here: 212 us
  Pallas kernels  192 us (90%)
  local copies, waits for them, and re-layouts  19.4 us (9%)
    pallas_call x1, Pallas kernels, per_device(): pl.pallas_call(functools.partial(block_kernel, sizes), out_shape=(like(ac...  188 us
    unnamed x24, local copies, waits for them, and re-layouts  18 us
    pallas_call x1, Pallas kernels, per_device(): pl.pallas_call(cast_kernel, grid=(steps,), out_shape=(like((full, units),...  4.38 us

profile of v2, /device:TPU:0, one launch (start us, length us, event | category | flops | bytes accessed | tf_op | source)
XLA Modules:
  0.0 212.3 jit_solution(11313454310565462886)
XLA Ops:
  0.6 1.6 copy.27.dec_ref
  2.2 1.6 copy.28.ang_ref
  3.8 1.6 copy.29.real_ref
  5.4 1.6 copy.30.imag_ref
  7.0 187.9 %block.1 = (f32[2,128,256]{2,1,0:T(8,128)}, f32[2,128,256]{2,1,0:T(8,128)}, f32[2,256,128]{2,1,0:T(8,128)}, f32[8,256]{1,0:T(8,128)}, bf16[1024,1024]{1,0:T(8,12...) custom-call(s32[2,16]{1,0:T(2,128)} %docs.1, f32[2,128,256]{2,1,0:T(8,128)} %x_ref.1, ...), custom_call_target="tpu_custom_call" | custom-call | tf_op jit(solution)/shard_map/block/pallas_call | solution.py:804
  194.9 0.0 copy-start
  194.9 1.6 copy-done
  196.5 0.0 copy-start.1
  196.5 1.6 copy-done.1
  198.1 0.0 copy-start.2
  198.1 1.0 copy-done.2
  199.1 0.0 copy-start.3
  199.1 1.0 copy-done.3
  200.2 0.0 copy-start.4
  200.2 0.9 copy-done.4
  201.1 0.0 copy-start.5
  201.1 0.9 copy-done.5
  202.1 0.0 copy-start.6
  202.1 0.9 copy-done.6
  203.0 0.0 copy-start.7
  203.0 0.7 copy-done.7
  203.7 4.4 %cast.1 = (f32[1024,1024]{1,0:T(8,128)}, f32[1024,1024]{1,0:T(8,128)}, f32[1024,256]{1,0:T(8,128)}, f32[1024,256]{1,0:T(8,128)}, f32[2,128,256]{2,1,0:T(8,128)},...) custom-call(bf16[1024,1024]{1,0:T(8,128)(2,1)S(1)} %copy-done, ...), custom_call_target="tpu_custom_call" | custom-call | tf_op jit(solution)/shard_map/cast/pallas_call | solution.py:831
  208.1 0.7 copy.31
  208.8 0.7 copy.32
  209.5 0.7 copy.33
  210.2 0.7 copy.34
  210.9 1.4 fusion
Async XLA Ops:
  194.9 1.6 copy-start
  196.5 1.6 copy-start.1
  198.1 1.0 copy-start.2
  199.1 1.0 copy-start.3
  200.2 0.9 copy-start.4
  201.1 0.9 copy-start.5
  202.1 0.9 copy-start.6
  203.0 0.7 copy-start.7

commit v3 on v2

v3 whole, which is shorter than its diff:
```python
import functools

import jax
import jax.numpy as jnp
from jax import lax
from jax.experimental import pallas as pl
from jax.experimental.pallas import tpu as pltpu
from jax.sharding import PartitionSpec as P

epsilon = 1e-05
LANES = 128
MESH = pl.DeviceIdType.MESH
VM = pl.BlockSpec(memory_space=pltpu.VMEM)
ANY = pl.BlockSpec(memory_space=pl.ANY)
GELU_A = 0.7978845608028654
GELU_B = 0.044715
NN = (((1,), (0,)), ((), ()))
NT = (((1,), (1,)), ((), ()))
f32, bf16 = jnp.float32, jnp.bfloat16


def gelu_parts(x):
    inner = GELU_A * (x + GELU_B * (x * x * x))
    t = jnp.tanh(inner)
    half = 0.5 * (1.0 + t)
    slope = half + 0.5 * x * (1.0 - t * t) * (GELU_A * (1.0 + 3.0 * GELU_B * (x * x)))
    return x * half, slope


def dot(a, b, dims=NN):
    return lax.dot_general(a, b, dims, preferred_element_type=f32)


def cmul(ar, ai, br, bi):
    return ar * br - ai * bi, ar * bi + ai * br


def power(re, im, count):
    out = None
    while count:
        if count & 1:
            out = (re, im) if out is None else cmul(*out, re, im)
        re, im = cmul(re, im, re, im)
        count >>= 1
    return out


def row(ref, b, p):
    return jnp.broadcast_to(ref[b, pl.ds(p, 1), :], (8, LANES))


def tile(ref, lead, rows, cols):
    return ref[(*lead, rows, cols)].reshape(-1, 8, LANES)


class Line:
    def __init__(self, own, count, at, send, inward, across, sems, where, hand_over, stores=None):
        self.own, self.count, self.at = own, count, at
        self.send, self.inward, self.across = send, inward, across
        self.sent, self.got = sems
        self.pairs, self.is_end, self.is_mid, self.toward, self.away, self.partner = where
        self.hand_over, self.stores = hand_over, stores

    def copy(self, src, dst, i, sent, got, to):
        return pltpu.make_async_remote_copy(
            src_ref=src, dst_ref=dst, send_sem=self.sent.at[sent, i], recv_sem=self.got.at[got, i],
            device_id=to, device_id_type=MESH,
        )

    def pass_in(self, i):
        self.copy(self.send.at[i], self.inward.at[i], i, 0, 0, self.toward).start()

    def pass_across(self, i):
        self.copy(self.send.at[i], self.across.at[i], i, 0, 1, self.toward).start()

    def pass_out(self, i):
        self.copy(self.at(i), self.at(i), i, 1, 2, self.away).start()

    def pass_pair(self, i):
        self.copy(self.at(i), self.at(i), i, 2, 3, self.partner).start()

    def arrived(self, i, kind):
        self.copy(self.send.at[i], self.send.at[i], i, 0, kind, self.toward).wait_recv()

    def begin(self, i):
        if self.pairs > 2:

            @pl.when(self.is_end)
            def _():
                self.send[i] = self.own(i).astype(self.send.dtype)
                self.pass_in(i)

    def join(self, i):
        if self.pairs == 2:
            self.send[i] = self.own(i).astype(self.send.dtype)
            self.pass_across(i)
            return

        @pl.when(jnp.logical_not(self.is_end))
        def _():
            total = self.own(i)
            self.arrived(i, 0)
            self.send[i] = (total + self.inward[i].astype(f32)).astype(self.send.dtype)
            if self.pairs == 4:
                self.pass_across(i)
                return

            @pl.when(self.is_mid)
            def _():
                self.pass_across(i)

            @pl.when(jnp.logical_not(self.is_mid))
            def _():
                self.pass_in(i)

    def settle(self, i):
        @pl.when(self.is_mid)
        def _():
            self.arrived(i, 1)
            total = self.send[i].astype(f32) + self.across[i].astype(f32)
            self.at(i)[...] = total.astype(self.send.dtype)
            if self.pairs > 2:
                self.pass_out(i)
            if self.hand_over:
                self.pass_pair(i)

    def relay(self, i):
        if self.pairs > 2:

            @pl.when(jnp.logical_not(self.is_mid))
            def _():
                self.arrived(i, 2)
                if self.pairs > 4:

                    @pl.when(jnp.logical_not(self.is_end))
                    def _():
                        self.pass_out(i)

                if self.hand_over:
                    self.pass_pair(i)

    def saves(self, i):
        return [pltpu.make_async_copy(src, dst, sem) for src, dst, sem in self.stores(i)]

    def store(self, i):
        self.arrived(i, 3)
        for save in self.saves(i):
            save.start()

    def finish(self):
        for i in range(self.count):
            if self.stores:
                for save in self.saves(i):
                    save.wait()
            self.copy(self.send.at[i], self.send.at[i], i, 0, 0, self.toward).wait_send()
            if self.pairs > 2:

                @pl.when(jnp.logical_not(self.is_end))
                def _(i=i):
                    self.copy(self.send.at[i], self.send.at[i], i, 1, 2, self.toward).wait_send()

            if self.hand_over:
                done = self.copy(self.send.at[i], self.send.at[i], i, 2, 3, self.toward)
                done.wait_send()


def block_kernel(
    sizes,
    docs, x_ref, og_ref, gain1, dec_ref, ang_ref, real_ref, imag_ref, skip_ref, gluv_hbm, glug_hbm, gain2, win_hbm, wout_hbm,
    block_out, in_grad, tables_out, gains_out, gin_hbm, gout_hbm, gv_hbm, gg_hbm,
    gin_out, gout_out, gv_out, gg_out, gluv, glug, win, wout,
    keep, first_mask, last_mask, valid,
    lam, coef, step_l, factor,
    gain_full, normed1, u_ref, y_ref, edge_sum, init, adj,
    act_full, val, gate, resid, normed2, grad_full, mid_full, hidden_grad, hidden, pre,
    act_t, mid_t, hidden_t, part_own, mid_grad, result_own, resid_grad, value_grad, gate_grad, act_own, mixer_grad, du,
    row_a, row_b, part, states,
    stat_send, stat_recv, rs_send, rs_recv,
    pair_send, pair_recv, line_send, line_recv, back_send, back_low, back_recv,
    table, table2, table_sum, table_send, table_in, table_across,
    gain_sums, gain_sums2, gains_sum, gains_send, gains_in, gains_across,
    grad2, act2, mid2, act_t2, mid_t2, hidden_t2, pre2, value2, gate2,
    in_send, in_in, in_across, out_send, out_in, out_across, gv_send, gv_in, gv_across, gg_send, gg_in, gg_across,
    load_sem, save_sem, chan_send, chan_recv, seq_send, seq_recv, fac_send, fac_recv, line_sent, line_got,
):
    n_seq, n_chan = sizes
    pairs = n_seq // 2
    streams, length, width = x_ref.shape
    n_states = lam.shape[1]
    tokens = streams * length
    full = width * n_chan
    units = win.shape[1]
    group = states.shape[3] * 8
    s, c = lax.axis_index("seq"), lax.axis_index("chan")
    odd = lax.rem(s, 2)
    level = lax.div(s, 2)
    partner = (s + 1 - 2 * odd, c)
    every = pl.ds(0, n_states)

    def chan_peer(j):
        return lax.rem(c + j, n_chan)

    def chan_block(k, size):
        return pl.ds(pl.multiple_of(k * size, size), size)

    own_cols = chan_block(c, width)

    barrier = pltpu.get_barrier_semaphore()
    for j in range(1, n_chan):
        pl.semaphore_signal(barrier, inc=1, device_id=(s, chan_peer(j)), device_id_type=MESH)
    pl.semaphore_signal(barrier, inc=1, device_id=partner, device_id_type=MESH)
    for d in range(1, pairs):
        other = 2 * lax.rem(level + d, pairs) + odd
        pl.semaphore_signal(barrier, inc=1, device_id=(other, c), device_id_type=MESH)

    loads = [
        pltpu.make_async_copy(src, dst, load_sem.at[i])
        for i, (src, dst) in enumerate(
            ((wout_hbm, wout), (gluv_hbm, gluv), (glug_hbm, glug), (win_hbm, win))
        )
    ]
    for load in loads:
        load.start()

    sent = []

    def chan_copy(src, dst, phase, j):
        return pltpu.make_async_remote_copy(
            src_ref=src, dst_ref=dst, send_sem=chan_send.at[phase, j - 1], recv_sem=chan_recv.at[phase, j - 1],
            device_id=(s, chan_peer(j)), device_id_type=MESH,
        )

    def chan_all(pick, phase):
        copies = []
        for j in range(1, n_chan):
            copy = chan_copy(*pick(j), phase, j)
            copy.start()
            copies.append(copy)
        sent.extend(copies)
        return copies

    def landed(copies):
        for copy in copies:
            copy.wait_recv()

    lane = lax.broadcasted_iota(jnp.int32, (tokens, LANES), 1)

    def stats_start(first, second, k, phase):
        packed = jnp.where(lane == 0, first, jnp.where(lane == 1, second, 0.0))
        stat_send[k] = packed.T[:8]
        return chan_all(lambda j: (stat_send.at[k], stat_recv.at[k, j - 1]), phase)

    def stats_end(copies, k):
        landed(copies)
        total = stat_send[k]
        for j in range(1, n_chan):
            total = total + stat_recv[k, j - 1]
        total = jnp.concatenate([total, jnp.zeros((LANES - 8, tokens), f32)], axis=0).T
        return total[:, 0:1] / full, total[:, 1:2] / full

    rows_in = x_ref[...].reshape(tokens, width)
    grad_full[:, own_cols] = og_ref[...].reshape(tokens, width).astype(bf16)
    sum1 = jnp.sum(rows_in, axis=1, keepdims=True)
    square1 = jnp.sum(rows_in * rows_in, axis=1, keepdims=True)
    pl.semaphore_wait(barrier, n_chan + pairs - 1)
    stat_copies = stats_start(sum1, square1, 0, 0)
    grad_copies = chan_all(lambda j: (grad_full.at[:, own_cols], grad_full.at[:, own_cols]), 1)
    gain_full[:, own_cols] = jnp.broadcast_to(gain2[...], (8, width))
    gain_copies = chan_all(lambda j: (gain_full.at[:, own_cols], gain_full.at[:, own_cols]), 11)

    start = s * length
    ends = []
    for b in range(streams):
        total, stream = 0, []
        for k in range(docs.shape[1]):
            total = total + docs[b, k]
            stream.append(total)
        ends.append(stream)

    def passed(b, at):
        count = jnp.int32(0)
        for end in ends[b]:
            count = count + jnp.where(end <= at, 1, 0)
        return count

    def kept(block, b):
        return jnp.where(
            passed(b, block * length - 1) == passed(b, block * length + length - 1), 1.0, 0.0
        )

    pair_flags = [[kept(2 * level + x, b) for b in range(2)] for x in range(2)]

    def line_flag(source):
        both = [kept(2 * source, b) * kept(2 * source + 1, b) for b in range(2)]
        return jnp.where(odd == 1, both[1], both[0])

    line_flags = [[line_flag(level + (d if back else -d)) for d in range(1, pairs)] for back in (False, True)]
    position = lax.broadcasted_iota(jnp.int32, (length, LANES), 0) + start
    for b in range(streams):
        here = jnp.zeros((length, LANES), jnp.int32)
        prior = jnp.zeros((length, LANES), jnp.int32)
        for end in ends[b]:
            here = here + jnp.where(position >= end, 1, 0)
            prior = prior + jnp.where(position > end, 1, 0)
        keep[b] = jnp.where(here == prior, 1.0, 0.0)
        first_mask[b] = jnp.where(here == passed(b, start - 1), 1.0, 0.0)
        last_mask[b] = jnp.where(here == passed(b, start + length - 1), 1.0, 0.0)
        valid[b] = jnp.where(position < ends[b][-1], 1.0, 0.0)

    decay, angle = dec_ref[...], ang_ref[...]
    magnitude = jnp.exp(-decay)
    a2 = angle * angle
    sine, cosine = jnp.ones_like(a2), jnp.ones_like(a2)
    for k in (13, 11, 9, 7, 5, 3):
        sine = 1.0 - sine * a2 * (1.0 / (k * (k - 1)))
    for k in (14, 12, 10, 8, 6, 4, 2):
        cosine = 1.0 - cosine * a2 * (1.0 / (k * (k - 1)))
    lam[0] = magnitude * cosine
    lam[1] = magnitude * (sine * angle)
    twice = 2.0 * decay
    series = jnp.ones_like(twice)
    for k in (9, 8, 7, 6, 5, 4, 3, 2):
        series = 1.0 - series * twice * (1.0 / k)
    factor[...] = jnp.sqrt(twice * series)
    coef[0] = real_ref[...] * factor[...]
    coef[1] = imag_ref[...] * factor[...]
    step_l[0], step_l[1] = power(lam[0], lam[1], length)

    average, square = stats_end(stat_copies, 0)
    scaler1 = lax.rsqrt(square - average * average + epsilon)
    normed1[...] = (rows_in - average) * scaler1
    for b in range(streams):
        rows = slice(b * length, (b + 1) * length)
        for k in range(width // LANES):
            cols = slice(k * LANES, (k + 1) * LANES)
            u_ref[b, :, cols] = normed1[rows, cols] * gain1[:, cols] * valid[b]

    def edges(values, mask, reverse, k):
            cols = pl.ds(k * LANES, LANES)
            row_a[...] = values[:, :, cols] * mask[...]
            for h in range(n_states // group):
                rows = pl.ds(h * group, group)
                l1r, l1i = tile(lam, (0,), rows, cols), tile(lam, (1,), rows, cols)
                l1i = -l1i if reverse else l1i
                l2r, l2i = cmul(l1r, l1i, l1r, l1i)
                l3r, l3i = cmul(l2r, l2i, l1r, l1i)
                l4r, l4i = cmul(l2r, l2i, l2r, l2i)

                def move(i, carry):
                    new = []
                    for b in range(streams):
                        sr, si = carry[2 * b], carry[2 * b + 1]
                        base = length - 4 - 4 * i if reverse else 4 * i
                        u = [row(row_a, b, base + (3 - j if reverse else j)) for j in range(4)]
                        nr = (l4r * sr - l4i * si) + (l3r * u[0] + l2r * u[1]) + (l1r * u[2] + u[3])
                        ni = (l4r * si + l4i * sr) + (l3i * u[0] + l2i * u[1]) + l1i * u[2]
                        new += [nr, ni]
                    return tuple(new)

                zero = jnp.zeros((group // 8, 8, LANES), f32)
                final = lax.fori_loop(0, length // 4, move, (zero,) * (2 * streams))
                cr, ci = tile(coef, (0,), rows, cols), tile(coef, (1,), rows, cols)
                for b in range(streams):
                    fr, fi = final[2 * b], final[2 * b + 1]
                    if reverse:
                        fr, fi = cmul(cr, -ci, fr, fi)
                    edge_sum[k, b, 0, rows] = fr.reshape(-1, LANES)
                    edge_sum[k, b, 1, rows] = fi.reshape(-1, LANES)

    class Carry:
        def __init__(self, target, which, reverse, k):
            self.target, self.which, self.reverse, self.k = target, which, reverse, k
            cols = pl.ds(k * LANES, LANES)
            self.sr = step_l[0, :, cols]
            self.si = -step_l[1, :, cols] if reverse else step_l[1, :, cols]
            self.leads = odd == (1 if reverse else 0)

        def copy(self, src, dst, i, to):
            return pltpu.make_async_remote_copy(
                src_ref=src.at[self.which, self.k], dst_ref=dst, send_sem=seq_send.at[self.which, self.k, i],
                recv_sem=seq_recv.at[self.which, self.k, i], device_id=to, device_id_type=MESH,
            )

        def advance(self, flag, vr, vi, ur, ui):
            r, i = cmul(ur, ui, vr, vi)
            return r * flag, i * flag

        def start(self):
            at = (self.which, self.k)
            pair_send[at] = edge_sum[self.k].astype(bf16)
            self.across = self.copy(pair_send, pair_recv.at[at], 0, partner)
            self.across.start()

        def line(self):
            at = (self.which, self.k)
            self.across.wait_recv()
            mine_r, mine_i = edge_sum[self.k, odd, 0], edge_sum[self.k, odd, 1]
            other_r, other_i = pair_recv[(*at, odd, 0)].astype(f32), pair_recv[(*at, odd, 1)].astype(f32)
            flag = jnp.where(odd == 1, *[pair_flags[0 if self.reverse else 1][b] for b in (1, 0)])
            lr, li = jnp.where(self.leads, mine_r, other_r), jnp.where(self.leads, mine_i, other_i)
            tr, ti = jnp.where(self.leads, other_r, mine_r), jnp.where(self.leads, other_i, mine_i)
            ar, ai = self.advance(flag, lr, li, self.sr, self.si)
            line_send[(*at, 0)] = (ar + tr).astype(bf16)
            line_send[(*at, 1)] = (ai + ti).astype(bf16)
            for d in range(1, pairs):
                to = level - d if self.reverse else level + d

                @pl.when(to >= 0 if self.reverse else to < pairs)
                def _(d=d, to=to):
                    self.onward(d, (2 * to + odd, c)).start()

        def onward(self, d, to=partner):
            return self.copy(line_send, line_recv.at[self.which, self.k, d - 1], 1 + d, to)

        def home(self):
            at = (self.which, self.k)
            dr, di = cmul(self.sr, self.si, self.sr, self.si)
            back_send[...] = jnp.zeros(back_send.shape, f32)
            for d in range(pairs - 1, 0, -1):
                source = level + d if self.reverse else level - d

                @pl.when(source < pairs if self.reverse else source >= 0)
                def _(d=d):
                    self.onward(d).wait_recv()
                    flag = line_flags[self.reverse][d - 1]
                    vr, vi = self.advance(flag, back_send[0], back_send[1], dr, di)
                    back_send[0] = vr + line_recv[(*at, d - 1, 0)].astype(f32)
                    back_send[1] = vi + line_recv[(*at, d - 1, 1)].astype(f32)

            back_low[at] = back_send[...].astype(bf16)
            self.back = self.copy(back_low, back_recv.at[at], 1, partner)
            self.back.start()

        def end(self):
            at = (self.which, self.k)
            cols = pl.ds(self.k * LANES, LANES)
            self.back.wait_recv()
            for b in range(streams):
                flag = pair_flags[1 if self.reverse else 0][b]
                near = [
                    jnp.where(odd == b, back_low[(*at, i)], back_recv[(*at, i)]).astype(f32) for i in range(2)
                ]
                far = self.advance(flag, *near, self.sr, self.si)
                for i in range(2):
                    other = far[i] + pair_recv[(*at, b, i)].astype(f32)
                    self.target[b, i, :, cols] = jnp.where(self.leads, near[i], other)

        def finish(self):
            self.across.wait_send()
            self.back.wait_send()

            for d in range(1, pairs):
                to = level - d if self.reverse else level + d

                @pl.when(to >= 0 if self.reverse else to < pairs)
                def _(d=d):
                    self.onward(d).wait_send()

    low_side = level < pairs // 2
    toward = (s + jnp.where(low_side, 2, -2), c)
    away = (s + jnp.where(low_side, -2, 2), c)
    where = (
        pairs,
        jnp.logical_or(level == 0, level == pairs - 1),
        jnp.logical_or(level == pairs // 2 - 1, level == pairs // 2),
        toward, away, partner,
    )
    factors = []

    def swap_factor(src, dst, k, to=partner):
        copy = pltpu.make_async_remote_copy(
            src_ref=src, dst_ref=dst, send_sem=fac_send.at[k], recv_sem=fac_recv.at[k], device_id=to, device_id_type=MESH
        )
        copy.start()
        factors.append(copy)
        return copy

    half_units = units // 2
    my_half = chan_block(odd, half_units)
    their_half = chan_block(1 - odd, half_units)
    wanted = {}

    def need(*names):
        for name in names:
            wanted[name].wait_recv()

    in_rows, in_cols = full // 2, half_units // 4
    out_cols = full // 8
    glu_rows, glu_half = full // 4, width // 2
    my_glu, their_glu = chan_block(odd, glu_half), chan_block(1 - odd, glu_half)

    def in_own(i):
        if i == 0:
            need("pre")
        rows, cols = pl.ds((i % 2) * in_rows, in_rows), (i // 2) * in_cols
        mine = pl.ds(pl.multiple_of(odd * half_units + cols, in_cols), in_cols)
        return dot(mid_t[rows, :], pre[:, mine]) + dot(mid_t2[rows, :], pre2[:, pl.ds(cols, in_cols)])

    def in_at(i):
        return gin_out.at[odd, i // 2, i % 2]

    def out_own(i):
        if i == 0:
            need("grad", "hidden")
        cols = pl.ds(i * out_cols, out_cols)
        return dot(hidden_t[my_half, :], grad_full[:, cols]) + dot(hidden_t2[...], grad2[:, cols])

    def out_at(i):
        return gout_out.at[odd, i]

    def glu_own(near, far, names):
        def own(i):
            if i == 0:
                need(*names)
            rows = pl.ds(i * glu_rows, glu_rows)
            return dot(act_t[rows, :], near[:, my_glu]) + dot(act_t2[rows, :], far[...])

        return own

    def glu_at(out):
        def at(i):
            return out.at[odd, i]

        return at

    def table_own(q):
        need(("table", q))
        return table[q] + table2[q]

    def gains_own(i):
        need("gains")
        return gain_sums[...] + gain_sums2[...]

    sem_at = [0]

    def line(own, count, at, bufs, hand_over, kept_at=None):
        spot, base = pl.ds(sem_at[0], count), sem_at[0]
        stores = None
        if kept_at:
            held, final, place = kept_at

            def stores(i):
                return [(held.at[(x, *place(i))], final.at[(x, *place(i))], save_sem.at[x, base + i]) for x in range(2)]

        sem_at[0] += count
        return Line(own, count, at, *bufs, (line_sent.at[:, spot], line_got.at[:, spot]), where, hand_over, stores)

    quarters = (width // LANES) * (n_states // group)
    in_line = line(in_own, 8, in_at, (in_send, in_in, in_across), True, (gin_out, gin_hbm, lambda i: (i // 2, i % 2)))
    out_line = line(out_own, 8, out_at, (out_send, out_in, out_across), True, (gout_out, gout_hbm, lambda i: (i,)))
    gv_line = line(glu_own(value_grad, value2, ("value",)), 4, glu_at(gv_out), (gv_send, gv_in, gv_across), True, (gv_out, gv_hbm, lambda i: (i,)))
    gg_line = line(glu_own(gate_grad, gate2, ("gate",)), 4, glu_at(gg_out), (gg_send, gg_in, gg_across), True, (gg_out, gg_hbm, lambda i: (i,)))
    table_line = line(table_own, quarters, lambda q: table_sum.at[q], (table_send, table_in, table_across), False)
    gains_line = line(gains_own, 1, lambda i: gains_sum.at[i], (gains_send, gains_in, gains_across), False)
    lines = [out_line, gv_line, in_line, gg_line, table_line, gains_line]
    pieces = [(entry, i) for entry in lines[:4] for i in range(entry.count)]
    tick, begun = [0], [0]
    MID, LAST, STORE = 2, 4, 8

    def launch(count):
        for _ in range(count):
            if begun[0] < len(pieces):
                entry, i = pieces[begun[0]]
                entry.begin(i)
            begun[0] += 1

    def pump(count, lead=3):
        for _ in range(count):
            t = tick[0]
            tick[0] += 1
            launch(t + 1 + lead - begun[0])
            for ahead, act in ((0, "join"), (-MID, "settle"), (-LAST, "relay"), (-STORE, "store")):
                if 0 <= t + ahead < len(pieces):
                    entry, i = pieces[t + ahead]
                    getattr(entry, act)(i)

    tiles = width // LANES
    forward = [Carry(init, 0, False, k) for k in range(tiles)]
    for k in range(tiles):
        edges(u_ref, last_mask, False, k)
        forward[k].start()
    unit_block = min(units, 256)

    def hidden_grad_part(i):
        cols = pl.ds(i * unit_block, unit_block)
        hidden_grad[:, cols] = dot(grad_full[...], wout[cols, :], NT)

    loads[0].wait()
    landed(grad_copies)
    blocks = units // unit_block
    for k in range(blocks // 2):
        hidden_grad_part(k)
    for k in range(tiles):
        forward[k].line()
    for k in range(blocks // 2, blocks):
        hidden_grad_part(k)
    for k in range(tiles):
        forward[k].home()
    wanted["grad"] = swap_factor(grad_full, grad2, 0)
    act_copies = []
    for k in range(tiles):
        forward[k].end()
        cols = pl.ds(k * LANES, LANES)
        lr, li = tile(lam, (0,), every, cols), tile(lam, (1,), every, cols)
        cr, ci = tile(coef, (0,), every, cols), tile(coef, (1,), every, cols)
        row_a[...] = u_ref[:, :, cols]
        for b in range(streams):

            def move(p, carry, b=b, lr=lr, li=li, cr=cr, ci=ci):
                sr, si = carry
                u = row(row_a, b, p)
                m = row(keep, b, p)
                sr = sr * m
                si = si * m
                nr = (lr * sr - li * si) + u
                ni = lr * si + li * sr
                part[pl.ds(pl.multiple_of(p * 8, 8), 8), :] = (cr * nr - ci * ni).sum(0)
                return nr, ni

            begin = (tile(init, (b, 0), every, cols), tile(init, (b, 1), every, cols))
            lax.fori_loop(0, length, move, begin, unroll=2)
            total = part[pl.ds(0, length, stride=8), :]
            for j in range(1, 8):
                total = total + part[pl.ds(j, length, stride=8), :]
            y = total + skip_ref[:, cols] * u_ref[b, :, cols]
            y_ref[b, :, cols] = y
            to = pl.ds(pl.multiple_of(c * width + k * LANES, LANES), LANES)
            act_full[b * length : (b + 1) * length, to] = gelu_parts(y)[0].astype(bf16)
        act_copies.append(chan_all(lambda j: (act_full.at[:, to], act_full.at[:, to]), 2 + k))
    base = 2 + width // LANES

    loads[1].wait()
    loads[2].wait()
    for copies in act_copies:
        landed(copies)
    beside = (s, c + 1 - 2 * lax.rem(c, 2))
    core_half = chan_block(lax.rem(c, 2), tokens // 2)
    wanted["act_near"] = swap_factor(act_full.at[core_half, :], act2.at[core_half, :], 1)
    val[...] = dot(act_full[...], gluv[...])
    gate[...] = jax.nn.sigmoid(dot(act_full[...], glug[...]))
    resid[...] = rows_in_of(x_ref, tokens, width) + val[...] * gate[...]

    sum2 = jnp.sum(resid[...], axis=1, keepdims=True)
    square2 = jnp.sum(resid[...] * resid[...], axis=1, keepdims=True)
    stat_copies = stats_start(sum2, square2, 1, base)
    average, square = stats_end(stat_copies, 1)
    scaler2 = lax.rsqrt(square - average * average + epsilon)
    normed2[...] = (resid[...] - average) * scaler2
    mid_full[:, own_cols] = (normed2[...] * gain2[...]).astype(bf16)
    mid_copies = chan_all(lambda j: (mid_full.at[:, own_cols], mid_full.at[:, own_cols]), base + 1)
    loads[3].wait()
    landed(mid_copies)

    for k in range(units // unit_block):
        cols = pl.ds(k * unit_block, unit_block)
        value, slope = gelu_parts(dot(mid_full[...], win[:, cols]))
        hidden[:, cols] = value.astype(bf16)
        pre[:, cols] = (hidden_grad[:, cols] * slope).astype(bf16)
        hidden_t[cols, :] = hidden[:, cols].T
    def scatter_fill(piece, own, k):
        for j in range(1, n_chan):
            rs_send[k, j - 1] = piece(chan_block(chan_peer(j), width)).astype(bf16)
        own[...] = piece(own_cols)

    def scatter_start(k, phase):
        return chan_all(lambda j: (rs_send.at[k, j - 1], rs_recv.at[k, j - 1]), phase)

    def transposed(source, target, count):
        for k in range(count):
            target[pl.ds(k * width, width), :] = source[:, k * width : (k + 1) * width].T

    def scatter_end(copies, own, k):
        landed(copies)
        total = own[...]
        for j in range(1, n_chan):
            total = total + rs_recv[k, j - 1].astype(f32)
        return total

    scatter_fill(lambda rows: dot(pre[...], win[rows, :], NT), part_own, 0)
    grad_parts = scatter_start(0, base + 2)
    wanted["hidden"] = swap_factor(hidden_t.at[their_half, :], hidden_t2, 4)
    landed(gain_copies)
    first, second = 0.0, 0.0
    for j in range(n_chan):
        cols = chan_block(chan_peer(j), width) if j else own_cols
        values = rs_send[0, j - 1].astype(f32) if j else part_own[...]
        first = first + jnp.sum(values * gain_full[0:1, cols], axis=1, keepdims=True)
        second = second + jnp.sum(values * mid_full[:, cols].astype(f32), axis=1, keepdims=True)
    stat_copies = stats_start(first, second, 2, base + 4)
    scatter_fill(lambda cols: dot(hidden[...], wout[:, cols]), result_own, 1)
    transposed(act_full, act_t, n_chan)
    transposed(mid_full, mid_t, n_chan)
    wanted["act_near"].wait_recv()
    wanted["act_far"] = swap_factor(act2.at[core_half, :], act2.at[core_half, :], 9, beside)
    launch(2)
    mid_grad[...] = scatter_end(grad_parts, part_own, 0)
    wanted["pre"] = swap_factor(pre.at[:, their_half], pre2, 5)
    gains = jnp.sum(mid_grad[...] * normed2[...], axis=0, keepdims=True)
    first, second = stats_end(stat_copies, 2)
    resid_grad[...] = og_ref[...].reshape(tokens, width) + scaler2 * (
        mid_grad[...] * gain2[...] - first - normed2[...] * second
    )

    value_grad[...] = (resid_grad[...] * gate[...]).astype(bf16)
    gate_grad[...] = (resid_grad[...] * val[...] * gate[...] * (1.0 - gate[...])).astype(bf16)
    scatter_fill(
        lambda rows: dot(value_grad[...], gluv[rows, :], NT) + dot(gate_grad[...], glug[rows, :], NT), act_own, 2
    )
    act_parts = scatter_start(2, base + 5)
    wanted["value"] = swap_factor(value_grad.at[:, their_glu], value2, 6)
    wanted["gate"] = swap_factor(gate_grad.at[:, their_glu], gate2, 7)
    pump(1, 2)
    act_grad = scatter_end(act_parts, act_own, 2)
    mixer_grad[...] = act_grad.reshape(streams, length, width) * gelu_parts(y_ref[...])[1]

    out_parts = scatter_start(1, base + 3)

    backward = [Carry(adj, 1, True, k) for k in range(tiles)]
    for k in range(tiles):
        edges(mixer_grad, first_mask, True, k)
        backward[k].start()
        if k == 0:
            pump(1, 2)
    pump(1, 2)
    for k in range(tiles):
        backward[k].line()
    wanted["mid_near"] = swap_factor(mid_full.at[core_half, :], mid2.at[core_half, :], 2)
    pump(2, 2)
    total = scatter_end(out_parts, result_own, 1)
    block_out[...] = (resid[...] + total).reshape(streams, length, width)
    for k in range(tiles):
        backward[k].home()
    need("act_far")
    transposed(act2, act_t2, n_chan)
    pump(2, 2)
    zero = jnp.zeros((group // 8, 8, LANES), f32)
    q = 0
    for k in range(width // LANES):
        backward[k].end()
        cols = pl.ds(k * LANES, LANES)
        row_a[...] = u_ref[:, :, cols]
        row_b[...] = mixer_grad[:, :, cols]
        for h in range(n_states // group):
            rows = pl.ds(h * group, group)
            lr, li = tile(lam, (0,), rows, cols), tile(lam, (1,), rows, cols)
            cr, ci = tile(coef, (0,), rows, cols), tile(coef, (1,), rows, cols)

            def again(p, carry, lr=lr, li=li):
                new = []
                for b in range(streams):
                    sr, si = carry[2 * b], carry[2 * b + 1]
                    u = row(row_a, b, p)
                    m = row(keep, b, p)
                    sr = sr * m
                    si = si * m
                    nr = (lr * sr - li * si) + u
                    ni = lr * si + li * sr
                    states[p + 1, b, 0] = nr
                    states[p + 1, b, 1] = ni
                    new += [nr, ni]
                return tuple(new)

            begin = []
            for b in range(streams):
                begin += [tile(init, (b, 0), rows, cols), tile(init, (b, 1), rows, cols)]
                states[0, b, 0] = begin[-2]
                states[0, b, 1] = begin[-1]
            lax.fori_loop(0, length, again, tuple(begin), unroll=2)
            pump(2)
            if q == 0:
                wanted["mid_near"].wait_recv()
                wanted["mid_far"] = swap_factor(mid2.at[core_half, :], mid2.at[core_half, :], 3, beside)
            if q > 0:
                table_line.begin(q - 1)
            if q > 1:
                table_line.settle(q - 2)

            def back(i, carry, h=h, lr=lr, li=li, cr=cr, ci=ci):
                glr, gli, gcr, gci = carry[:4]
                adjoint = carry[4:]
                p = length - 1 - i
                new = []
                for b in range(streams):
                    ar, ai = adjoint[2 * b], adjoint[2 * b + 1]
                    g = row(row_b, b, p)
                    m = row(keep, b, p)
                    nr = (lr * ar + li * ai) + cr * g
                    ni = (lr * ai - li * ar) - ci * g
                    spot = pl.ds(pl.multiple_of((b * length + p) * 8, 8), 8)
                    if h == 0:
                        part[spot, :] = nr.sum(0)
                    else:
                        part[spot, :] += nr.sum(0)
                    gcr = gcr + g * states[p + 1, b, 0]
                    gci = gci - g * states[p + 1, b, 1]
                    nr = nr * m
                    ni = ni * m
                    sr, si = states[p, b, 0], states[p, b, 1]
                    glr = glr + (nr * sr + ni * si)
                    gli = gli + (ni * sr - nr * si)
                    new += [nr, ni]
                return (glr, gli, gcr, gci, *new)

            begin = []
            for b in range(streams):
                begin += [tile(adj, (b, 0), rows, cols), tile(adj, (b, 1), rows, cols)]
            sums = lax.fori_loop(0, length, back, (zero, zero, zero, zero, *begin))
            glr, gli, gcr, gci = [item.reshape(-1, LANES) for item in sums[:4]]
            share = factor[rows, cols]
            ratio = (1.0 - share * share) / share
            spots = [pl.ds(i * group, group) for i in range(4)]
            table[q, spots[0], :] = (gcr * real_ref[rows, cols] + gci * imag_ref[rows, cols]) * ratio - (
                glr * lam[0, rows, cols] + gli * lam[1, rows, cols]
            )
            table[q, spots[1], :] = gli * lam[0, rows, cols] - glr * lam[1, rows, cols]
            table[q, spots[2], :] = share * gcr
            table[q, spots[3], :] = share * gci
            wanted["table", q] = swap_factor(table.at[q], table2.at[q], 10 + q)
            if q == 0:
                need("mid_far")
                transposed(mid2, mid_t2, n_chan)
            pump(2)
            if q > 0:
                table_line.join(q - 1)
            if q > 1:
                table_line.relay(q - 2)
            q += 1
        for b in range(streams):
            total = part[pl.ds(b * length * 8, length, stride=8), :]
            for j in range(1, 8):
                total = total + part[pl.ds(b * length * 8 + j, length, stride=8), :]
            u_grad = total + skip_ref[:, cols] * row_b[b]
            du[b * length : (b + 1) * length, cols] = u_grad * valid[b]

    scaled = du[...] * gain1[...]
    stat_copies = stats_start(
        jnp.sum(scaled, axis=1, keepdims=True),
        jnp.sum(scaled * normed1[...], axis=1, keepdims=True), 3, base + 6,
    )
    gain_rows = [
        jnp.sum(du[...] * normed1[...], axis=0, keepdims=True),
        jnp.sum(jnp.sum(mixer_grad[...] * u_ref[...], axis=0), axis=0, keepdims=True),
        gains,
    ]
    gain_sums[...] = jnp.concatenate([*gain_rows, jnp.zeros((5, width), f32)], axis=0)
    wanted["gains"] = swap_factor(gain_sums, gain_sums2, 8)
    last = quarters - 1
    table_line.begin(last)
    if last > 0:
        table_line.settle(last - 1)
    first, second = stats_end(stat_copies, 3)
    in_grad[...] = (
        resid_grad[...] + scaler1 * (du[...] * gain1[...] - first - normed1[...] * second)
    ).reshape(streams, length, width)
    gains_line.begin(0)
    pump(1)
    table_line.join(last)
    if last > 0:
        table_line.relay(last - 1)
    gains_line.join(0)
    pump(2)
    table_line.settle(last)
    gains_line.settle(0)
    pump(2)
    table_line.relay(last)
    gains_line.relay(0)
    while tick[0] < len(pieces) + STORE:
        pump(1)
    for k in range(width // LANES):
        for h in range(n_states // group):
            for i in range(4):
                tables_out[i, h * group : (h + 1) * group, k * LANES : (k + 1) * LANES] = table_sum[
                    k * (n_states // group) + h, i * group : (i + 1) * group, :
                ]
    gains_out[...] = gains_sum[0]
    for entry in lines:
        entry.finish()
    for copy in factors:
        copy.wait_send()
    for copy in sent:
        copy.wait_send()
    for carry in (*forward, *backward):
        carry.finish()


def rows_in_of(ref, tokens, width):
    return ref[...].reshape(tokens, width)


def cast_kernel(
    steps, gin, gout, gv, gg, block, grad, tables, gains,
    gin_hbm, gout_hbm, gv_hbm, gg_hbm, block_out, grad_out, dec_out, ang_out, real_out, imag_out, gain_a, gain_b, gain_c,
    gin_low, gout_low, gv_low, gg_low, gin_out, gout_out, gv_out, gg_out, table_low, gain_low, block_low, grad_low, load_sem, save_sem, small_sem,
):
    whole = [
        pltpu.make_async_copy(src, dst, small_sem.at[i])
        for i, (src, dst) in enumerate(
            [(tables, table_low), (gains, gain_low), (block, block_low), (grad, grad_low)]
        )
    ]
    full, units = gin_out.shape
    loads, saves = [], []
    for p in range(steps):
        high = 2 * p // steps
        low = p % (steps // 2)
        rows, tall = full // steps, units // steps
        part = pl.ds(low * rows, rows)
        tall_part = pl.ds(low * tall, tall)
        here, tall_here = pl.ds(p * rows, rows), pl.ds(p * tall, tall)
        loads.append(
            [
                pltpu.make_async_copy(gin.at[:, :, high, part], gin_low.at[:, :, high, part], load_sem.at[0, p]),
                pltpu.make_async_copy(gout.at[high, :, tall_part], gout_low.at[high, :, tall_part], load_sem.at[1, p]),
                pltpu.make_async_copy(gv.at[:, here], gv_low.at[:, here], load_sem.at[2, p]),
                pltpu.make_async_copy(gg.at[:, here], gg_low.at[:, here], load_sem.at[3, p]),
            ]
        )
        saves.append(
            [
                pltpu.make_async_copy(gin_out.at[here], gin_hbm.at[here], save_sem.at[0, p]),
                pltpu.make_async_copy(gout_out.at[tall_here], gout_hbm.at[tall_here], save_sem.at[1, p]),
                pltpu.make_async_copy(gv_out.at[here], gv_hbm.at[here], save_sem.at[2, p]),
                pltpu.make_async_copy(gg_out.at[here], gg_hbm.at[here], save_sem.at[3, p]),
            ]
        )
    for copies in loads:
        for copy in copies:
            copy.start()
    for copy in whole:
        copy.start()
    for p in range(steps):
        high, low = 2 * p // steps, p % (steps // 2)
        rows, tall = full // steps, units // steps
        part, tall_part = slice(low * rows, (low + 1) * rows), slice(low * tall, (low + 1) * tall)
        here, tall_here = slice(p * rows, (p + 1) * rows), slice(p * tall, (p + 1) * tall)
        for copy in loads[p]:
            copy.wait()
        cols = gin.shape[-1]
        for x in range(2):
            for i in range(4):
                at = (4 * x + i) * cols
                gin_out[here, at : at + cols] = gin_low[x, i, high, part].astype(f32)
        cols = gout.shape[-1]
        for i in range(8):
            gout_out[tall_here, i * cols : (i + 1) * cols] = gout_low[high, i, tall_part].astype(f32)
        cols = gv.shape[-1]
        for x in range(2):
            gv_out[here, x * cols : (x + 1) * cols] = gv_low[x, here].astype(f32)
            gg_out[here, x * cols : (x + 1) * cols] = gg_low[x, here].astype(f32)
        for copy in saves[p]:
            copy.start()
    for copy in whole:
        copy.wait()
    passed_on = [
        pltpu.make_async_copy(block_low, block_out, small_sem.at[4]),
        pltpu.make_async_copy(grad_low, grad_out, small_sem.at[5]),
    ]
    for copy in passed_on:
        copy.start()
    for k, out in enumerate((dec_out, ang_out, real_out, imag_out)):
        out[...] = table_low[k]
    for k, out in enumerate((gain_a, gain_b, gain_c)):
        out[...] = gain_low[k : k + 1, :]
    for copies in (*saves, passed_on):
        for copy in copies:
            copy.wait()


def per_device(
    sizes, block_in, doc_lengths, out_grad, first_gain, decay_rate, turn_angle, out_real, out_imag,
    skip_gain, glu_value, glu_gate, second_gain, ffn_in, ffn_out,
):
    n_seq, n_chan = sizes
    pairs = n_seq // 2
    streams, length, width = block_in.shape
    n_states = decay_rate.shape[1]
    tokens = streams * length
    full = width * n_chan
    units = ffn_in.shape[1]
    glu_cols = glu_value.shape[1]
    group = min(32, n_states)
    like = jax.ShapeDtypeStruct
    quarters = (width // LANES) * (n_states // group)
    phases = 12
    act = (streams, length, width)
    flat = (tokens, width)
    mask = (streams, length, LANES)
    tab, lane_tab = (2, n_states, width), (2, n_states, LANES)
    tiles = width // LANES
    V = pltpu.VMEM
    scratch = [
        V((2, 4, 2, full // 2, units // 8), bf16), V((2, 8, units // 2, full // 8), bf16), *[V((2, 4, full // 4, glu_cols // 2), bf16)] * 2,
        V((full, glu_cols), bf16), V((full, glu_cols), bf16), V((full, units), bf16), V((units, full), bf16),
        V(mask, f32), V(mask, f32), V(mask, f32), V(mask, f32),
        V(tab, f32), V(tab, f32), V(tab, f32), V((n_states, width), f32),
        V((8, full), f32), V(flat, f32), V(act, f32), V(act, f32), V((tiles, streams, 2, n_states, LANES), f32), V((streams, *tab), f32), V((streams, *tab), f32),
        V((tokens, full), bf16), V((tokens, glu_cols), f32), V((tokens, glu_cols), f32), V(flat, f32), V(flat, f32),
        V((tokens, full), bf16), V((tokens, full), bf16), V((tokens, units), f32), V((tokens, units), bf16), V((tokens, units), bf16),
        V((full, tokens), bf16), V((full, tokens), bf16), V((units, tokens), bf16),
        V(flat, f32), V(flat, f32), V(flat, f32), V(flat, f32), V((tokens, glu_cols), bf16), V((tokens, glu_cols), bf16), V(flat, f32),
        V(act, f32), V(flat, f32),
        V(mask, f32), V(mask, f32), V((tokens * 8, LANES), f32), V((length + 1, streams, 2, group // 8, 8, LANES), f32),
        V((4, 8, tokens), f32), V((4, n_chan - 1, 8, tokens), f32), V((3, n_chan - 1, *flat), bf16), V((3, n_chan - 1, *flat), bf16),
        *[V((2, tiles, streams, *lane_tab), bf16)] * 2, V((2, tiles, *lane_tab), bf16), V((2, tiles, pairs - 1, *lane_tab), bf16),
        V(lane_tab, f32), *[V((2, tiles, *lane_tab), bf16)] * 2,
        *[V((quarters, 4 * group, LANES), f32)] * 6,
        V((8, width), f32), V((8, width), f32), *[V((1, 8, width), f32)] * 4,
        *[V((tokens, full), bf16)] * 3, V((full, tokens), bf16), V((full, tokens), bf16), V((units // 2, tokens), bf16),
        V((tokens, units // 2), bf16), V((tokens, glu_cols // 2), bf16), V((tokens, glu_cols // 2), bf16),
        *[V((8, full // 2, units // 8), bf16)] * 3, *[V((8, units // 2, full // 8), bf16)] * 3,
        *[V((4, full // 4, glu_cols // 2), bf16)] * 6,
        pltpu.SemaphoreType.DMA((4,)), pltpu.SemaphoreType.DMA((2, 24)),
        pltpu.SemaphoreType.DMA((phases, n_chan - 1)), pltpu.SemaphoreType.DMA((phases, n_chan - 1)),
        pltpu.SemaphoreType.DMA((2, tiles, pairs + 1)), pltpu.SemaphoreType.DMA((2, tiles, pairs + 1)),
        pltpu.SemaphoreType.DMA((10 + quarters,)), pltpu.SemaphoreType.DMA((10 + quarters,)),
        pltpu.SemaphoreType.DMA((3, 25 + quarters)), pltpu.SemaphoreType.DMA((4, 25 + quarters)),
    ]
    specs = [pl.BlockSpec(memory_space=pltpu.SMEM)] + [VM] * 8 + [ANY, ANY, VM, ANY, ANY]
    made = pl.pallas_call(
        functools.partial(block_kernel, sizes),
        out_shape=(
            like(act, f32), like(act, f32), like((4, n_states, width), f32), like((8, width), f32),
            like((2, 4, 2, full // 2, units // 8), bf16), like((2, 8, units // 2, full // 8), bf16),
            like((2, 4, full // 4, glu_cols // 2), bf16), like((2, 4, full // 4, glu_cols // 2), bf16),
        ),
        in_specs=specs,
        out_specs=(VM,) * 4 + (ANY,) * 4,
        scratch_shapes=scratch,
        compiler_params=pltpu.CompilerParams(
            collective_id=0, has_side_effects=True, vmem_limit_bytes=58 * 1024 * 1024
        ),
        name="block",
    )(
        doc_lengths, block_in, out_grad, first_gain[None], decay_rate.T, turn_angle.T, out_real.T, out_imag.T, skip_gain[None],
        glu_value, glu_gate, second_gain[None], ffn_in, ffn_out,
    )
    block_out, in_grad, tables, gains, gin, gout, gv, gg = made
    steps = 4
    small = (n_states, width)
    low_glu = (2, full, glu_cols // 2)
    cast = pl.pallas_call(
        functools.partial(cast_kernel, steps),
        out_shape=(
            like((full, units), f32), like((units, full), f32), like((full, glu_cols), f32), like((full, glu_cols), f32),
            like(act, f32), like(act, f32), like(small, f32), like(small, f32), like(small, f32), like(small, f32),
            *[like((1, width), f32)] * 3,
        ),
        in_specs=[ANY] * 8,
        out_specs=(ANY,) * 6 + (VM,) * 7,
        scratch_shapes=[
            V(gin.shape, bf16), V(gout.shape, bf16), V(low_glu, bf16), V(low_glu, bf16),
            V((full, units), f32), V((units, full), f32), V((full, glu_cols), f32), V((full, glu_cols), f32),
            V(tables.shape, f32), V(gains.shape, f32), V(act, f32), V(act, f32),
            pltpu.SemaphoreType.DMA((4, steps)), pltpu.SemaphoreType.DMA((4, steps)), pltpu.SemaphoreType.DMA((6,)),
        ],
        compiler_params=pltpu.CompilerParams(vmem_limit_bytes=58 * 1024 * 1024),
        name="cast",
    )(gin, gout, gv.reshape(low_glu), gg.reshape(low_glu), block_out, in_grad, tables, gains)
    gin, gout, gv, gg, block_out, in_grad, dec, ang, real, imag, *gains = cast
    return (
        block_out, in_grad, gains[0][0], dec.T, ang.T, real.T, imag.T, gains[1][0], gv, gg, gains[2][0], gin, gout,
    )


def solution(mesh):
    act = P(None, "seq", "chan")
    vec, mat = P("chan"), P("chan", None)
    col = P(None, "chan")
    sizes = (mesh.shape["seq"], mesh.shape["chan"])
    return jax.shard_map(
        functools.partial(per_device, sizes),
        mesh=mesh,
        in_specs=(act, P(), act, vec, mat, mat, mat, mat, vec, col, col, vec, col, mat),
        out_specs=(act, act, vec, mat, mat, mat, mat, vec, col, col, vec, col, mat),
        check_vma=False,
    )
```

time: 213 us -> 158 us (0.74)
  Pallas kernels: 192 us -> 157 us
  local copies, waits for them, and re-layouts: 19.4 us -> 0 us
    pallas_call x1, Pallas kernels: 188 us -> 150 us  [per_device(): pl.pallas_call(functools.partial(block_kernel, sizes), out_shape=(like(ac...]
    unnamed x24 -> x0, local copies, waits for them, and re-layouts: 18 us -> none
where the time goes in v3:
time: 158 us
  Pallas kernels  157 us (99%)
    pallas_call x1, Pallas kernels, per_device(): pl.pallas_call(functools.partial(block_kernel, sizes), out_shape=(like(ac...  150 us
    pallas_call x1, Pallas kernels, per_device(): pl.pallas_call(functools.partial(cast_kernel, steps), out_shape=(like((fu...  6.5 us

profile of v3, /device:TPU:0, one launch (start us, length us, event | category | flops | bytes accessed | tf_op | source)
XLA Modules:
  0.0 157.8 jit_solution(14783369532747001144)
XLA Ops:
  0.7 150.5 %block.1 = (f32[2,128,256]{2,1,0:T(8,128)}, f32[2,128,256]{2,1,0:T(8,128)}, f32[4,64,256]{2,1,0:T(8,128)}, f32[8,256]{1,0:T(8,128)}, bf16[2,4,2,512,128]{4,3,2,1...) custom-call(s32[2,16]{1,0:T(2,128)} %docs.1, ...), custom_call_target="tpu_custom_call" | custom-call | tf_op jit(solution)/shard_map/block/pallas_call | solution.py:1019
  151.1 6.5 %cast.1 = (f32[1024,1024]{1,0:T(8,128)}, f32[1024,1024]{1,0:T(8,128)}, f32[1024,256]{1,0:T(8,128)}, f32[1024,256]{1,0:T(8,128)}, f32[2,128,256]{2,1,0:T(8,128)},...) custom-call(bf16[2,4,2,512,128]{4,3,2,1,0:T(8,128)(2,1)} %get-tuple-, ...), custom_call_target="tpu_custom_call" | custom-call | tf_op jit(solution)/shard_map/cast/pallas_call | solution.py:1041

commit v4 on v3

--- a/solution.py
+++ b/solution.py
@@ -172,16 +172,16 @@
     keep, first_mask, last_mask, valid,
     lam, coef, step_l, factor,
     gain_full, normed1, u_ref, y_ref, edge_sum, init, adj,
-    act_full, val, gate, resid, normed2, grad_full, mid_full, hidden_grad, hidden, pre,
-    act_t, mid_t, hidden_t, part_own, mid_grad, result_own, resid_grad, value_grad, gate_grad, act_own, mixer_grad, du,
-    row_a, row_b, part, states,
+    act_full, centred, val, gate, resid, normed2, grad_full, mid_full, hidden_grad, hidden, pre,
+    act_t, mid_t, hidden_t, part_own, mid_grad, result_own, resid_grad, value_grad, gate_grad, mixer_grad,
+    row_a, row_b, u_rows, keep4, tails, part, states,
     stat_send, stat_recv, rs_send, rs_recv,
     pair_send, pair_recv, line_send, line_recv, back_send, back_low, back_recv,
     table, table2, table_sum, table_send, table_in, table_across,
-    gain_sums, gain_sums2, gains_sum, gains_send, gains_in, gains_across,
+    gain_all,
     grad2, act2, mid2, act_t2, mid_t2, hidden_t2, pre2, value2, gate2,
     in_send, in_in, in_across, out_send, out_in, out_across, gv_send, gv_in, gv_across, gg_send, gg_in, gg_across,
-    load_sem, save_sem, chan_send, chan_recv, seq_send, seq_recv, fac_send, fac_recv, line_sent, line_got,
+    load_sem, save_sem, chan_send, chan_recv, seq_send, seq_recv, fac_send, fac_recv, gain_send, gain_recv, line_sent, line_got,
 ):
     n_seq, n_chan = sizes
     pairs = n_seq // 2
@@ -190,12 +190,13 @@
     tokens = streams * length
     full = width * n_chan
     units = win.shape[1]
-    group = states.shape[3] * 8
+    group = states.shape[4] * 8
     s, c = lax.axis_index("seq"), lax.axis_index("chan")
     odd = lax.rem(s, 2)
     level = lax.div(s, 2)
     partner = (s + 1 - 2 * odd, c)
     every = pl.ds(0, n_states)
+    tiles = width // LANES
 
     def chan_peer(j):
         return lax.rem(c + j, n_chan)
@@ -208,10 +209,8 @@
     barrier = pltpu.get_barrier_semaphore()
     for j in range(1, n_chan):
         pl.semaphore_signal(barrier, inc=1, device_id=(s, chan_peer(j)), device_id_type=MESH)
-    pl.semaphore_signal(barrier, inc=1, device_id=partner, device_id_type=MESH)
-    for d in range(1, pairs):
-        other = 2 * lax.rem(level + d, pairs) + odd
-        pl.semaphore_signal(barrier, inc=1, device_id=(other, c), device_id_type=MESH)
+    for d in range(1, n_seq):
+        pl.semaphore_signal(barrier, inc=1, device_id=(lax.rem(s + d, n_seq), c), device_id_type=MESH)
 
     loads = [
         pltpu.make_async_copy(src, dst, load_sem.at[i])
@@ -262,11 +261,11 @@
     grad_full[:, own_cols] = og_ref[...].reshape(tokens, width).astype(bf16)
     sum1 = jnp.sum(rows_in, axis=1, keepdims=True)
     square1 = jnp.sum(rows_in * rows_in, axis=1, keepdims=True)
-    pl.semaphore_wait(barrier, n_chan + pairs - 1)
+    pl.semaphore_wait(barrier, n_chan + n_seq - 2)
     stat_copies = stats_start(sum1, square1, 0, 0)
     grad_copies = chan_all(lambda j: (grad_full.at[:, own_cols], grad_full.at[:, own_cols]), 1)
     gain_full[:, own_cols] = jnp.broadcast_to(gain2[...], (8, width))
-    gain_copies = chan_all(lambda j: (gain_full.at[:, own_cols], gain_full.at[:, own_cols]), 11)
+    gain_copies = chan_all(lambda j: (gain_full.at[:, own_cols], gain_full.at[:, own_cols]), 9 + streams * tiles)
 
     start = s * length
     ends = []
@@ -484,15 +483,18 @@
         for name in names:
             wanted[name].wait_recv()
 
-    in_rows, in_cols = full // 2, half_units // 4
-    out_cols = full // 8
+    in_rows, in_cols = full // 4, units // 4
+    out_rows, out_cols = units // 4, full // 4
     glu_rows, glu_half = full // 4, width // 2
     my_glu, their_glu = chan_block(odd, glu_half), chan_block(1 - odd, glu_half)
 
+    ready = []
+
     def in_own(i):
+        assert "mid" in ready
         if i == 0:
             need("pre")
-        rows, cols = pl.ds((i % 2) * in_rows, in_rows), (i // 2) * in_cols
+        rows, cols = pl.ds((i // 2) * in_rows, in_rows), (i % 2) * in_cols
         mine = pl.ds(pl.multiple_of(odd * half_units + cols, in_cols), in_cols)
         return dot(mid_t[rows, :], pre[:, mine]) + dot(mid_t2[rows, :], pre2[:, pl.ds(cols, in_cols)])
 
@@ -501,17 +503,21 @@
 
     def out_own(i):
         if i == 0:
-            need("grad", "hidden")
-        cols = pl.ds(i * out_cols, out_cols)
-        return dot(hidden_t[my_half, :], grad_full[:, cols]) + dot(hidden_t2[...], grad2[:, cols])
+            need("grad", ("hidden", 0))
+        if i == 4:
+            need(("hidden", 1))
+        rows, cols = (i // 4) * out_rows, pl.ds((i % 4) * out_cols, out_cols)
+        mine = pl.ds(pl.multiple_of(odd * half_units + rows, out_rows), out_rows)
+        return dot(hidden_t[mine, :], grad_full[:, cols]) + dot(hidden_t2[pl.ds(rows, out_rows), :], grad2[:, cols])
 
     def out_at(i):
-        return gout_out.at[odd, i]
+        return gout_out.at[odd, i // 4, i % 4]
 
     def glu_own(near, far, names):
         def own(i):
             if i == 0:
                 need(*names)
+            assert "act" in ready
             rows = pl.ds(i * glu_rows, glu_rows)
             return dot(act_t[rows, :], near[:, my_glu]) + dot(act_t2[rows, :], far[...])
 
@@ -526,10 +532,6 @@
     def table_own(q):
         need(("table", q))
         return table[q] + table2[q]
-
-    def gains_own(i):
-        need("gains")
-        return gain_sums[...] + gain_sums2[...]
 
     sem_at = [0]
 
@@ -547,12 +549,11 @@
 
     quarters = (width // LANES) * (n_states // group)
     in_line = line(in_own, 8, in_at, (in_send, in_in, in_across), True, (gin_out, gin_hbm, lambda i: (i // 2, i % 2)))
-    out_line = line(out_own, 8, out_at, (out_send, out_in, out_across), True, (gout_out, gout_hbm, lambda i: (i,)))
+    out_line = line(out_own, 8, out_at, (out_send, out_in, out_across), True, (gout_out, gout_hbm, lambda i: (i // 4, i % 4)))
     gv_line = line(glu_own(value_grad, value2, ("value",)), 4, glu_at(gv_out), (gv_send, gv_in, gv_across), True, (gv_out, gv_hbm, lambda i: (i,)))
     gg_line = line(glu_own(gate_grad, gate2, ("gate",)), 4, glu_at(gg_out), (gg_send, gg_in, gg_across), True, (gg_out, gg_hbm, lambda i: (i,)))
     table_line = line(table_own, quarters, lambda q: table_sum.at[q], (table_send, table_in, table_across), False)
-    gains_line = line(gains_own, 1, lambda i: gains_sum.at[i], (gains_send, gains_in, gains_across), False)
-    lines = [out_line, gv_line, in_line, gg_line, table_line, gains_line]
+    lines = [out_line, gv_line, in_line, gg_line, table_line]
     pieces = [(entry, i) for entry in lines[:4] for i in range(entry.count)]
     tick, begun = [0], [0]
     MID, LAST, STORE = 2, 4, 8
@@ -564,7 +565,7 @@
                 entry.begin(i)
             begun[0] += 1
 
-    def pump(count, lead=3):
+    def pump(count, lead=4):
         for _ in range(count):
             t = tick[0]
             tick[0] += 1
@@ -574,7 +575,6 @@
                     entry, i = pieces[t + ahead]
                     getattr(entry, act)(i)
 
-    tiles = width // LANES
     forward = [Carry(init, 0, False, k) for k in range(tiles)]
     for k in range(tiles):
         edges(u_ref, last_mask, False, k)
@@ -601,33 +601,111 @@
     for k in range(tiles):
         forward[k].end()
         cols = pl.ds(k * LANES, LANES)
-        lr, li = tile(lam, (0,), every, cols), tile(lam, (1,), every, cols)
-        cr, ci = tile(coef, (0,), every, cols), tile(coef, (1,), every, cols)
-        row_a[...] = u_ref[:, :, cols]
+        u_rows[k] = u_ref[:, :, cols]
+        near = [jnp.sum(coef[0, :, cols], axis=0, keepdims=True)]
+        qr, qi = coef[0, :, cols], coef[1, :, cols]
+        for _ in range(3):
+            qr, qi = cmul(qr, qi, lam[0, :, cols], lam[1, :, cols])
+            near.append(jnp.sum(qr, axis=0, keepdims=True))
+        fours = length // 4
+        local, through = [], []
         for b in range(streams):
-
-            def move(p, carry, b=b, lr=lr, li=li, cr=cr, ci=ci):
-                sr, si = carry
-                u = row(row_a, b, p)
+            us = [u_rows[k, b, pl.ds(j, fours, stride=4), :] for j in range(4)]
+            ks = [keep[b, pl.ds(j, fours, stride=4), :] for j in range(4)]
+            reach = ks[0]
+            passed_by = [reach]
+            for j in range(1, 4):
+                reach = reach * ks[j]
+                passed_by.append(reach)
+            through.append(passed_by)
+            keep4[b] = reach
+            terms, outs = [], []
+            for j in range(4):
+                terms = [term * ks[j] for term in terms] + [us[j]]
+                out = skip_ref[:, cols] * us[j]
+                for i, term in enumerate(terms):
+                    out = out + near[j - i] * term
+                outs.append(out)
+            local.append(outs)
+            for j in range(4):
+                tails[b, j] = terms[j]
+        for h in range(n_states // group):
+            rows = pl.ds(h * group, group)
+            l1r, l1i = tile(lam, (0,), rows, cols), tile(lam, (1,), rows, cols)
+            l2r, l2i = cmul(l1r, l1i, l1r, l1i)
+            l3r, l3i = cmul(l2r, l2i, l1r, l1i)
+            l4r, l4i = cmul(l2r, l2i, l2r, l2i)
+            cr, ci = tile(coef, (0,), rows, cols), tile(coef, (1,), rows, cols)
+            taps = [cmul(cr, ci, *power_of) for power_of in ((l1r, l1i), (l2r, l2i), (l3r, l3i), (l4r, l4i))]
+
+            def move(i, carry, h=h, l1=(l1r, l1i), l2=(l2r, l2i), l3=(l3r, l3i), l4=(l4r, l4i), taps=taps):
+                new = []
+                for b in range(streams):
+                    sr, si = carry[2 * b], carry[2 * b + 1]
+                    for j in range(4):
+                        spot = pl.ds(pl.multiple_of(((b * 4 + j) * fours + i) * 8, 8), 8)
+                        out = (taps[j][0] * sr - taps[j][1] * si).sum(0)
+                        if h == 0:
+                            part[spot, :] = out
+                        else:
+                            part[spot, :] += out
+                    m = row(keep4, b, i)
+                    t = [row(tails.at[b], j, i) for j in range(4)]
+                    sr = sr * m
+                    si = si * m
+                    nr = (l4[0] * sr - l4[1] * si) + (l3[0] * t[0] + l2[0] * t[1]) + (l1[0] * t[2] + t[3])
+                    ni = (l4[0] * si + l4[1] * sr) + (l3[1] * t[0] + l2[1] * t[1]) + l1[1] * t[2]
+                    new += [nr, ni]
+                return tuple(new)
+
+            begin = []
+            for b in range(streams):
+                begin += [tile(init, (b, 0), rows, cols), tile(init, (b, 1), rows, cols)]
+            lax.fori_loop(0, fours, move, tuple(begin))
+        for b in range(streams):
+            for j in range(4):
+                first = (b * 4 + j) * fours * 8
+                total = part[pl.ds(first, fours, stride=8), :]
+                for i in range(1, 8):
+                    total = total + part[pl.ds(first + i, fours, stride=8), :]
+                row_a[b, pl.ds(j, fours, stride=4), :] = through[b][j] * total + local[b][j]
+            y = row_a[b]
+            y_ref[b, :, cols] = y
+            to = pl.ds(pl.multiple_of(c * width + k * LANES, LANES), LANES)
+            here = pl.ds(b * length, length)
+            act_full[here, to] = gelu_parts(y)[0].astype(bf16)
+            act_copies.append(
+                chan_all(lambda j: (act_full.at[here, to], act_full.at[here, to]), 2 + streams * k + b)
+            )
+    base = 2 + streams * tiles
+
+    def again_pass(q):
+        k, h = q // (n_states // group), q % (n_states // group)
+        rows, cols = pl.ds(h * group, group), pl.ds(k * LANES, LANES)
+        lr, li = tile(lam, (0,), rows, cols), tile(lam, (1,), rows, cols)
+        held = states.at[q % 2]
+
+        def again(p, carry):
+            new = []
+            for b in range(streams):
+                sr, si = carry[2 * b], carry[2 * b + 1]
+                u = row(u_rows.at[k], b, p)
                 m = row(keep, b, p)
                 sr = sr * m
                 si = si * m
                 nr = (lr * sr - li * si) + u
                 ni = lr * si + li * sr
-                part[pl.ds(pl.multiple_of(p * 8, 8), 8), :] = (cr * nr - ci * ni).sum(0)
-                return nr, ni
-
-            begin = (tile(init, (b, 0), every, cols), tile(init, (b, 1), every, cols))
-            lax.fori_loop(0, length, move, begin, unroll=2)
-            total = part[pl.ds(0, length, stride=8), :]
-            for j in range(1, 8):
-                total = total + part[pl.ds(j, length, stride=8), :]
-            y = total + skip_ref[:, cols] * u_ref[b, :, cols]
-            y_ref[b, :, cols] = y
-            to = pl.ds(pl.multiple_of(c * width + k * LANES, LANES), LANES)
-            act_full[b * length : (b + 1) * length, to] = gelu_parts(y)[0].astype(bf16)
-        act_copies.append(chan_all(lambda j: (act_full.at[:, to], act_full.at[:, to]), 2 + k))
-    base = 2 + width // LANES
+                held[p + 1, b, 0] = nr
+                held[p + 1, b, 1] = ni
+                new += [nr, ni]
+            return tuple(new)
+
+        begin = []
+        for b in range(streams):
+            begin += [tile(init, (b, 0), rows, cols), tile(init, (b, 1), rows, cols)]
+            held[0, b, 0] = begin[-2]
+            held[0, b, 1] = begin[-1]
+        lax.fori_loop(0, length, again, tuple(begin), unroll=2)
 
     loads[1].wait()
     loads[2].wait()
@@ -642,21 +720,39 @@
 
     sum2 = jnp.sum(resid[...], axis=1, keepdims=True)
     square2 = jnp.sum(resid[...] * resid[...], axis=1, keepdims=True)
+    centred[:, own_cols] = (resid[...] - sum2 / width).astype(bf16)
     stat_copies = stats_start(sum2, square2, 1, base)
-    average, square = stats_end(stat_copies, 1)
+    mid_copies = chan_all(lambda j: (centred.at[:, own_cols], centred.at[:, own_cols]), base + 1)
+    landed(gain_copies)
+    landed(stat_copies)
+    shares = [stat_send[1], *[stat_recv[1, j - 1] for j in range(1, n_chan)]]
+    shares = jnp.concatenate([*shares, jnp.zeros((LANES - 8 * n_chan, tokens), f32)], axis=0).T
+    average, square = 0.0, 0.0
+    for j in range(n_chan):
+        average = average + shares[:, 8 * j : 8 * j + 1] / full
+        square = square + shares[:, 8 * j + 1 : 8 * j + 2] / full
     scaler2 = lax.rsqrt(square - average * average + epsilon)
     normed2[...] = (resid[...] - average) * scaler2
     mid_full[:, own_cols] = (normed2[...] * gain2[...]).astype(bf16)
-    mid_copies = chan_all(lambda j: (mid_full.at[:, own_cols], mid_full.at[:, own_cols]), base + 1)
+    landed(mid_copies)
+    for j in range(1, n_chan):
+        cols = chan_block(lax.rem(c - j + n_chan, n_chan), width)
+        shift = shares[:, 8 * j : 8 * j + 1] / width - average
+        mid_full[:, cols] = ((centred[:, cols].astype(f32) + shift) * scaler2 * gain_full[0:1, cols]).astype(bf16)
     loads[3].wait()
-    landed(mid_copies)
-
-    for k in range(units // unit_block):
-        cols = pl.ds(k * unit_block, unit_block)
+
+    for k in range(4):
+        cols = pl.ds(k * out_rows, out_rows)
         value, slope = gelu_parts(dot(mid_full[...], win[:, cols]))
         hidden[:, cols] = value.astype(bf16)
         pre[:, cols] = (hidden_grad[:, cols] * slope).astype(bf16)
         hidden_t[cols, :] = hidden[:, cols].T
+    for k in range(2):
+        theirs = pl.ds(pl.multiple_of((1 - odd) * half_units + k * out_rows, out_rows), out_rows)
+        wanted["hidden", k] = swap_factor(
+            hidden_t.at[theirs, :], hidden_t2.at[pl.ds(k * out_rows, out_rows), :], 4 if k == 0 else 10 + quarters
+        )
+
     def scatter_fill(piece, own, k):
         for j in range(1, n_chan):
             rs_send[k, j - 1] = piece(chan_block(chan_peer(j), width)).astype(bf16)
@@ -678,8 +774,6 @@
 
     scatter_fill(lambda rows: dot(pre[...], win[rows, :], NT), part_own, 0)
     grad_parts = scatter_start(0, base + 2)
-    wanted["hidden"] = swap_factor(hidden_t.at[their_half, :], hidden_t2, 4)
-    landed(gain_copies)
     first, second = 0.0, 0.0
     for j in range(n_chan):
         cols = chan_block(chan_peer(j), width) if j else own_cols
@@ -692,7 +786,9 @@
     transposed(mid_full, mid_t, n_chan)
     wanted["act_near"].wait_recv()
     wanted["act_far"] = swap_factor(act2.at[core_half, :], act2.at[core_half, :], 9, beside)
-    launch(2)
+    for q in range(min(2, quarters)):
+        again_pass(q)
+    launch(4)
     mid_grad[...] = scatter_end(grad_parts, part_own, 0)
     wanted["pre"] = swap_factor(pre.at[:, their_half], pre2, 5)
     gains = jnp.sum(mid_grad[...] * normed2[...], axis=0, keepdims=True)
@@ -704,13 +800,13 @@
     value_grad[...] = (resid_grad[...] * gate[...]).astype(bf16)
     gate_grad[...] = (resid_grad[...] * val[...] * gate[...] * (1.0 - gate[...])).astype(bf16)
     scatter_fill(
-        lambda rows: dot(value_grad[...], gluv[rows, :], NT) + dot(gate_grad[...], glug[rows, :], NT), act_own, 2
+        lambda rows: dot(value_grad[...], gluv[rows, :], NT) + dot(gate_grad[...], glug[rows, :], NT), val, 2
     )
     act_parts = scatter_start(2, base + 5)
     wanted["value"] = swap_factor(value_grad.at[:, their_glu], value2, 6)
     wanted["gate"] = swap_factor(gate_grad.at[:, their_glu], gate2, 7)
-    pump(1, 2)
-    act_grad = scatter_end(act_parts, act_own, 2)
+    pump(2, 2)
+    act_grad = scatter_end(act_parts, val, 2)
     mixer_grad[...] = act_grad.reshape(streams, length, width) * gelu_parts(y_ref[...])[1]
 
     out_parts = scatter_start(1, base + 3)
@@ -725,48 +821,29 @@
     for k in range(tiles):
         backward[k].line()
     wanted["mid_near"] = swap_factor(mid_full.at[core_half, :], mid2.at[core_half, :], 2)
-    pump(2, 2)
+    pump(1, 2)
     total = scatter_end(out_parts, result_own, 1)
     block_out[...] = (resid[...] + total).reshape(streams, length, width)
     for k in range(tiles):
         backward[k].home()
     need("act_far")
     transposed(act2, act_t2, n_chan)
-    pump(2, 2)
+    ready.append("act")
+    pump(2)
     zero = jnp.zeros((group // 8, 8, LANES), f32)
     q = 0
     for k in range(width // LANES):
         backward[k].end()
         cols = pl.ds(k * LANES, LANES)
-        row_a[...] = u_ref[:, :, cols]
         row_b[...] = mixer_grad[:, :, cols]
         for h in range(n_states // group):
             rows = pl.ds(h * group, group)
             lr, li = tile(lam, (0,), rows, cols), tile(lam, (1,), rows, cols)
             cr, ci = tile(coef, (0,), rows, cols), tile(coef, (1,), rows, cols)
 
-            def again(p, carry, lr=lr, li=li):
-                new = []
-                for b in range(streams):
-                    sr, si = carry[2 * b], carry[2 * b + 1]
-                    u = row(row_a, b, p)
-                    m = row(keep, b, p)
-                    sr = sr * m
-                    si = si * m
-                    nr = (lr * sr - li * si) + u
-                    ni = lr * si + li * sr
-                    states[p + 1, b, 0] = nr
-                    states[p + 1, b, 1] = ni
-                    new += [nr, ni]
-                return tuple(new)
-
-            begin = []
-            for b in range(streams):
-                begin += [tile(init, (b, 0), rows, cols), tile(init, (b, 1), rows, cols)]
-                states[0, b, 0] = begin[-2]
-                states[0, b, 1] = begin[-1]
-            lax.fori_loop(0, length, again, tuple(begin), unroll=2)
-            pump(2)
+            if q > 1:
+                again_pass(q)
+            pump(2, 3 if q == 0 else 4)
             if q == 0:
                 wanted["mid_near"].wait_recv()
                 wanted["mid_far"] = swap_factor(mid2.at[core_half, :], mid2.at[core_half, :], 3, beside)
@@ -774,8 +851,9 @@
                 table_line.begin(q - 1)
             if q > 1:
                 table_line.settle(q - 2)
-
-            def back(i, carry, h=h, lr=lr, li=li, cr=cr, ci=ci):
+            held = states.at[q % 2]
+
+            def back(i, carry, h=h, held=held, lr=lr, li=li, cr=cr, ci=ci):
                 glr, gli, gcr, gci = carry[:4]
                 adjoint = carry[4:]
                 p = length - 1 - i
@@ -791,11 +869,11 @@
                         part[spot, :] = nr.sum(0)
                     else:
                         part[spot, :] += nr.sum(0)
-                    gcr = gcr + g * states[p + 1, b, 0]
-                    gci = gci - g * states[p + 1, b, 1]
+                    gcr = gcr + g * held[p + 1, b, 0]
+                    gci = gci - g * held[p + 1, b, 1]
                     nr = nr * m
                     ni = ni * m
-                    sr, si = states[p, b, 0], states[p, b, 1]
+                    sr, si = held[p, b, 0], held[p, b, 1]
                     glr = glr + (nr * sr + ni * si)
                     gli = gli + (ni * sr - nr * si)
                     new += [nr, ni]
@@ -819,6 +897,7 @@
             if q == 0:
                 need("mid_far")
                 transposed(mid2, mid_t2, n_chan)
+                ready.append("mid")
             pump(2)
             if q > 0:
                 table_line.join(q - 1)
@@ -830,40 +909,43 @@
             for j in range(1, 8):
                 total = total + part[pl.ds(b * length * 8 + j, length, stride=8), :]
             u_grad = total + skip_ref[:, cols] * row_b[b]
-            du[b * length : (b + 1) * length, cols] = u_grad * valid[b]
-
-    scaled = du[...] * gain1[...]
+            part_own[b * length : (b + 1) * length, cols] = u_grad * valid[b]
+
+    last = quarters - 1
+    pump(1)
+    table_line.begin(last)
+    if last > 0:
+        table_line.settle(last - 1)
+    scaled = part_own[...] * gain1[...]
     stat_copies = stats_start(
         jnp.sum(scaled, axis=1, keepdims=True),
         jnp.sum(scaled * normed1[...], axis=1, keepdims=True), 3, base + 6,
     )
     gain_rows = [
-        jnp.sum(du[...] * normed1[...], axis=0, keepdims=True),
+        jnp.sum(part_own[...] * normed1[...], axis=0, keepdims=True),
         jnp.sum(jnp.sum(mixer_grad[...] * u_ref[...], axis=0), axis=0, keepdims=True),
         gains,
     ]
-    gain_sums[...] = jnp.concatenate([*gain_rows, jnp.zeros((5, width), f32)], axis=0)
-    wanted["gains"] = swap_factor(gain_sums, gain_sums2, 8)
-    last = quarters - 1
-    table_line.begin(last)
-    if last > 0:
-        table_line.settle(last - 1)
+    gain_all[s] = jnp.concatenate([*gain_rows, jnp.zeros((5, width), f32)], axis=0)
+    for d in range(1, n_seq):
+        copy = pltpu.make_async_remote_copy(
+            src_ref=gain_all.at[s], dst_ref=gain_all.at[s], send_sem=gain_send.at[d], recv_sem=gain_recv.at[s],
+            device_id=(lax.rem(s + d, n_seq), c), device_id_type=MESH,
+        )
+        copy.start()
+        sent.append(copy)
+    pump(1)
     first, second = stats_end(stat_copies, 3)
     in_grad[...] = (
-        resid_grad[...] + scaler1 * (du[...] * gain1[...] - first - normed1[...] * second)
+        resid_grad[...] + scaler1 * (part_own[...] * gain1[...] - first - normed1[...] * second)
     ).reshape(streams, length, width)
-    gains_line.begin(0)
-    pump(1)
     table_line.join(last)
     if last > 0:
         table_line.relay(last - 1)
-    gains_line.join(0)
-    pump(2)
+    pump(1)
     table_line.settle(last)
-    gains_line.settle(0)
     pump(2)
     table_line.relay(last)
-    gains_line.relay(0)
     while tick[0] < len(pieces) + STORE:
         pump(1)
     for k in range(width // LANES):
@@ -872,7 +954,16 @@
                 tables_out[i, h * group : (h + 1) * group, k * LANES : (k + 1) * LANES] = table_sum[
                     k * (n_states // group) + h, i * group : (i + 1) * group, :
                 ]
-    gains_out[...] = gains_sum[0]
+    for d in range(1, n_seq):
+        source = lax.rem(s + d, n_seq)
+        pltpu.make_async_remote_copy(
+            src_ref=gain_all.at[s], dst_ref=gain_all.at[source], send_sem=gain_send.at[d], recv_sem=gain_recv.at[source],
+            device_id=(source, c), device_id_type=MESH,
+        ).wait_recv()
+    total = gain_all[0]
+    for k in range(1, n_seq):
+        total = total + gain_all[k]
+    gains_out[...] = total
     for entry in lines:
         entry.finish()
     for copy in factors:
@@ -899,20 +990,16 @@
         )
     ]
     full, units = gin_out.shape
+    rows, tall = full // steps, units // steps
     loads, saves = [], []
     for p in range(steps):
-        high = 2 * p // steps
-        low = p % (steps // 2)
-        rows, tall = full // steps, units // steps
-        part = pl.ds(low * rows, rows)
-        tall_part = pl.ds(low * tall, tall)
         here, tall_here = pl.ds(p * rows, rows), pl.ds(p * tall, tall)
         loads.append(
             [
-                pltpu.make_async_copy(gin.at[:, :, high, part], gin_low.at[:, :, high, part], load_sem.at[0, p]),
-                pltpu.make_async_copy(gout.at[high, :, tall_part], gout_low.at[high, :, tall_part], load_sem.at[1, p]),
-                pltpu.make_async_copy(gv.at[:, here], gv_low.at[:, here], load_sem.at[2, p]),
-                pltpu.make_async_copy(gg.at[:, here], gg_low.at[:, here], load_sem.at[3, p]),
+                pltpu.make_async_copy(gin.at[:, p], gin_low.at[:, p], load_sem.at[0, p]),
+                pltpu.make_async_copy(gout.at[p // 2, p % 2], gout_low.at[p // 2, p % 2], load_sem.at[1, p]),
+                pltpu.make_async_copy(gv.at[:, p], gv_low.at[:, p], load_sem.at[2, p]),
+                pltpu.make_async_copy(gg.at[:, p], gg_low.at[:, p], load_sem.at[3, p]),
             ]
         )
         saves.append(
@@ -929,24 +1016,19 @@
     for copy in whole:
         copy.start()
     for p in range(steps):
-        high, low = 2 * p // steps, p % (steps // 2)
-        rows, tall = full // steps, units // steps
-        part, tall_part = slice(low * rows, (low + 1) * rows), slice(low * tall, (low + 1) * tall)
         here, tall_here = slice(p * rows, (p + 1) * rows), slice(p * tall, (p + 1) * tall)
         for copy in loads[p]:
             copy.wait()
-        cols = gin.shape[-1]
+        for i in range(4):
+            cols = slice(i * tall, (i + 1) * tall)
+            gin_out[here, cols] = gin_low[i // 2, p, i % 2].astype(f32)
+        for i in range(4):
+            cols = slice(i * rows, (i + 1) * rows)
+            gout_out[tall_here, cols] = gout_low[p // 2, p % 2, i].astype(f32)
         for x in range(2):
-            for i in range(4):
-                at = (4 * x + i) * cols
-                gin_out[here, at : at + cols] = gin_low[x, i, high, part].astype(f32)
-        cols = gout.shape[-1]
-        for i in range(8):
-            gout_out[tall_here, i * cols : (i + 1) * cols] = gout_low[high, i, tall_part].astype(f32)
-        cols = gv.shape[-1]
-        for x in range(2):
-            gv_out[here, x * cols : (x + 1) * cols] = gv_low[x, here].astype(f32)
-            gg_out[here, x * cols : (x + 1) * cols] = gg_low[x, here].astype(f32)
+            cols = slice(x * gv.shape[-1], (x + 1) * gv.shape[-1])
+            gv_out[here, cols] = gv_low[x, p].astype(f32)
+            gg_out[here, cols] = gg_low[x, p].astype(f32)
         for copy in saves[p]:
             copy.start()
     for copy in whole:
@@ -981,7 +1063,7 @@
     group = min(32, n_states)
     like = jax.ShapeDtypeStruct
     quarters = (width // LANES) * (n_states // group)
-    phases = 12
+    phases = 10 + streams * (width // LANES)
     act = (streams, length, width)
     flat = (tokens, width)
     mask = (streams, length, LANES)
@@ -989,30 +1071,31 @@
     tiles = width // LANES
     V = pltpu.VMEM
     scratch = [
-        V((2, 4, 2, full // 2, units // 8), bf16), V((2, 8, units // 2, full // 8), bf16), *[V((2, 4, full // 4, glu_cols // 2), bf16)] * 2,
+        V((2, 4, 2, full // 4, units // 4), bf16), V((2, 2, 4, units // 4, full // 4), bf16), *[V((2, 4, full // 4, glu_cols // 2), bf16)] * 2,
         V((full, glu_cols), bf16), V((full, glu_cols), bf16), V((full, units), bf16), V((units, full), bf16),
         V(mask, f32), V(mask, f32), V(mask, f32), V(mask, f32),
         V(tab, f32), V(tab, f32), V(tab, f32), V((n_states, width), f32),
         V((8, full), f32), V(flat, f32), V(act, f32), V(act, f32), V((tiles, streams, 2, n_states, LANES), f32), V((streams, *tab), f32), V((streams, *tab), f32),
-        V((tokens, full), bf16), V((tokens, glu_cols), f32), V((tokens, glu_cols), f32), V(flat, f32), V(flat, f32),
+        V((tokens, full), bf16), V((tokens, full), bf16), V((tokens, glu_cols), f32), V((tokens, glu_cols), f32), V(flat, f32), V(flat, f32),
         V((tokens, full), bf16), V((tokens, full), bf16), V((tokens, units), f32), V((tokens, units), bf16), V((tokens, units), bf16),
         V((full, tokens), bf16), V((full, tokens), bf16), V((units, tokens), bf16),
-        V(flat, f32), V(flat, f32), V(flat, f32), V(flat, f32), V((tokens, glu_cols), bf16), V((tokens, glu_cols), bf16), V(flat, f32),
-        V(act, f32), V(flat, f32),
-        V(mask, f32), V(mask, f32), V((tokens * 8, LANES), f32), V((length + 1, streams, 2, group // 8, 8, LANES), f32),
+        V(flat, f32), V(flat, f32), V(flat, f32), V(flat, f32), V((tokens, glu_cols), bf16), V((tokens, glu_cols), bf16),
+        V(act, f32),
+        V(mask, f32), V(mask, f32), V((tiles, *mask), f32), V((streams, length // 4, LANES), f32), V((streams, 4, length // 4, LANES), f32), V((tokens * 8, LANES), f32), V((2, length + 1, streams, 2, group // 8, 8, LANES), f32),
         V((4, 8, tokens), f32), V((4, n_chan - 1, 8, tokens), f32), V((3, n_chan - 1, *flat), bf16), V((3, n_chan - 1, *flat), bf16),
         *[V((2, tiles, streams, *lane_tab), bf16)] * 2, V((2, tiles, *lane_tab), bf16), V((2, tiles, pairs - 1, *lane_tab), bf16),
         V(lane_tab, f32), *[V((2, tiles, *lane_tab), bf16)] * 2,
         *[V((quarters, 4 * group, LANES), f32)] * 6,
-        V((8, width), f32), V((8, width), f32), *[V((1, 8, width), f32)] * 4,
+        V((n_seq, 8, width), f32),
         *[V((tokens, full), bf16)] * 3, V((full, tokens), bf16), V((full, tokens), bf16), V((units // 2, tokens), bf16),
         V((tokens, units // 2), bf16), V((tokens, glu_cols // 2), bf16), V((tokens, glu_cols // 2), bf16),
-        *[V((8, full // 2, units // 8), bf16)] * 3, *[V((8, units // 2, full // 8), bf16)] * 3,
+        *[V((8, full // 4, units // 4), bf16)] * 3, *[V((8, units // 4, full // 4), bf16)] * 3,
         *[V((4, full // 4, glu_cols // 2), bf16)] * 6,
         pltpu.SemaphoreType.DMA((4,)), pltpu.SemaphoreType.DMA((2, 24)),
         pltpu.SemaphoreType.DMA((phases, n_chan - 1)), pltpu.SemaphoreType.DMA((phases, n_chan - 1)),
         pltpu.SemaphoreType.DMA((2, tiles, pairs + 1)), pltpu.SemaphoreType.DMA((2, tiles, pairs + 1)),
-        pltpu.SemaphoreType.DMA((10 + quarters,)), pltpu.SemaphoreType.DMA((10 + quarters,)),
+        pltpu.SemaphoreType.DMA((11 + quarters,)), pltpu.SemaphoreType.DMA((11 + quarters,)),
+        pltpu.SemaphoreType.DMA((n_seq,)), pltpu.SemaphoreType.DMA((n_seq,)),
         pltpu.SemaphoreType.DMA((3, 25 + quarters)), pltpu.SemaphoreType.DMA((4, 25 + quarters)),
     ]
     specs = [pl.BlockSpec(memory_space=pltpu.SMEM)] + [VM] * 8 + [ANY, ANY, VM, ANY, ANY]
@@ -1020,14 +1103,14 @@
         functools.partial(block_kernel, sizes),
         out_shape=(
             like(act, f32), like(act, f32), like((4, n_states, width), f32), like((8, width), f32),
-            like((2, 4, 2, full // 2, units // 8), bf16), like((2, 8, units // 2, full // 8), bf16),
+            like((2, 4, 2, full // 4, units // 4), bf16), like((2, 2, 4, units // 4, full // 4), bf16),
             like((2, 4, full // 4, glu_cols // 2), bf16), like((2, 4, full // 4, glu_cols // 2), bf16),
         ),
         in_specs=specs,
         out_specs=(VM,) * 4 + (ANY,) * 4,
         scratch_shapes=scratch,
         compiler_params=pltpu.CompilerParams(
-            collective_id=0, has_side_effects=True, vmem_limit_bytes=58 * 1024 * 1024
+            collective_id=0, has_side_effects=True, vmem_limit_bytes=60 * 1024 * 1024
         ),
         name="block",
     )(
@@ -1037,7 +1120,6 @@
     block_out, in_grad, tables, gains, gin, gout, gv, gg = made
     steps = 4
     small = (n_states, width)
-    low_glu = (2, full, glu_cols // 2)
     cast = pl.pallas_call(
         functools.partial(cast_kernel, steps),
         out_shape=(
@@ -1048,14 +1130,14 @@
         in_specs=[ANY] * 8,
         out_specs=(ANY,) * 6 + (VM,) * 7,
         scratch_shapes=[
-            V(gin.shape, bf16), V(gout.shape, bf16), V(low_glu, bf16), V(low_glu, bf16),
+            V(gin.shape, bf16), V(gout.shape, bf16), V(gv.shape, bf16), V(gg.shape, bf16),
             V((full, units), f32), V((units, full), f32), V((full, glu_cols), f32), V((full, glu_cols), f32),
             V(tables.shape, f32), V(gains.shape, f32), V(act, f32), V(act, f32),
             pltpu.SemaphoreType.DMA((4, steps)), pltpu.SemaphoreType.DMA((4, steps)), pltpu.SemaphoreType.DMA((6,)),
         ],
         compiler_params=pltpu.CompilerParams(vmem_limit_bytes=58 * 1024 * 1024),
         name="cast",
-    )(gin, gout, gv.reshape(low_glu), gg.reshape(low_glu), block_out, in_grad, tables, gains)
+    )(gin, gout, gv, gg, block_out, in_grad, tables, gains)
     gin, gout, gv, gg, block_out, in_grad, dec, ang, real, imag, *gains = cast
     return (
         block_out, in_grad, gains[0][0], dec.T, ang.T, real.T, imag.T, gains[1][0], gv, gg, gains[2][0], gin, gout,

time: 158 us -> 152 us (0.962)
  Pallas kernels: 157 us -> 151 us
    pallas_call x1, Pallas kernels: 150 us -> 144 us  [per_device(): pl.pallas_call(functools.partial(block_kernel, sizes), out_shape=(like(ac...]
where the time goes in v4:
time: 152 us
  Pallas kernels  151 us (99%)
    pallas_call x1, Pallas kernels, per_device(): pl.pallas_call(functools.partial(block_kernel, sizes), out_shape=(like(ac...  144 us
    pallas_call x1, Pallas kernels, per_device(): pl.pallas_call(functools.partial(cast_kernel, steps), out_shape=(like((fu...  6.44 us

profile of v4, /device:TPU:0, one launch (start us, length us, event | category | flops | bytes accessed | tf_op | source)
XLA Modules:
  0.0 151.7 jit_solution(2142968894660849283)
XLA Ops:
  0.7 144.5 %block.1 = (f32[2,128,256]{2,1,0:T(8,128)}, f32[2,128,256]{2,1,0:T(8,128)}, f32[4,64,256]{2,1,0:T(8,128)}, f32[8,256]{1,0:T(8,128)}, bf16[2,4,2,256,256]{4,3,2,1...) custom-call(s32[2,16]{1,0:T(2,128)} %docs.1, ...), custom_call_target="tpu_custom_call" | custom-call | tf_op jit(solution)/shard_map/block/pallas_call | solution.py:1102
  145.1 6.4 %cast.1 = (f32[1024,1024]{1,0:T(8,128)}, f32[1024,1024]{1,0:T(8,128)}, f32[1024,256]{1,0:T(8,128)}, f32[1024,256]{1,0:T(8,128)}, f32[2,128,256]{2,1,0:T(8,128)},...) custom-call(bf16[2,4,2,256,256]{4,3,2,1,0:T(8,128)(2,1)} %get-tuple-, ...), custom_call_target="tpu_custom_call" | custom-call | tf_op jit(solution)/shard_map/cast/pallas_call | solution.py:1123

commit v5 on v4

--- a/solution.py
+++ b/solution.py
@@ -166,9 +166,9 @@
 
 def block_kernel(
     sizes,
-    docs, x_ref, og_ref, gain1, dec_ref, ang_ref, real_ref, imag_ref, skip_ref, gluv_hbm, glug_hbm, gain2, win_hbm, wout_hbm,
+    docs, x_hbm, og_hbm, gain1, dec_hbm, ang_hbm, real_hbm, imag_hbm, skip_ref, gluv_hbm, glug_hbm, gain2, win_hbm, wout_hbm,
     block_out, in_grad, tables_out, gains_out, gin_hbm, gout_hbm, gv_hbm, gg_hbm,
-    gin_out, gout_out, gv_out, gg_out, gluv, glug, win, wout,
+    gin_out, gout_out, gv_out, gg_out, gluv, glug, win, wout, x_ref, og_ref, dec_ref, ang_ref, real_ref, imag_ref,
     keep, first_mask, last_mask, valid,
     lam, coef, step_l, factor,
     gain_full, normed1, u_ref, y_ref, edge_sum, init, adj,
@@ -185,7 +185,7 @@
 ):
     n_seq, n_chan = sizes
     pairs = n_seq // 2
-    streams, length, width = x_ref.shape
+    streams, length, width = x_hbm.shape
     n_states = lam.shape[1]
     tokens = streams * length
     full = width * n_chan
@@ -215,11 +215,14 @@
     loads = [
         pltpu.make_async_copy(src, dst, load_sem.at[i])
         for i, (src, dst) in enumerate(
-            ((wout_hbm, wout), (gluv_hbm, gluv), (glug_hbm, glug), (win_hbm, win))
+            (
+                (wout_hbm, wout), (gluv_hbm, gluv), (glug_hbm, glug), (win_hbm, win), (x_hbm, x_ref), (og_hbm, og_ref),
+                (dec_hbm, dec_ref), (ang_hbm, ang_ref), (real_hbm, real_ref), (imag_hbm, imag_ref),
+            )
         )
     ]
-    for load in loads:
-        load.start()
+    for i in (4, 5, 6, 7, 8, 9, 0, 1, 2, 3):
+        loads[i].start()
 
     sent = []
 
@@ -257,6 +260,8 @@
         total = jnp.concatenate([total, jnp.zeros((LANES - 8, tokens), f32)], axis=0).T
         return total[:, 0:1] / full, total[:, 1:2] / full
 
+    loads[4].wait()
+    loads[5].wait()
     rows_in = x_ref[...].reshape(tokens, width)
     grad_full[:, own_cols] = og_ref[...].reshape(tokens, width).astype(bf16)
     sum1 = jnp.sum(rows_in, axis=1, keepdims=True)
@@ -306,6 +311,8 @@
         last_mask[b] = jnp.where(here == passed(b, start + length - 1), 1.0, 0.0)
         valid[b] = jnp.where(position < ends[b][-1], 1.0, 0.0)
 
+    for load in loads[6:]:
+        load.wait()
     decay, angle = dec_ref[...], ang_ref[...]
     magnitude = jnp.exp(-decay)
     a2 = angle * angle
@@ -357,7 +364,7 @@
                     return tuple(new)
 
                 zero = jnp.zeros((group // 8, 8, LANES), f32)
-                final = lax.fori_loop(0, length // 4, move, (zero,) * (2 * streams))
+                final = lax.fori_loop(0, length // 4, move, (zero,) * (2 * streams), unroll=2)
                 cr, ci = tile(coef, (0,), rows, cols), tile(coef, (1,), rows, cols)
                 for b in range(streams):
                     fr, fi = final[2 * b], final[2 * b + 1]
@@ -661,7 +668,7 @@
             begin = []
             for b in range(streams):
                 begin += [tile(init, (b, 0), rows, cols), tile(init, (b, 1), rows, cols)]
-            lax.fori_loop(0, fours, move, tuple(begin))
+            lax.fori_loop(0, fours, move, tuple(begin), unroll=2)
         for b in range(streams):
             for j in range(4):
                 first = (b * 4 + j) * fours * 8
@@ -832,6 +839,12 @@
     pump(2)
     zero = jnp.zeros((group // 8, 8, LANES), f32)
     q = 0
+
+    def tables(**steps):
+        for act, i in steps.items():
+            if 0 <= i < quarters:
+                getattr(table_line, act)(i)
+
     for k in range(width // LANES):
         backward[k].end()
         cols = pl.ds(k * LANES, LANES)
@@ -843,14 +856,11 @@
 
             if q > 1:
                 again_pass(q)
-            pump(2, 3 if q == 0 else 4)
+            pump(2, 3)
             if q == 0:
                 wanted["mid_near"].wait_recv()
                 wanted["mid_far"] = swap_factor(mid2.at[core_half, :], mid2.at[core_half, :], 3, beside)
-            if q > 0:
-                table_line.begin(q - 1)
-            if q > 1:
-                table_line.settle(q - 2)
+            tables(begin=q - 1, join=q - 2, relay=q - 3)
             held = states.at[q % 2]
 
             def back(i, carry, h=h, held=held, lr=lr, li=li, cr=cr, ci=ci):
@@ -882,7 +892,7 @@
             begin = []
             for b in range(streams):
                 begin += [tile(adj, (b, 0), rows, cols), tile(adj, (b, 1), rows, cols)]
-            sums = lax.fori_loop(0, length, back, (zero, zero, zero, zero, *begin))
+            sums = lax.fori_loop(0, length, back, (zero, zero, zero, zero, *begin), unroll=2)
             glr, gli, gcr, gci = [item.reshape(-1, LANES) for item in sums[:4]]
             share = factor[rows, cols]
             ratio = (1.0 - share * share) / share
@@ -898,11 +908,8 @@
                 need("mid_far")
                 transposed(mid2, mid_t2, n_chan)
                 ready.append("mid")
-            pump(2)
-            if q > 0:
-                table_line.join(q - 1)
-            if q > 1:
-                table_line.relay(q - 2)
+            pump(2, 3)
+            tables(settle=q - 2)
             q += 1
         for b in range(streams):
             total = part[pl.ds(b * length * 8, length, stride=8), :]
@@ -912,10 +919,6 @@
             part_own[b * length : (b + 1) * length, cols] = u_grad * valid[b]
 
     last = quarters - 1
-    pump(1)
-    table_line.begin(last)
-    if last > 0:
-        table_line.settle(last - 1)
     scaled = part_own[...] * gain1[...]
     stat_copies = stats_start(
         jnp.sum(scaled, axis=1, keepdims=True),
@@ -935,17 +938,22 @@
         copy.start()
         sent.append(copy)
     pump(1)
+    tables(join=last - 1, relay=last - 2)
+    pump(1)
+    tables(begin=last)
+    pump(1)
+    tables(settle=last - 1)
     first, second = stats_end(stat_copies, 3)
     in_grad[...] = (
         resid_grad[...] + scaler1 * (part_own[...] * gain1[...] - first - normed1[...] * second)
     ).reshape(streams, length, width)
-    table_line.join(last)
-    if last > 0:
-        table_line.relay(last - 1)
+    tables(join=last)
     pump(1)
-    table_line.settle(last)
-    pump(2)
-    table_line.relay(last)
+    tables(relay=last - 1)
+    pump(1)
+    tables(settle=last)
+    pump(1)
+    tables(relay=last)
     while tick[0] < len(pieces) + STORE:
         pump(1)
     for k in range(width // LANES):
@@ -1073,6 +1081,7 @@
     scratch = [
         V((2, 4, 2, full // 4, units // 4), bf16), V((2, 2, 4, units // 4, full // 4), bf16), *[V((2, 4, full // 4, glu_cols // 2), bf16)] * 2,
         V((full, glu_cols), bf16), V((full, glu_cols), bf16), V((full, units), bf16), V((units, full), bf16),
+        V(act, f32), V(act, f32), *[V((n_states, width), f32)] * 4,
         V(mask, f32), V(mask, f32), V(mask, f32), V(mask, f32),
         V(tab, f32), V(tab, f32), V(tab, f32), V((n_states, width), f32),
         V((8, full), f32), V(flat, f32), V(act, f32), V(act, f32), V((tiles, streams, 2, n_states, LANES), f32), V((streams, *tab), f32), V((streams, *tab), f32),
@@ -1091,14 +1100,14 @@
         V((tokens, units // 2), bf16), V((tokens, glu_cols // 2), bf16), V((tokens, glu_cols // 2), bf16),
         *[V((8, full // 4, units // 4), bf16)] * 3, *[V((8, units // 4, full // 4), bf16)] * 3,
         *[V((4, full // 4, glu_cols // 2), bf16)] * 6,
-        pltpu.SemaphoreType.DMA((4,)), pltpu.SemaphoreType.DMA((2, 24)),
+        pltpu.SemaphoreType.DMA((10,)), pltpu.SemaphoreType.DMA((2, 24)),
         pltpu.SemaphoreType.DMA((phases, n_chan - 1)), pltpu.SemaphoreType.DMA((phases, n_chan - 1)),
         pltpu.SemaphoreType.DMA((2, tiles, pairs + 1)), pltpu.SemaphoreType.DMA((2, tiles, pairs + 1)),
         pltpu.SemaphoreType.DMA((11 + quarters,)), pltpu.SemaphoreType.DMA((11 + quarters,)),
         pltpu.SemaphoreType.DMA((n_seq,)), pltpu.SemaphoreType.DMA((n_seq,)),
         pltpu.SemaphoreType.DMA((3, 25 + quarters)), pltpu.SemaphoreType.DMA((4, 25 + quarters)),
     ]
-    specs = [pl.BlockSpec(memory_space=pltpu.SMEM)] + [VM] * 8 + [ANY, ANY, VM, ANY, ANY]
+    specs = [pl.BlockSpec(memory_space=pltpu.SMEM), ANY, ANY, VM, ANY, ANY, ANY, ANY, VM, ANY, ANY, VM, ANY, ANY]
     made = pl.pallas_call(
         functools.partial(block_kernel, sizes),
         out_shape=(

time: 152 us -> 148 us (0.974)
  Pallas kernels: 151 us -> 147 us
    pallas_call x1, Pallas kernels: 144 us -> 140 us  [per_device(): pl.pallas_call(functools.partial(block_kernel, sizes), out_shape=(like(ac...]
where the time goes in v5:
time: 148 us; the launch traced here: 147 us
  Pallas kernels  147 us (99%)
    pallas_call x1, Pallas kernels, per_device(): pl.pallas_call(functools.partial(block_kernel, sizes), out_shape=(like(ac...  140 us
    pallas_call x1, Pallas kernels, per_device(): pl.pallas_call(functools.partial(cast_kernel, steps), out_shape=(like((fu...  6.44 us

profile of v5, /device:TPU:0, one launch (start us, length us, event | category | flops | bytes accessed | tf_op | source)
XLA Modules:
  0.0 147.4 jit_solution(8599286585429393336)
XLA Ops:
  0.7 140.1 %block.1 = (f32[2,128,256]{2,1,0:T(8,128)}, f32[2,128,256]{2,1,0:T(8,128)}, f32[4,64,256]{2,1,0:T(8,128)}, f32[8,256]{1,0:T(8,128)}, bf16[2,4,2,256,256]{4,3,2,1...) custom-call(s32[2,16]{1,0:T(2,128)} %docs.1, ...), custom_call_target="tpu_custom_call" | custom-call | tf_op jit(solution)/shard_map/block/pallas_call | solution.py:1111
  140.8 6.4 %cast.1 = (f32[1024,1024]{1,0:T(8,128)}, f32[1024,1024]{1,0:T(8,128)}, f32[1024,256]{1,0:T(8,128)}, f32[1024,256]{1,0:T(8,128)}, f32[2,128,256]{2,1,0:T(8,128)},...) custom-call(bf16[2,4,2,256,256]{4,3,2,1,0:T(8,128)(2,1)} %get-tuple-, ...), custom_call_target="tpu_custom_call" | custom-call | tf_op jit(solution)/shard_map/cast/pallas_call | solution.py:1132

commit v6 on v5

--- a/solution.py
+++ b/solution.py
@@ -53,6 +53,9 @@
     return ref[(*lead, rows, cols)].reshape(-1, 8, LANES)
 
 
+TURNS = (8, 8, 8)
+
+
 class Line:
     def __init__(self, own, count, at, send, inward, across, sems, where, hand_over, stores=None):
         self.own, self.count, self.at = own, count, at
@@ -63,20 +66,31 @@
 
     def copy(self, src, dst, i, sent, got, to):
         return pltpu.make_async_remote_copy(
-            src_ref=src, dst_ref=dst, send_sem=self.sent.at[sent, i], recv_sem=self.got.at[got, i],
+            src_ref=src, dst_ref=dst, send_sem=self.sent.at[sent, i % TURNS[sent]], recv_sem=self.got.at[got, i],
             device_id=to, device_id_type=MESH,
         )
 
+    def free(self, i, kind):
+        if i >= TURNS[kind]:
+            self.gone(i - TURNS[kind], kind)
+
+    def gone(self, i, kind):
+        self.copy(self.send.at[i], self.send.at[i], i, kind, 0, self.toward).wait_send()
+
     def pass_in(self, i):
+        self.free(i, 0)
         self.copy(self.send.at[i], self.inward.at[i], i, 0, 0, self.toward).start()
 
     def pass_across(self, i):
+        self.free(i, 0)
         self.copy(self.send.at[i], self.across.at[i], i, 0, 1, self.toward).start()
 
     def pass_out(self, i):
+        self.free(i, 1)
         self.copy(self.at(i), self.at(i), i, 1, 2, self.away).start()
 
     def pass_pair(self, i):
+        self.free(i, 2)
         self.copy(self.at(i), self.at(i), i, 2, 3, self.partner).start()
 
     def arrived(self, i, kind):
@@ -139,41 +153,35 @@
                 if self.hand_over:
                     self.pass_pair(i)
 
-    def saves(self, i):
-        return [pltpu.make_async_copy(src, dst, sem) for src, dst, sem in self.stores(i)]
-
     def store(self, i):
         self.arrived(i, 3)
-        for save in self.saves(i):
-            save.start()
+        self.stores(i)
 
     def finish(self):
-        for i in range(self.count):
-            if self.stores:
-                for save in self.saves(i):
-                    save.wait()
-            self.copy(self.send.at[i], self.send.at[i], i, 0, 0, self.toward).wait_send()
+        for i in range(max(0, self.count - TURNS[0]), self.count):
+            self.gone(i, 0)
+        for i in range(max(0, self.count - TURNS[1]), self.count):
             if self.pairs > 2:
 
                 @pl.when(jnp.logical_not(self.is_end))
                 def _(i=i):
-                    self.copy(self.send.at[i], self.send.at[i], i, 1, 2, self.toward).wait_send()
-
-            if self.hand_over:
-                done = self.copy(self.send.at[i], self.send.at[i], i, 2, 3, self.toward)
-                done.wait_send()
+                    self.gone(i, 1)
+
+        if self.hand_over:
+            for i in range(max(0, self.count - TURNS[2]), self.count):
+                self.gone(i, 2)
 
 
 def block_kernel(
     sizes,
     docs, x_hbm, og_hbm, gain1, dec_hbm, ang_hbm, real_hbm, imag_hbm, skip_ref, gluv_hbm, glug_hbm, gain2, win_hbm, wout_hbm,
-    block_out, in_grad, tables_out, gains_out, gin_hbm, gout_hbm, gv_hbm, gg_hbm,
-    gin_out, gout_out, gv_out, gg_out, gluv, glug, win, wout, x_ref, og_ref, dec_ref, ang_ref, real_ref, imag_ref,
+    block_hbm, grad_hbm, tables_hbm, gains_hbm, gin_hbm, gout_hbm, gv_hbm, gg_hbm,
+    block_out, in_grad, gains_out, gin_out, gout_out, gv_out, gg_out, gluv, glug, win, wout, x_ref, og_ref, dec_ref, ang_ref, real_ref, imag_ref,
     keep, first_mask, last_mask, valid,
     lam, coef, step_l, factor,
     gain_full, normed1, u_ref, y_ref, edge_sum, init, adj,
-    act_full, centred, val, gate, resid, normed2, grad_full, mid_full, hidden_grad, hidden, pre,
-    act_t, mid_t, hidden_t, part_own, mid_grad, result_own, resid_grad, value_grad, gate_grad, mixer_grad,
+    act_full, val, gate, resid, normed2, grad_full, mid_full, hidden_grad, hidden, pre,
+    act_t, mid_t, hidden_t, part_own, result_own, resid_grad, value_grad, gate_grad, mixer_grad,
     row_a, row_b, u_rows, keep4, tails, part, states,
     stat_send, stat_recv, rs_send, rs_recv,
     pair_send, pair_recv, line_send, line_recv, back_send, back_low, back_recv,
@@ -181,7 +189,7 @@
     gain_all,
     grad2, act2, mid2, act_t2, mid_t2, hidden_t2, pre2, value2, gate2,
     in_send, in_in, in_across, out_send, out_in, out_across, gv_send, gv_in, gv_across, gg_send, gg_in, gg_across,
-    load_sem, save_sem, chan_send, chan_recv, seq_send, seq_recv, fac_send, fac_recv, gain_send, gain_recv, line_sent, line_got,
+    load_sem, save_sem, last_sem, chan_send, chan_recv, seq_send, seq_recv, fac_send, fac_recv, gain_send, gain_recv, line_sent, line_got,
 ):
     n_seq, n_chan = sizes
     pairs = n_seq // 2
@@ -224,21 +232,33 @@
     for i in (4, 5, 6, 7, 8, 9, 0, 1, 2, 3):
         loads[i].start()
 
-    sent = []
-
-    def chan_copy(src, dst, phase, j):
+    sent, saved = [], []
+
+    def save(src, dst, i):
+        copy = pltpu.make_async_copy(src, dst, last_sem.at[i])
+        copy.start()
+        saved.append(copy)
+
+    chan_turns, chan_count = [], [0]
+
+    def chan_copy(src, dst, phase, j, turn):
         return pltpu.make_async_remote_copy(
-            src_ref=src, dst_ref=dst, send_sem=chan_send.at[phase, j - 1], recv_sem=chan_recv.at[phase, j - 1],
+            src_ref=src, dst_ref=dst, send_sem=chan_send.at[turn, j - 1], recv_sem=chan_recv.at[phase, j - 1],
             device_id=(s, chan_peer(j)), device_id_type=MESH,
         )
 
     def chan_all(pick, phase):
         copies = []
+        turn = chan_count[0] % 6
+        chan_count[0] += 1
+        if len(chan_turns) == 6:
+            for copy in chan_turns.pop(0):
+                copy.wait_send()
         for j in range(1, n_chan):
-            copy = chan_copy(*pick(j), phase, j)
+            copy = chan_copy(*pick(j), phase, j, turn)
             copy.start()
             copies.append(copy)
-        sent.extend(copies)
+        chan_turns.append(copies)
         return copies
 
     def landed(copies):
@@ -540,19 +560,33 @@
         need(("table", q))
         return table[q] + table2[q]
 
-    sem_at = [0]
+    sem_at = [0, 0]
+
+    storing, stored = [], [0]
 
     def line(own, count, at, bufs, hand_over, kept_at=None):
-        spot, base = pl.ds(sem_at[0], count), sem_at[0]
+        spot = pl.ds(sem_at[0], count)
+        turns = pl.ds(sem_at[1], min(count, TURNS[0]))
         stores = None
         if kept_at:
             held, final, place = kept_at
 
             def stores(i):
-                return [(held.at[(x, *place(i))], final.at[(x, *place(i))], save_sem.at[x, base + i]) for x in range(2)]
+                turn = stored[0] % 4
+                stored[0] += 1
+                if len(storing) == 4:
+                    for copy in storing.pop(0):
+                        copy.wait()
+                copies = [
+                    pltpu.make_async_copy(held.at[(x, *place(i))], final.at[(x, *place(i))], save_sem.at[x, turn]) for x in range(2)
+                ]
+                for copy in copies:
+                    copy.start()
+                storing.append(copies)
 
         sem_at[0] += count
-        return Line(own, count, at, *bufs, (line_sent.at[:, spot], line_got.at[:, spot]), where, hand_over, stores)
+        sem_at[1] += min(count, TURNS[0])
+        return Line(own, count, at, *bufs, (line_sent.at[:, turns], line_got.at[:, spot]), where, hand_over, stores)
 
     quarters = (width // LANES) * (n_states // group)
     in_line = line(in_own, 8, in_at, (in_send, in_in, in_across), True, (gin_out, gin_hbm, lambda i: (i // 2, i % 2)))
@@ -727,9 +761,9 @@
 
     sum2 = jnp.sum(resid[...], axis=1, keepdims=True)
     square2 = jnp.sum(resid[...] * resid[...], axis=1, keepdims=True)
-    centred[:, own_cols] = (resid[...] - sum2 / width).astype(bf16)
+    mid2[:, own_cols] = (resid[...] - sum2 / width).astype(bf16)
     stat_copies = stats_start(sum2, square2, 1, base)
-    mid_copies = chan_all(lambda j: (centred.at[:, own_cols], centred.at[:, own_cols]), base + 1)
+    mid_copies = chan_all(lambda j: (mid2.at[:, own_cols], mid2.at[:, own_cols]), base + 1)
     landed(gain_copies)
     landed(stat_copies)
     shares = [stat_send[1], *[stat_recv[1, j - 1] for j in range(1, n_chan)]]
@@ -745,7 +779,7 @@
     for j in range(1, n_chan):
         cols = chan_block(lax.rem(c - j + n_chan, n_chan), width)
         shift = shares[:, 8 * j : 8 * j + 1] / width - average
-        mid_full[:, cols] = ((centred[:, cols].astype(f32) + shift) * scaler2 * gain_full[0:1, cols]).astype(bf16)
+        mid_full[:, cols] = ((mid2[:, cols].astype(f32) + shift) * scaler2 * gain_full[0:1, cols]).astype(bf16)
     loads[3].wait()
 
     for k in range(4):
@@ -781,6 +815,9 @@
 
     scatter_fill(lambda rows: dot(pre[...], win[rows, :], NT), part_own, 0)
     grad_parts = scatter_start(0, base + 2)
+    for copy in mid_copies:
+        copy.wait_send()
+    mid_copies.clear()
     first, second = 0.0, 0.0
     for j in range(n_chan):
         cols = chan_block(chan_peer(j), width) if j else own_cols
@@ -796,12 +833,12 @@
     for q in range(min(2, quarters)):
         again_pass(q)
     launch(4)
-    mid_grad[...] = scatter_end(grad_parts, part_own, 0)
+    resid_grad[...] = scatter_end(grad_parts, part_own, 0)
     wanted["pre"] = swap_factor(pre.at[:, their_half], pre2, 5)
-    gains = jnp.sum(mid_grad[...] * normed2[...], axis=0, keepdims=True)
+    gains = jnp.sum(resid_grad[...] * normed2[...], axis=0, keepdims=True)
     first, second = stats_end(stat_copies, 2)
     resid_grad[...] = og_ref[...].reshape(tokens, width) + scaler2 * (
-        mid_grad[...] * gain2[...] - first - normed2[...] * second
+        resid_grad[...] * gain2[...] - first - normed2[...] * second
     )
 
     value_grad[...] = (resid_grad[...] * gate[...]).astype(bf16)
@@ -831,6 +868,7 @@
     pump(1, 2)
     total = scatter_end(out_parts, result_own, 1)
     block_out[...] = (resid[...] + total).reshape(streams, length, width)
+    save(block_out, block_hbm, 0)
     for k in range(tiles):
         backward[k].home()
     need("act_far")
@@ -947,6 +985,7 @@
     in_grad[...] = (
         resid_grad[...] + scaler1 * (part_own[...] * gain1[...] - first - normed1[...] * second)
     ).reshape(streams, length, width)
+    save(in_grad, grad_hbm, 1)
     tables(join=last)
     pump(1)
     tables(relay=last - 1)
@@ -956,12 +995,8 @@
     tables(relay=last)
     while tick[0] < len(pieces) + STORE:
         pump(1)
-    for k in range(width // LANES):
-        for h in range(n_states // group):
-            for i in range(4):
-                tables_out[i, h * group : (h + 1) * group, k * LANES : (k + 1) * LANES] = table_sum[
-                    k * (n_states // group) + h, i * group : (i + 1) * group, :
-                ]
+    for q in range(quarters):
+        save(table_sum.at[q], tables_hbm.at[q], 3 + q)
     for d in range(1, n_seq):
         source = lax.rem(s + d, n_seq)
         pltpu.make_async_remote_copy(
@@ -972,11 +1007,14 @@
     for k in range(1, n_seq):
         total = total + gain_all[k]
     gains_out[...] = total
+    save(gains_out, gains_hbm, 2)
     for entry in lines:
         entry.finish()
     for copy in factors:
         copy.wait_send()
-    for copy in sent:
+    for copy in (*saved, *sum(storing, [])):
+        copy.wait()
+    for copy in (*sent, *sum(chan_turns, [])):
         copy.wait_send()
     for carry in (*forward, *backward):
         carry.finish()
@@ -1047,8 +1085,13 @@
     ]
     for copy in passed_on:
         copy.start()
-    for k, out in enumerate((dec_out, ang_out, real_out, imag_out)):
-        out[...] = table_low[k]
+    group, lanes = table_low.shape[1] // 4, table_low.shape[2]
+    halves = dec_out.shape[0] // group
+    for q in range(table_low.shape[0]):
+        rows = slice(q % halves * group, (q % halves + 1) * group)
+        cols = slice(q // halves * lanes, (q // halves + 1) * lanes)
+        for k, out in enumerate((dec_out, ang_out, real_out, imag_out)):
+            out[rows, cols] = table_low[q, k * group : (k + 1) * group, :]
     for k, out in enumerate((gain_a, gain_b, gain_c)):
         out[...] = gain_low[k : k + 1, :]
     for copies in (*saves, passed_on):
@@ -1079,16 +1122,17 @@
     tiles = width // LANES
     V = pltpu.VMEM
     scratch = [
+        V(act, f32), V(act, f32), V((8, width), f32),
         V((2, 4, 2, full // 4, units // 4), bf16), V((2, 2, 4, units // 4, full // 4), bf16), *[V((2, 4, full // 4, glu_cols // 2), bf16)] * 2,
         V((full, glu_cols), bf16), V((full, glu_cols), bf16), V((full, units), bf16), V((units, full), bf16),
         V(act, f32), V(act, f32), *[V((n_states, width), f32)] * 4,
         V(mask, f32), V(mask, f32), V(mask, f32), V(mask, f32),
         V(tab, f32), V(tab, f32), V(tab, f32), V((n_states, width), f32),
         V((8, full), f32), V(flat, f32), V(act, f32), V(act, f32), V((tiles, streams, 2, n_states, LANES), f32), V((streams, *tab), f32), V((streams, *tab), f32),
-        V((tokens, full), bf16), V((tokens, full), bf16), V((tokens, glu_cols), f32), V((tokens, glu_cols), f32), V(flat, f32), V(flat, f32),
+        V((tokens, full), bf16), V((tokens, glu_cols), f32), V((tokens, glu_cols), f32), V(flat, f32), V(flat, f32),
         V((tokens, full), bf16), V((tokens, full), bf16), V((tokens, units), f32), V((tokens, units), bf16), V((tokens, units), bf16),
         V((full, tokens), bf16), V((full, tokens), bf16), V((units, tokens), bf16),
-        V(flat, f32), V(flat, f32), V(flat, f32), V(flat, f32), V((tokens, glu_cols), bf16), V((tokens, glu_cols), bf16),
+        V(flat, f32), V(flat, f32), V(flat, f32), V((tokens, glu_cols), bf16), V((tokens, glu_cols), bf16),
         V(act, f32),
         V(mask, f32), V(mask, f32), V((tiles, *mask), f32), V((streams, length // 4, LANES), f32), V((streams, 4, length // 4, LANES), f32), V((tokens * 8, LANES), f32), V((2, length + 1, streams, 2, group // 8, 8, LANES), f32),
         V((4, 8, tokens), f32), V((4, n_chan - 1, 8, tokens), f32), V((3, n_chan - 1, *flat), bf16), V((3, n_chan - 1, *flat), bf16),
@@ -1100,23 +1144,23 @@
         V((tokens, units // 2), bf16), V((tokens, glu_cols // 2), bf16), V((tokens, glu_cols // 2), bf16),
         *[V((8, full // 4, units // 4), bf16)] * 3, *[V((8, units // 4, full // 4), bf16)] * 3,
         *[V((4, full // 4, glu_cols // 2), bf16)] * 6,
-        pltpu.SemaphoreType.DMA((10,)), pltpu.SemaphoreType.DMA((2, 24)),
-        pltpu.SemaphoreType.DMA((phases, n_chan - 1)), pltpu.SemaphoreType.DMA((phases, n_chan - 1)),
+        pltpu.SemaphoreType.DMA((10,)), pltpu.SemaphoreType.DMA((2, 4)), pltpu.SemaphoreType.DMA((3 + quarters,)),
+        pltpu.SemaphoreType.DMA((6, n_chan - 1)), pltpu.SemaphoreType.DMA((phases, n_chan - 1)),
         pltpu.SemaphoreType.DMA((2, tiles, pairs + 1)), pltpu.SemaphoreType.DMA((2, tiles, pairs + 1)),
         pltpu.SemaphoreType.DMA((11 + quarters,)), pltpu.SemaphoreType.DMA((11 + quarters,)),
         pltpu.SemaphoreType.DMA((n_seq,)), pltpu.SemaphoreType.DMA((n_seq,)),
-        pltpu.SemaphoreType.DMA((3, 25 + quarters)), pltpu.SemaphoreType.DMA((4, 25 + quarters)),
+        pltpu.SemaphoreType.DMA((3, 24 + quarters)), pltpu.SemaphoreType.DMA((4, 24 + quarters)),
     ]
     specs = [pl.BlockSpec(memory_space=pltpu.SMEM), ANY, ANY, VM, ANY, ANY, ANY, ANY, VM, ANY, ANY, VM, ANY, ANY]
     made = pl.pallas_call(
         functools.partial(block_kernel, sizes),
         out_shape=(
-            like(act, f32), like(act, f32), like((4, n_states, width), f32), like((8, width), f32),
+            like(act, f32), like(act, f32), like((quarters, 4 * group, LANES), f32), like((8, width), f32),
             like((2, 4, 2, full // 4, units // 4), bf16), like((2, 2, 4, units // 4, full // 4), bf16),
             like((2, 4, full // 4, glu_cols // 2), bf16), like((2, 4, full // 4, glu_cols // 2), bf16),
         ),
         in_specs=specs,
-        out_specs=(VM,) * 4 + (ANY,) * 4,
+        out_specs=(ANY,) * 8,
         scratch_shapes=scratch,
         compiler_params=pltpu.CompilerParams(
             collective_id=0, has_side_effects=True, vmem_limit_bytes=60 * 1024 * 1024

time: 148 us -> 147 us (level)
  Pallas kernels: 147 us -> 144 us
    pallas_call x1, Pallas kernels: 140 us -> 138 us  [per_device(): pl.pallas_call(functools.partial(block_kernel, sizes), out_shape=(like(ac...]
where the time goes in v6:
time: 147 us; the launch traced here: 145 us
  Pallas kernels  144 us (98%)
    pallas_call x1, Pallas kernels, per_device(): pl.pallas_call(functools.partial(block_kernel, sizes), out_shape=(like(ac...  138 us
    pallas_call x1, Pallas kernels, per_device(): pl.pallas_call(functools.partial(cast_kernel, steps), out_shape=(like((fu...  6.44 us

profile of v6, /device:TPU:0, one launch (start us, length us, event | category | flops | bytes accessed | tf_op | source)
XLA Modules:
  0.0 144.9 jit_solution(7057752099794918666)
XLA Ops:
  0.7 137.7 %block.1 = (f32[2,128,256]{2,1,0:T(8,128)}, f32[2,128,256]{2,1,0:T(8,128)}, f32[4,128,128]{2,1,0:T(8,128)}, f32[8,256]{1,0:T(8,128)}, bf16[2,4,2,256,256]{4,3,2,...) custom-call(s32[2,16]{1,0:T(2,128)} %docs.1, ...), custom_call_target="tpu_custom_call" | custom-call | tf_op jit(solution)/shard_map/block/pallas_call | solution.py:1155
  138.3 6.4 %cast.1 = (f32[1024,1024]{1,0:T(8,128)}, f32[1024,1024]{1,0:T(8,128)}, f32[1024,256]{1,0:T(8,128)}, f32[1024,256]{1,0:T(8,128)}, f32[2,128,256]{2,1,0:T(8,128)},...) custom-call(bf16[2,4,2,256,256]{4,3,2,1,0:T(8,128)(2,1)} %get-tuple-, ...), custom_call_target="tpu_custom_call" | custom-call | tf_op jit(solution)/shard_map/cast/pallas_call | solution.py:1176
